TPU v7x, 32 devices: a whole 2x2x4 slice. The times are simulated.
32 devices in a mesh: groups: 2 (over y), dom: 4 (over z), rep: 2 (over x), sub: 2 (over core).
Axes of the slice: x: 2, y: 2, z: 4, core: 2. Of those that a mesh axis runs over, the one named last changes fastest.
Arguments:
- adjacency: bfloat16 [2048, 4, 256], P(('groups', 'dom'), None, 'rep'), parts along dimension 0, may hold values from 0 to 1, as said below
- block_presence_mask: int32 [16, 4, 2], P(('groups', 'dom'), None, 'rep'), parts along dimension 0, may hold values from 0 to 1, as said below
- features: bfloat16 [2048, 128], P(('groups', 'dom', 'rep')), parts along dimension 0, may hold values from -20 to 20
- weight: bfloat16 [128, 256], P(None, 'sub'), may hold values from -0.5 to 0.5
- bias: float32 [256], P('sub'), may hold values from -3 to 3
- cotangent: bfloat16 [2048, 256], P(('groups', 'dom', 'rep'), 'sub'), parts along dimension 0, may hold values from -6 to 6
Outputs:
- activation: bfloat16 [2048, 256], P(('groups', 'dom', 'rep'), 'sub'), parts along dimension 0
- grad_input: bfloat16 [2048, 128], P(('groups', 'dom', 'rep')), parts along dimension 0
- grad_weight: float32 [256, 256], P('groups', 'sub'), parts along dimension 0
There are 2 independent parts, one for each index of `groups`. A program takes and returns all parts, laid end to end along the dimension named above; an argument that names none is the same for every part. Nothing has to cross between parts.
Inputs may be any that keep to these rules, and one draw needn't show every extreme that they name: Read as a 1024 x 1024 matrix, the adjacency is symmetric. Read as a square matrix of blocks, block_presence_mask is symmetric; every diagonal block, every block beside the diagonal, and every block whose block row and block column differ by exactly 4 is 1.
All inputs are finite; a program needn't handle non-finite values.
Results may differ from a plain program's by a relative error of at most 0.0062.
Values may be sent and summed in bfloat16 or wider, within the bound.
No kernel may reach another device: no remote copies, remote signals or barrier semaphores. Data moves between devices by JAX's collectives and lax.ppermute only.
A program may use at most 64 MiB of HBM per device.

v0:
```python
import math

import jax
import jax.numpy as jnp
from jax import lax
from jax.sharding import PartitionSpec as P


def on_device(adjacency, block_presence_mask, features, weight, bias, cotangent):
    grouped_row_set, row_sections_list, feature_width = adjacency.shape
    mask_row_index, unused_sections, mask_column_index = block_presence_mask.shape
    block_extent = feature_width // mask_column_index
    block_alive_flags = block_presence_mask.astype(jnp.bfloat16)
    block_alive_flags = jnp.broadcast_to(
        block_alive_flags[:, None, :, :, None],
        (mask_row_index, block_extent, row_sections_list, mask_column_index, block_extent),
    )
    block_alive_flags = block_alive_flags.reshape(grouped_row_set, row_sections_list, feature_width)
    graph_operator = (adjacency * block_alive_flags).reshape(
        grouped_row_set, row_sections_list * feature_width
    )
    support = jnp.dot(features, weight, preferred_element_type=jnp.float32).astype(jnp.bfloat16)
    columns = graph_operator
    partial_value = jnp.dot(
        columns,
        lax.all_gather(support, "dom", axis=0, tiled=True),
        preferred_element_type=jnp.float32,
    )
    pre = lax.psum_scatter(partial_value, "rep", scatter_dimension=0, tiled=True) + bias[None, :]
    sigma = jax.nn.sigmoid(pre)
    activation = (pre * sigma).astype(jnp.bfloat16)
    grad_pre = (cotangent.astype(jnp.float32) * sigma * (1.0 + pre * (1.0 - sigma))).astype(
        jnp.bfloat16
    )
    block_grads = lax.all_gather(grad_pre, "rep", axis=0, tiled=True)
    columns = graph_operator
    gradient_of_support = lax.psum_scatter(
        lax.dot_general(
            columns, block_grads, (((0,), (0,)), ((), ())), preferred_element_type=jnp.float32
        ),
        "dom",
        scatter_dimension=0,
        tiled=True,
    )
    node_total = grouped_row_set * row_sections_list
    weight_term = lax.dot_general(
        features.astype(jnp.float32),
        gradient_of_support,
        (((0,), (0,)), ((), ())),
        precision=lax.Precision.HIGHEST,
    ) / math.sqrt(node_total)
    grad_weight = lax.psum(weight_term, ("dom", "rep"))
    input_term = lax.dot_general(
        gradient_of_support,
        weight.astype(jnp.float32),
        (((1,), (1,)), ((), ())),
        precision=lax.Precision.HIGHEST,
    )
    grad_input = lax.psum(input_term, "sub").astype(jnp.bfloat16)
    return (activation, grad_input, grad_weight)


def solution(mesh):
    return jax.shard_map(
        on_device,
        mesh=mesh,
        in_specs=(
            P(("groups", "dom"), None, "rep"),
            P(("groups", "dom"), None, "rep"),
            P(("groups", "dom", "rep"), None),
            P(None, "sub"),
            P("sub"),
            P(("groups", "dom", "rep"), "sub"),
        ),
        out_specs=(
            P(("groups", "dom", "rep"), "sub"),
            P(("groups", "dom", "rep"), None),
            P("groups", "sub"),
        ),
        check_vma=False,
    )
```

profile of v0, /device:TPU:0, one launch (start us, length us, event | category | flops | bytes accessed | tf_op | source)
XLA Modules:
  0.0 143.0 jit_solution(8650641123876878723)
XLA Ops:
  7.2 0.0 copy-start
  7.2 0.0 copy-start.1
  7.2 0.0 reduce-scatter.3.cloned.1.call-start
  7.2 0.7 convert_element_type.20
  8.0 0.0 copy-done
  8.0 0.9 convolution_convert_fusion
  8.8 15.1 %all_gather.6 = bf16[512,128]{1,0:T(8,128)(2,1)S(1)} all-gather(bf16[128,128]{1,0:T(8,128)(2,1)S(1)} %convolution_convert_fusion), channel_id=1, replica_groups=mesh['groups'=2,'dom'=4,'rep'=2,'sub'=2] {'dom'}, dimensions={0}, use_global_device_ids=true | all-gather | bytes 163840 | tf_op jit(solution)/shard_map/all_gather | solution.py:26
  23.9 0.0 copy-done.1
  23.9 0.3 broadcast_multiply_fusion
  24.3 0.9 fusion.3
  25.1 0.0 copy-start.4
  25.1 0.0 copy-start.5
  25.1 0.0 reduce-scatter.3.cloned.1.call-update
  25.2 0.0 reduce-scatter.5.cloned.1.call-start
  25.2 11.7 %reduce-scatter.3.cloned.1.call-done = f32[128,128]{1,0:T(8,128)} async-done(((f32[256,128]{1,0:T(8,128)}), f32[128,128]{1,0:T(8,128)}) %reduce-scatter.3.cloned.1.call-update) | async-done | bytes 65552 | tf_op jit(solution)/shard_map/reduce_scatter | solution.py:29
  36.9 0.0 copy-done.4
  36.9 0.0 copy-done.5
  36.9 1.5 %multiply_convert_fusion = (bf16[128,128]{1,0:T(8,128)(2,1)S(1)}, bf16[128,128]{1,0:T(8,128)(2,1)}) fusion(bf16[128,128]{1,0:T(8,128)(2,1)S(1)} %copy-done.4, f32[128,128]{1,0:T(8,128)} %reduce-scatter.3.cloned.1.call-done, f32[128]{0:T(128)S(1)} %copy-done.5), kind=kLoop, calls=%fused_computation.10 | loop fusion | flops 212992 | bytes 164352 | tf_op jit(solution)/shard_map/convert_element_type | solution.py:32
  38.4 4.6 %all_gather.7 = bf16[256,128]{1,0:T(8,128)(2,1)S(1)} all-gather(bf16[128,128]{1,0:T(8,128)(2,1)S(1)} %get-tuple-element.6), channel_id=1, replica_groups=mesh['groups'=2,'dom'=4,'rep'=2,'sub'=2] {'rep'}, dimensions={0}, use_global_device_ids=true | all-gather | bytes 98304 | tf_op jit(solution)/shard_map/all_gather | solution.py:35
  43.0 1.0 fusion.1
  44.0 0.0 reduce-scatter.5.cloned.1.call-update
  44.0 0.0 all-reduce.2.cloned.1.call-start
  44.0 19.8 %reduce-scatter.5.cloned.1.call-done = f32[128,128]{1,0:T(8,128)} async-done(((f32[512,128]{1,0:T(8,128)}), f32[128,128]{1,0:T(8,128)}) %reduce-scatter.5.cloned.1.call-update) | async-done | bytes 65552 | tf_op jit(solution)/shard_map/reduce_scatter | solution.py:37
  63.8 0.0 copy-start.3
  63.8 1.7 %fusion = f32[128,128]{0,1:T(8,128)} fusion(f32[128,128]{1,0:T(8,128)} %reduce-scatter.5.cloned.1.call-done, bf16[128,128]{1,0:T(8,128)(2,1)S(1)} %copy-done), kind=kOutput, calls=%fused_computation.1 | convolution fusion | flops 25182208 | bytes 163840 | tf_op jit(solution)/shard_map/dot_general | solution.py:46
  65.5 0.0 copy-start.2
  65.6 0.0 all-reduce.2.cloned.1.call-update
  65.6 0.0 copy-done.3
  65.6 0.8 copy-done.2
  66.4 0.2 fusion.7
  66.6 4.2 %psum.14 = bf16[128,128]{1,0:T(8,128)(2,1)} all-reduce(f32[128,128]{1,0:T(8,128)S(1)} %fusion.7), channel_id=1, replica_groups=mesh['groups'=2,'dom'=4,'rep'=2,'sub'=2] {'sub'}, use_global_device_ids=true, to_apply=%region_2.0 | all-reduce | flops 16384 | bytes 98304 | tf_op jit(solution)/shard_map/psum | solution.py:59
  70.8 64.2 %all-reduce.2.cloned.1.call-done = f32[128,128]{0,1:T(8,128)} async-done(((f32[128,128]{0,1:T(8,128)}), f32[128,128]{0,1:T(8,128)}) %all-reduce.2.cloned.1.call-update) | async-done | bytes 65552 | tf_op jit(solution)/shard_map/psum | solution.py:52
  134.9 1.6 %copy.9 = f32[128,128]{1,0:T(8,128)} copy(f32[128,128]{0,1:T(8,128)} %all-reduce.2.cloned.1.call-done) | data formatting | bytes 131072
  (2 shorter events, 0.0 us)
Async XLA Ops:
  7.2 0.8 copy-start
  7.2 16.7 %copy-start.1 = (bf16[256,4,128]{2,1,0:T(4,128)(2,1)S(1)}, bf16[256,4,128]{2,1,0:T(4,128)(2,1)}, u32[]{:S(2)}) copy-start(bf16[256,4,128]{2,1,0:T(4,128)(2,1)} %param.6) | copy-start | bytes 786436
  7.2 29.7 %reduce-scatter.3.cloned.1.call-start = ((), (), s32[]{:S(2)}) async-start(), calls=%async_computation.2 | async-start | bytes 196608 | tf_op jit(solution)/shard_map/reduce_scatter | solution.py:29
  25.1 11.8 %copy-start.4 = (bf16[128,128]{1,0:T(8,128)(2,1)S(1)}, bf16[128,128]{1,0:T(8,128)(2,1)}, u32[]{:S(2)}) copy-start(bf16[128,128]{1,0:T(8,128)(2,1)} %param.11) | copy-start | bytes 98308
  25.1 11.8 %copy-start.5 = (f32[128]{0:T(128)S(1)}, f32[128]{0:T(128)}, u32[]{:S(2)}) copy-start(f32[128]{0:T(128)} %param.10) | copy-start | bytes 1540
  25.2 38.6 %reduce-scatter.5.cloned.1.call-start = ((), (), s32[]{:S(2)}) async-start(), calls=%async_computation.3 | async-start | bytes 327680 | tf_op jit(solution)/shard_map/reduce_scatter | solution.py:37
  44.0 90.9 %all-reduce.2.cloned.1.call-start = ((), (), s32[]{:S(2)}) async-start(), calls=%async_computation.4 | async-start | bytes 131072 | tf_op jit(solution)/shard_map/psum | solution.py:52
  63.8 1.8 %copy-start.3 = (bf16[128,128]{1,0:T(8,128)(2,1)S(1)}, bf16[128,128]{1,0:T(8,128)(2,1)}, u32[]{:S(2)}) copy-start(bf16[128,128]{1,0:T(8,128)(2,1)} %param.9) | copy-start | bytes 98308
  65.5 0.8 copy-start.2
Sparse Core Ops, SparseCore 0:
  25.3 11.5 reduce-scatter.2
  44.1 19.6 reduce-scatter.4
  68.2 66.6 all-reduce.1
where the time goes:
time: 143 us
  waiting for transfers between devices  95.7 us (67%)
  blocking collectives  23.8 us (17%)
  between operations  13.8 us (10%)
  matrix products  4.65 us (3%)
  other arithmetic  2.55 us (2%)
  local copies, waits for them, and re-layouts  2.41 us (2%)
    psum x1, waiting for transfers between devices, on_device(): grad_weight = lax.psum(weight_term, ('dom', 'rep'))  64.2 us
    reduce_scatter x1, waiting for transfers between devices, on_device(): lax.psum_scatter(lax.dot_general(columns, block_grads, (((0,), (0,)), (()...  19.8 us
    all_gather x1, blocking collectives, on_device(): lax.all_gather(support, 'dom', axis=0, tiled=True)  15.1 us
    reduce_scatter x1, waiting for transfers between devices, on_device(): lax.psum_scatter(partial_value, 'rep', scatter_dimension=0, tiled=True)  11.7 us
    all_gather x1, blocking collectives, on_device(): block_grads = lax.all_gather(grad_pre, 'rep', axis=0, tiled=True)  4.58 us
    psum x1, blocking collectives, on_device(): grad_input = lax.psum(input_term, 'sub').astype(jnp.bfloat16)  4.17 us
  transfers between devices with their start and end apart: 3, of which 3 were waited for; matrix products, arithmetic and copies ran while one was open for 0% of the time, Pallas kernels for 0%

commit v1 on v0

v1 whole, which is shorter than its diff:
```python
import math

import jax
import jax.numpy as jnp
from jax import lax
from jax.experimental import pallas as pl
from jax.experimental.pallas import tpu as pltpu
from jax.sharding import PartitionSpec as P

CHIPS = ("dom", "rep")
CORES = ("dom", "rep", "sub")
F32 = jnp.float32
BF16 = jnp.bfloat16


def forward_and_gp(operator, features, weight, bias, cotangent):
    z = jnp.dot(operator, features, preferred_element_type=F32)
    high = z.astype(BF16)
    low = (z - high.astype(F32)).astype(BF16)
    both = jnp.concatenate([high, low], axis=1)
    pre = jnp.dot(both, jnp.concatenate([weight, weight], axis=0), preferred_element_type=F32) + bias
    sigma = jax.nn.sigmoid(pre)
    activation = (pre * sigma).astype(BF16)
    grad_pre = (cotangent.astype(F32) * sigma * (1.0 + pre * (1.0 - sigma))).astype(BF16)
    back = lax.dot_general(
        grad_pre, weight, (((1,), (1,)), ((), ())), preferred_element_type=F32
    ).astype(BF16)
    return high, low, activation, grad_pre, back


def weight_term(high, low, grads):
    return lax.dot_general(
        jnp.concatenate([high, low], axis=0),
        jnp.concatenate([grads, grads], axis=0),
        (((0,), (0,)), ((), ())),
        preferred_element_type=F32,
    )


def masked_rows(adjacency, mask, which, nodes):
    _, sections, width = adjacency.shape
    per = mask.shape[0] * nodes // adjacency.shape[0]
    rows = lax.dynamic_slice_in_dim(adjacency, which * nodes, nodes, axis=0)
    flags = lax.dynamic_slice_in_dim(mask, which * per, per, axis=0).astype(BF16)
    flags = jnp.broadcast_to(
        flags[:, None, :, :, None],
        (per, nodes // per, sections, mask.shape[2], width // mask.shape[2]),
    ).reshape(nodes, sections, width)
    return (rows * flags).transpose(1, 0, 2)


def general(mesh, adjacency, mask, features, weight, bias, cotangent):
    reps = mesh.shape["rep"]
    nodes, width = features.shape[0], adjacency.shape[2]
    sections = adjacency.shape[1]
    pieces = jnp.stack([masked_rows(adjacency, mask, q, nodes) for q in range(reps)])
    pieces = lax.all_to_all(pieces, "rep", 0, 0, tiled=True)
    operator = pieces.transpose(2, 1, 0, 3).reshape(nodes, sections * reps * width)
    everyone = lax.all_gather(features, CHIPS, axis=0, tiled=True)
    whole_weight = lax.all_gather(weight, "sub", axis=1, tiled=True)
    whole_bias = lax.all_gather(bias, "sub", axis=0, tiled=True)
    whole_cotangent = lax.all_gather(cotangent, "sub", axis=1, tiled=True)
    high, low, activation, grad_pre, back = forward_and_gp(
        operator, everyone, whole_weight, whole_bias[None, :], whole_cotangent
    )
    half = weight.shape[1]
    mine = lax.axis_index("sub") * half
    activation = lax.dynamic_slice_in_dim(activation, mine, half, axis=1)
    grads = lax.dynamic_slice_in_dim(grad_pre, mine, half, axis=1)
    total = lax.psum(weight_term(high, low, grads), CHIPS)
    backs = lax.all_gather(back, CHIPS, axis=0, tiled=True)
    grad_input = jnp.dot(operator, backs, preferred_element_type=F32).astype(BF16)
    return activation, grad_input, total / math.sqrt(sections * reps * width)


SHARED = (((3, 1), (2, 1)), ((2, 0), (3, 0)), ((1, 0), (1, 1)))


def fetch(value, first, second=None):
    pairs = []
    for d in range(4):
        for r in range(2):
            for c, off in enumerate((first, first if second is None else second)):
                source = (d * 2 + r) * 2 + c
                pairs.append((source, ((d ^ off[0]) * 2 + (r ^ off[1])) * 2 + c))
    return lax.ppermute(value, CORES, pairs)


def swap(value):
    return lax.ppermute(value, "sub", [(0, 1), (1, 0)])


def vmem_call(body, outs, *operands):
    return pl.pallas_call(
        body,
        out_shape=outs,
        in_specs=[pl.BlockSpec(memory_space=pltpu.VMEM)] * len(operands),
        out_specs=[pl.BlockSpec(memory_space=pltpu.VMEM)] * len(outs),
    )(*operands)


def in_order(first, second):
    zero = lax.axis_index("sub") == 0
    return jnp.where(zero, first, second), jnp.where(zero, second, first)


def operator_rows(own, other, offsets):
    d = lax.axis_index("dom")
    return jnp.concatenate([(other if rx else own)[d ^ dx] for dx, rx in offsets], axis=1)


def ordered_offsets(pairs):
    return [off for pair in pairs for off in pair]


def forward_kernel(own, other, x, x0, x1, x2, y0, y1, y2, w, w_, b, b_, g, g_, act, msg):
    n = x.shape[0]
    blocks = [x[...], other[4]]
    for direct, swapped in ((x0, y0), (x1, y1), (x2, y2)):
        blocks += in_order(direct[...], swapped[...])
    rows = operator_rows(own, other, [(0, 0), (0, 1)] + ordered_offsets(SHARED))
    weight = jnp.concatenate(in_order(w[...], w_[...]), axis=1)
    bias = jnp.concatenate(in_order(b[...], b_[...]), axis=1)
    cotangent = jnp.concatenate(in_order(g[...], g_[...]), axis=1)
    high, low, activation, grad_pre, back = forward_and_gp(
        rows, jnp.concatenate(blocks, axis=0), weight, bias, cotangent
    )
    half = w.shape[1]
    zero = lax.axis_index("sub") == 0
    act[...] = jnp.where(zero, activation[:, :half], activation[:, half:])
    grads = jnp.where(zero, grad_pre[:, :half], grad_pre[:, half:])
    term = weight_term(high, low, grads)
    msg[:n] = back
    upper = term.astype(BF16)
    msg[n : 2 * n] = upper
    msg[2 * n :] = (term - upper.astype(F32)).astype(BF16)


NEAR = ((0, 1), (1, 0), (1, 1))
FAR = SHARED[:2]


def plane_sum_kernel(n, a, b, c, d, out):
    def term(ref):
        return ref[n : 2 * n].astype(F32) + ref[2 * n :].astype(F32)

    out[...] = (term(a) + term(b)) + (term(c) + term(d))


def backward_kernel(own, other, m, m0, m1, m2, v0, v1, u0, u1, gi):
    n = own.shape[1]
    blocks = [m[:n], m0[:n], m1[:n], m2[:n]]
    for direct, swapped in ((v0, u0), (v1, u1)):
        blocks += in_order(direct[...], swapped[...])
    rows = operator_rows(own, other, [(0, 0)] + list(NEAR) + ordered_offsets(FAR))
    gi[...] = jnp.dot(rows, jnp.concatenate(blocks, axis=0), preferred_element_type=F32).astype(BF16)


def direct(mesh, adjacency, mask, features, weight, bias, cotangent):
    nodes, feat = features.shape
    sections, width = adjacency.shape[1:]
    half = weight.shape[1]
    r = lax.axis_index("rep")

    xs = [fetch(features, *pair) for pair in SHARED]
    give = masked_rows(adjacency, mask, 1 - r, nodes)
    other = fetch(jnp.concatenate([give, features[None]], axis=0), (0, 1))
    own = masked_rows(adjacency, mask, r, nodes)
    row = bias[None, :]
    w_, b_, g_ = swap(weight), swap(row), swap(cotangent)
    ys = [swap(x) for x in xs]
    act, msg = vmem_call(
        forward_kernel,
        [
            jax.ShapeDtypeStruct((nodes, half), BF16),
            jax.ShapeDtypeStruct((nodes + 2 * feat, half), BF16),
        ],
        own, other, features, *xs, *ys, weight, w_, row, b_, cotangent, g_,
    )
    near = [fetch(msg, off) for off in NEAR]
    back = msg[:nodes]
    far = [fetch(back, *pair) for pair in FAR]
    (plane,) = vmem_call(
        lambda *refs: plane_sum_kernel(nodes, *refs),
        [jax.ShapeDtypeStruct((feat, half), F32)],
        msg, *near,
    )
    across = fetch(plane, (2, 0))
    swapped = [swap(v) for v in far]
    (grad_input,) = vmem_call(
        backward_kernel,
        [jax.ShapeDtypeStruct((nodes, feat), BF16)],
        own, other, msg, *near, *far, *swapped,
    )
    total = (plane + across) / math.sqrt(sections * 2 * width)
    return act, grad_input, total


def solution(mesh):
    small = dict(mesh.shape) == {"groups": mesh.shape["groups"], "dom": 4, "rep": 2, "sub": 2}
    body = direct if small else general
    return jax.shard_map(
        lambda *arrays: body(mesh, *arrays),
        mesh=mesh,
        in_specs=(
            P(("groups", "dom"), None, "rep"),
            P(("groups", "dom"), None, "rep"),
            P(("groups", "dom", "rep"), None),
            P(None, "sub"),
            P("sub"),
            P(("groups", "dom", "rep"), "sub"),
        ),
        out_specs=(
            P(("groups", "dom", "rep"), "sub"),
            P(("groups", "dom", "rep"), None),
            P("groups", "sub"),
        ),
        check_vma=False,
    )
```

time: 143 us -> 39.3 us (0.27)
  waiting for transfers between devices: 95.7 us -> 6.26 us
  blocking collectives: 23.8 us -> 0 us
  starting transfers between devices: 0.12 us -> 17.8 us
  between operations: 13.8 us -> 0.82 us
  Pallas kernels: 0 us -> 6.03 us
  matrix products: 4.65 us -> 0 us
  local copies, waits for them, and re-layouts: 2.41 us -> 6.52 us
    psum x1 -> x0, waiting for transfers between devices: 64.2 us -> none  [on_device(): grad_weight = lax.psum(weight_term, ('dom', 'rep'))]
    reduce_scatter x2 -> x0, waiting for transfers between devices: 31.5 us -> none  [the longest x1 19.8 us: on_device(): lax.psum_scatter(lax.dot_general(columns, block_grads, (((0,), (0,)), (()...]
    all_gather x2 -> x0, blocking collectives: 19.6 us -> none  [the longest x1 15.1 us: on_device(): lax.all_gather(support, 'dom', axis=0, tiled=True)]
    ppermute x0 -> x18, starting transfers between devices: none -> 17.8 us  [the longest x10 16.6 us: fetch(): return lax.ppermute(value, CORES, pairs)]
    ppermute x0 -> x18, waiting for transfers between devices: none -> 6.26 us  [the longest x10 4.73 us: fetch(): return lax.ppermute(value, CORES, pairs)]
    pallas_call x0 -> x3, Pallas kernels: none -> 6.03 us  [vmem_call(): pl.pallas_call(body, out_shape=outs, in_specs=[pl.BlockSpec(memory_space=...]
    dot_general x5 -> x0, matrix products: 4.65 us -> none  [the longest x1 1.73 us: on_device(): lax.dot_general(features.astype(jnp.float32), gradient_of_support, (((0,)...]
    psum x1 -> x0, blocking collectives: 4.17 us -> none  [on_device(): grad_input = lax.psum(input_term, 'sub').astype(jnp.bfloat16)]
  transfers between devices with their start and end apart: 3 -> 18, of which waited for: 3 -> 5; matrix products, arithmetic and copies ran while one was open for 0% -> 7% of each run, Pallas kernels for 0% -> 10%
where the time goes in v1:
time: 39.3 us; the launch traced here: 38.9 us
  starting transfers between devices  17.8 us (45%)
  local copies, waits for them, and re-layouts  6.52 us (17%)
  waiting for transfers between devices  6.26 us (16%)
  Pallas kernels  6.03 us (15%)
  other arithmetic  1.47 us (4%)
  between operations  0.82 us (2%)
    ppermute x10, starting transfers between devices, fetch(): return lax.ppermute(value, CORES, pairs)  16.6 us
    pallas_call x3, Pallas kernels, vmem_call(): pl.pallas_call(body, out_shape=outs, in_specs=[pl.BlockSpec(memory_space=...  6.03 us
    ppermute x10, waiting for transfers between devices, fetch(): return lax.ppermute(value, CORES, pairs)  4.73 us
    unnamed x44, local copies, waits for them, and re-layouts  4.67 us
    ppermute x8, waiting for transfers between devices, swap(): return lax.ppermute(value, 'sub', [(0, 1), (1, 0)])  1.53 us
    ppermute x8, starting transfers between devices, swap(): return lax.ppermute(value, 'sub', [(0, 1), (1, 0)])  1.16 us
    dynamic_slice x1, local copies, waits for them, and re-layouts, masked_rows(): rows = lax.dynamic_slice_in_dim(adjacency, which * nodes, nodes, axis=0)  1.06 us
    transpose x2, other arithmetic, masked_rows(): return (rows * flags).transpose(1, 0, 2)  0.81 us
  transfers between devices with their start and end apart: 18, of which 5 were waited for; matrix products, arithmetic and copies ran while one was open for 7% of the time, Pallas kernels for 10%

profile of v1, /device:TPU:0, one launch (start us, length us, event | category | flops | bytes accessed | tf_op | source)
XLA Modules:
  0.0 38.9 jit_solution(10467768928595753637)
XLA Ops:
  0.6 0.0 copy-start.20
  0.6 4.1 %collective-permute-start.2 = (bf16[128,128]{1,0:T(8,128)(2,1)}, bf16[128,128]{1,0:T(8,128)(2,1)S(1)}, u32[]{:S(2)}, u32[]{:S(2)}) collective-permute-start(bf16[128,128]{1,0:T(8,128)(2,1)} %x.1), channel_id=1, source_target_pairs={{0,8},{1,13},{2,10},{3,15},{4,12},{5,9},{6,14},{7,11},{8,0},{9,5},... | collective-permute-start | bytes 98312 | tf_op jit(solution)/shard_map/ppermute | solution.py:86
  4.7 2.3 %collective-permute-start.1 = (bf16[128,128]{1,0:T(8,128)(2,1)}, bf16[128,128]{1,0:T(8,128)(2,1)S(1)}, u32[]{:S(2)}, u32[]{:S(2)}) collective-permute-start(bf16[128,128]{1,0:T(8,128)(2,1)} %x.1), channel_id=1, source_target_pairs={{0,14},{1,11},{2,12},{3,9},{4,10},{5,15},{6,8},{7,13},{8,6},{9,3},... | collective-permute-start | bytes 98312 | tf_op jit(solution)/shard_map/ppermute | solution.py:86
  7.0 0.0 collective-permute-start.3
  7.0 0.0 copy-done.20
  7.0 0.0 collective-permute-start.8
  7.0 0.5 %collective-permute-start.7 = (bf16[128,128]{1,0:T(8,128)(2,1)}, bf16[128,128]{1,0:T(8,128)(2,1)S(1)}, u32[]{:S(2)}, u32[]{:S(2)}) collective-permute-start(bf16[128,128]{1,0:T(8,128)(2,1)} %w.1), channel_id=1, source_target_pairs={{0,1},{1,0},{2,3},{3,2},{4,5},{5,4},{6,7},{7,6},{8,9},{9,8},{10,11... | collective-permute-start | bytes 98312 | tf_op jit(solution)/shard_map/ppermute | solution.py:90
  7.5 0.7 %copy-done.19 = s32[2,4,1]{1,2,0:T(1,128)S(1)} copy-done((s32[2,4,1]{1,2,0:T(1,128)S(1)}, s32[2,4,1]{1,2,0:T(1,128)}, u32[]{:S(2)}) %copy-start.19) | copy-done | bytes 56
  8.2 1.1 %constant_dynamic-slice_fusion.1 = (bf16[128,4,128]{2,1,0:T(4,128)(2,1)S(1)}, bf16[128,4,128]{2,1,0:T(4,128)(2,1)S(1)}) fusion(bf16[256,4,128]{2,1,0:T(4,128)(2,1)} %param.6, s32[]{:T(128)S(6)} %select_n.14, s32[]{:T(128)S(6)} %select_n.12), kind=kLoop, calls=%fused_computation.7 | loop fusion | bytes 524296 | tf_op jit(solution)/shard_map/dynamic_slice | solution.py:43
  9.3 0.0 copy-start.5
  9.3 0.1 fusion
  9.4 0.7 %copy-done.5 = bf16[128,128]{1,0:T(8,128)(2,1)S(1)} copy-done((bf16[128,128]{1,0:T(8,128)(2,1)S(1)}, bf16[128,128]{1,0:T(8,128)(2,1)}, u32[]{:S(2)}) %copy-start.5) | copy-done | bytes 32792
  10.1 0.0 collective-permute-done.8.b_
  10.1 0.7 %copy-done.6 = bf16[128,128]{1,0:T(8,128)(2,1)S(1)} copy-done((bf16[128,128]{1,0:T(8,128)(2,1)S(1)}, bf16[128,128]{1,0:T(8,128)(2,1)}, u32[]{:S(2)}) %copy-start.6) | copy-done | bytes 32792
  10.8 0.1 collective-permute-start.9
  10.9 0.0 collective-permute-done.7.w_
  10.9 1.0 %collective-permute-start = (bf16[5,128,128]{2,1,0:T(8,128)(2,1)S(1)}, bf16[5,128,128]{2,1,0:T(8,128)(2,1)S(1)}, u32[]{:S(2)}, u32[]{:S(2)}) collective-permute-start(bf16[5,128,128]{2,1,0:T(8,128)(2,1)S(1)} %pad_maximum_fusion), channel_id=1, source_target_pairs={{0,2},{1,3},{2,0},{3,1},{4,6},{5,7},{6,4},{7,5},{8,10},{9,11},{10,... | collective-permute-start | bytes 491528 | tf_op jit(solution)/shard_map/ppermute | solution.py:86
  11.9 0.0 collective-permute-done.2.x1
  11.9 0.0 collective-permute-start.5
  11.9 0.0 collective-permute-done.1.x0
  11.9 0.0 copy-start.8
  11.9 0.5 %collective-permute-start.4 = (bf16[128,128]{1,0:T(8,128)(2,1)S(1)}, bf16[128,128]{1,0:T(8,128)(2,1)S(1)}, u32[]{:S(2)}, u32[]{:S(2)}) collective-permute-start(bf16[128,128]{1,0:T(8,128)(2,1)S(1)} %collective-permute-done.1.x0), channel_id=1, source_target_pairs={{0,1},{1,0},{2,3},{3,2},{4,5},{5,4},{6,7},{7,6},{8,9},{9,8},{10,11... | collective-permute-start | bytes 98312 | tf_op jit(solution)/shard_map/ppermute | solution.py:90
  12.4 0.0 collective-permute-done.3.x2
  12.4 0.1 collective-permute-start.6
  12.5 0.0 copy-done.21
  12.5 0.7 %fusion.1.own = bf16[4,128,128]{2,1,0:T(8,128)(2,1)} fusion(bf16[128,4,128]{2,1,0:T(4,128)(2,1)S(1)} %get-tuple-element.8, bf16[4]{0:T(256)(128)(2,1)S(1)} %get-tuple-element.10), kind=kLoop, calls=%fused_computation.4 | loop fusion | flops 65536 | bytes 262152 | tf_op jit(solution)/shard_map/transpose | solution.py:49
  13.2 0.0 copy-done.10
  13.2 0.0 copy-done.7
  13.2 0.0 copy-done.8
  13.2 0.0 collective-permute-done.9.g_
  13.2 0.0 copy-start.11
  13.2 0.0 collective-permute-done.5.y1
  13.3 0.0 collective-permute-done.4.y0
  13.3 0.3 collective-permute-done.6.y2
  13.6 3.8 %collective-permute-done.other = bf16[5,128,128]{2,1,0:T(8,128)(2,1)S(1)} collective-permute-done((bf16[5,128,128]{2,1,0:T(8,128)(2,1)S(1)}, bf16[5,128,128]{2,1,0:T(8,128)(2,1)S(1)}, u32[]{:S(2)}, u32[]{:S(2)}) %collective-permute-start) | collective-permute-done | bytes 163872 | tf_op jit(solution)/shard_map/ppermute | solution.py:86
  17.4 0.0 copy-done.11
  17.4 0.0 copy-done.13
  17.5 0.6 %copy-done = bf16[5,128,128]{2,1,0:T(8,128)(2,1)} copy-done((bf16[5,128,128]{2,1,0:T(8,128)(2,1)}, bf16[5,128,128]{2,1,0:T(8,128)(2,1)S(1)}, u32[]{:S(2)}) %copy-start) | copy-done | bytes 163864
  18.1 2.3 %shard_map.85 = (bf16[128,128]{1,0:T(8,128)(2,1)}, bf16[384,128]{1,0:T(8,128)(2,1)}) custom-call(bf16[4,128,128]{2,1,0:T(8,128)(2,1)} %fusion.1.own, bf16[5,128,128]{2,1,0:T(8,128)(2,1)} %copy-done, bf16[128,128]{1,0:T(8,128)(2,1)} %x.1, bf16[128,128]{1,0:T(8,128)(2,1)} %copy-done.8, bf16[128,128]{1,0:T(8,128)(2,1)} %copy-done.7, ...), custom_call_target="tpu_custom_call" | custom-call | tf_op jit(solution)/shard_map/pallas_call | solution.py:94
  20.4 2.0 %collective-permute-start.12 = (bf16[384,128]{1,0:T(8,128)(2,1)}, bf16[384,128]{1,0:T(8,128)(2,1)S(1)}, u32[]{:S(2)}, u32[]{:S(2)}) collective-permute-start(bf16[384,128]{1,0:T(8,128)(2,1)} %get-tuple-element.6.m.refs_0_), channel_id=1, source_target_pairs={{0,6},{1,7},{2,4},{3,5},{4,2},{5,3},{6,0},{7,1},{8,14},{9,15},{10,... | collective-permute-start | bytes 294920 | tf_op jit(solution)/shard_map/ppermute | solution.py:86
  22.4 0.2 collective-permute-start.11
  22.7 1.3 %collective-permute-start.10 = (bf16[384,128]{1,0:T(8,128)(2,1)}, bf16[384,128]{1,0:T(8,128)(2,1)S(1)}, u32[]{:S(2)}, u32[]{:S(2)}) collective-permute-start(bf16[384,128]{1,0:T(8,128)(2,1)} %get-tuple-element.6.m.refs_0_), channel_id=1, source_target_pairs={{0,2},{1,3},{2,0},{3,1},{4,6},{5,7},{6,4},{7,5},{8,10},{9,11},{10,... | collective-permute-start | bytes 294920 | tf_op jit(solution)/shard_map/ppermute | solution.py:86
  23.9 0.8 %slice.3 = bf16[128,128]{1,0:T(8,128)(2,1)S(1)} slice(bf16[384,128]{1,0:T(8,128)(2,1)} %get-tuple-element.6.m.refs_0_), slice={[0:128], [0:128]} | slice | bytes 65536 | tf_op jit(solution)/shard_map/slice | solution.py:181
  24.7 3.0 %collective-permute-start.14 = (bf16[128,128]{1,0:T(8,128)(2,1)S(1)}, bf16[128,128]{1,0:T(8,128)(2,1)S(1)}, u32[]{:S(2)}, u32[]{:S(2)}) collective-permute-start(bf16[128,128]{1,0:T(8,128)(2,1)S(1)} %slice.3), channel_id=1, source_target_pairs={{0,8},{1,13},{2,10},{3,15},{4,12},{5,9},{6,14},{7,11},{8,0},{9,5},... | collective-permute-start | bytes 98312 | tf_op jit(solution)/shard_map/ppermute | solution.py:86
  27.8 1.3 %collective-permute-start.13 = (bf16[128,128]{1,0:T(8,128)(2,1)S(1)}, bf16[128,128]{1,0:T(8,128)(2,1)S(1)}, u32[]{:S(2)}, u32[]{:S(2)}) collective-permute-start(bf16[128,128]{1,0:T(8,128)(2,1)S(1)} %slice.3), channel_id=1, source_target_pairs={{0,14},{1,11},{2,12},{3,9},{4,10},{5,15},{6,8},{7,13},{8,6},{9,3},... | collective-permute-start | bytes 98312 | tf_op jit(solution)/shard_map/ppermute | solution.py:86
  29.1 0.0 collective-permute-done.12.m2.refs_3_
  29.1 0.0 collective-permute-done.11.m1.refs_2_
  29.1 0.0 collective-permute-done.10.m0.refs_1_
  29.1 0.6 %copy-done.1 = bf16[384,128]{1,0:T(8,128)(2,1)} copy-done((bf16[384,128]{1,0:T(8,128)(2,1)}, bf16[384,128]{1,0:T(8,128)(2,1)S(1)}, u32[]{:S(2)}) %copy-start.1) | copy-done | bytes 98328
  29.7 0.0 copy-done.2
  29.7 0.6 %copy-done.3 = bf16[384,128]{1,0:T(8,128)(2,1)} copy-done((bf16[384,128]{1,0:T(8,128)(2,1)}, bf16[384,128]{1,0:T(8,128)(2,1)S(1)}, u32[]{:S(2)}) %copy-start.3) | copy-done | bytes 98328
  30.4 1.7 %shard_map.87 = f32[128,128]{1,0:T(8,128)} custom-call(bf16[384,128]{1,0:T(8,128)(2,1)} %get-tuple-element.6.m.refs_0_, bf16[384,128]{1,0:T(8,128)(2,1)} %copy-done.3, bf16[384,128]{1,0:T(8,128)(2,1)} %copy-done.2, bf16[384,128]{1,0:T(8,128)(2,1)} %copy-done.1), custom_call_target="tpu_custom_call" | custom-call | tf_op jit(solution)/shard_map/pallas_call | solution.py:94
  32.1 1.4 %collective-permute-start.17 = (f32[128,128]{1,0:T(8,128)}, f32[128,128]{1,0:T(8,128)S(1)}, u32[]{:S(2)}, u32[]{:S(2)}) collective-permute-start(f32[128,128]{1,0:T(8,128)} %shard_map.87), channel_id=1, source_target_pairs={{0,8},{1,9},{2,10},{3,11},{4,12},{5,13},{6,14},{7,15},{8,0},{9,1},... | collective-permute-start | bytes 196616 | tf_op jit(solution)/shard_map/ppermute | solution.py:86
  33.5 0.0 collective-permute-done.14.v1
  33.5 0.0 collective-permute-start.16
  33.5 0.9 %collective-permute-done.13.v0 = bf16[128,128]{1,0:T(8,128)(2,1)S(1)} collective-permute-done((bf16[128,128]{1,0:T(8,128)(2,1)S(1)}, bf16[128,128]{1,0:T(8,128)(2,1)S(1)}, u32[]{:S(2)}, u32[]{:S(2)}) %collective-permute-start.13) | collective-permute-done | bytes 32800 | tf_op jit(solution)/shard_map/ppermute | solution.py:86
  34.4 0.0 collective-permute-start.15
  34.4 0.3 collective-permute-done.16.u1
  34.7 0.9 %collective-permute-done.15.u0 = bf16[128,128]{1,0:T(8,128)(2,1)S(1)} collective-permute-done((bf16[128,128]{1,0:T(8,128)(2,1)S(1)}, bf16[128,128]{1,0:T(8,128)(2,1)S(1)}, u32[]{:S(2)}, u32[]{:S(2)}) %collective-permute-start.15) | collective-permute-done | bytes 32800 | tf_op jit(solution)/shard_map/ppermute | solution.py:90
  35.6 0.0 copy-done.17
  35.6 0.6 %copy-done.18 = bf16[128,128]{1,0:T(8,128)(2,1)} copy-done((bf16[128,128]{1,0:T(8,128)(2,1)}, bf16[128,128]{1,0:T(8,128)(2,1)S(1)}, u32[]{:S(2)}) %copy-start.18) | copy-done | bytes 32792
  36.2 2.0 %shard_map.86 = bf16[128,128]{1,0:T(8,128)(2,1)} custom-call(bf16[4,128,128]{2,1,0:T(8,128)(2,1)} %fusion.1.own, bf16[5,128,128]{2,1,0:T(8,128)(2,1)} %copy-done, bf16[384,128]{1,0:T(8,128)(2,1)} %get-tuple-element.6.m.refs_0_, bf16[384,128]{1,0:T(8,128)(2,1)} %copy-done.3, bf16[384,128]{1,0:T(8,128)(2,1)} %copy-done.2, bf16[384,128]{1,0:T(8,128)(2,1)} %copy-done.1, ...), custom_call_target="tpu_custom_call" | custom-call | tf_op jit(solution)/shard_map/pallas_call | solution.py:94
  38.2 0.0 collective-permute-done.17
  38.3 0.6 %add_multiply_fusion = f32[128,128]{1,0:T(8,128)} fusion(f32[128,128]{1,0:T(8,128)S(1)} %copy-done.4, f32[128,128]{1,0:T(8,128)S(1)} %collective-permute-done.17), kind=kLoop, calls=%fused_computation.5 | loop fusion | flops 32768 | bytes 196608 | tf_op jit(solution)/shard_map/div | solution.py:195
  (26 shorter events, 0.1 us)
Async XLA Ops:
  0.6 6.4 %copy-start.20 = (f32[128]{0:T(128)S(1)}, f32[128]{0:T(128)}, u32[]{:S(2)}) copy-start(f32[128]{0:T(128)} %param.10) | copy-start | bytes 1540
  0.6 11.2 %collective-permute-start.2 = (bf16[128,128]{1,0:T(8,128)(2,1)}, bf16[128,128]{1,0:T(8,128)(2,1)S(1)}, u32[]{:S(2)}, u32[]{:S(2)}) collective-permute-start(bf16[128,128]{1,0:T(8,128)(2,1)} %x.1), channel_id=1, source_target_pairs={{0,8},{1,13},{2,10},{3,15},{4,12},{5,9},{6,14},{7,11},{8,0},{9,5},... | collective-permute-start | bytes 98312 | tf_op jit(solution)/shard_map/ppermute | solution.py:86
  4.7 7.1 %collective-permute-start.1 = (bf16[128,128]{1,0:T(8,128)(2,1)}, bf16[128,128]{1,0:T(8,128)(2,1)S(1)}, u32[]{:S(2)}, u32[]{:S(2)}) collective-permute-start(bf16[128,128]{1,0:T(8,128)(2,1)} %x.1), channel_id=1, source_target_pairs={{0,14},{1,11},{2,12},{3,9},{4,10},{5,15},{6,8},{7,13},{8,6},{9,3},... | collective-permute-start | bytes 98312 | tf_op jit(solution)/shard_map/ppermute | solution.py:86
  7.0 5.4 %collective-permute-start.3 = (bf16[128,128]{1,0:T(8,128)(2,1)}, bf16[128,128]{1,0:T(8,128)(2,1)S(1)}, u32[]{:S(2)}, u32[]{:S(2)}) collective-permute-start(bf16[128,128]{1,0:T(8,128)(2,1)} %x.1), channel_id=1, source_target_pairs={{0,4},{1,7},{2,6},{3,5},{4,0},{5,3},{6,2},{7,1},{8,12},{9,15},{10,... | collective-permute-start | bytes 98312 | tf_op jit(solution)/shard_map/ppermute | solution.py:86
  7.0 3.0 %collective-permute-start.8 = (f32[1,128]{1,0:T(1,128)S(1)}, f32[1,128]{1,0:T(1,128)S(1)}, u32[]{:S(2)}, u32[]{:S(2)}) collective-permute-start(f32[1,128]{1,0:T(1,128)S(1)} %bitcast.12), channel_id=1, source_target_pairs={{0,1},{1,0},{2,3},{3,2},{4,5},{5,4},{6,7},{7,6},{8,9},{9,8},{10,11... | collective-permute-start | bytes 1544 | tf_op jit(solution)/shard_map/ppermute | solution.py:90
  7.0 3.8 %collective-permute-start.7 = (bf16[128,128]{1,0:T(8,128)(2,1)}, bf16[128,128]{1,0:T(8,128)(2,1)S(1)}, u32[]{:S(2)}, u32[]{:S(2)}) collective-permute-start(bf16[128,128]{1,0:T(8,128)(2,1)} %w.1), channel_id=1, source_target_pairs={{0,1},{1,0},{2,3},{3,2},{4,5},{5,4},{6,7},{7,6},{8,9},{9,8},{10,11... | collective-permute-start | bytes 98312 | tf_op jit(solution)/shard_map/ppermute | solution.py:90
  7.5 0.7 %copy-start.19 = (s32[2,4,1]{1,2,0:T(1,128)S(1)}, s32[2,4,1]{1,2,0:T(1,128)}, u32[]{:S(2)}) copy-start(s32[2,4,1]{1,2,0:T(1,128)} %param.7) | copy-start | bytes 100
  9.3 0.8 %copy-start.5 = (bf16[128,128]{1,0:T(8,128)(2,1)S(1)}, bf16[128,128]{1,0:T(8,128)(2,1)}, u32[]{:S(2)}) copy-start(bf16[128,128]{1,0:T(8,128)(2,1)} %x.1) | copy-start | bytes 98308
  10.0 0.8 %copy-start.6 = (bf16[128,128]{1,0:T(8,128)(2,1)S(1)}, bf16[128,128]{1,0:T(8,128)(2,1)}, u32[]{:S(2)}) copy-start(bf16[128,128]{1,0:T(8,128)(2,1)} %g.1) | copy-start | bytes 98308
  10.8 1.7 %copy-start.21 = (f32[1,128]{1,0:T(1,128)}, f32[1,128]{1,0:T(1,128)S(1)}, u32[]{:S(2)}) copy-start(f32[1,128]{1,0:T(1,128)S(1)} %collective-permute-done.8.b_) | copy-start | bytes 1540
  10.8 2.4 %collective-permute-start.9 = (bf16[128,128]{1,0:T(8,128)(2,1)S(1)}, bf16[128,128]{1,0:T(8,128)(2,1)S(1)}, u32[]{:S(2)}, u32[]{:S(2)}) collective-permute-start(bf16[128,128]{1,0:T(8,128)(2,1)S(1)} %copy-done.6), channel_id=1, source_target_pairs={{0,1},{1,0},{2,3},{3,2},{4,5},{5,4},{6,7},{7,6},{8,9},{9,8},{10,11... | collective-permute-start | bytes 98312 | tf_op jit(solution)/shard_map/ppermute | solution.py:90
  10.9 2.3 %copy-start.10 = (bf16[128,128]{1,0:T(8,128)(2,1)}, bf16[128,128]{1,0:T(8,128)(2,1)S(1)}, u32[]{:S(2)}) copy-start(bf16[128,128]{1,0:T(8,128)(2,1)S(1)} %collective-permute-done.7.w_) | copy-start | bytes 98308
  10.9 6.6 %collective-permute-start = (bf16[5,128,128]{2,1,0:T(8,128)(2,1)S(1)}, bf16[5,128,128]{2,1,0:T(8,128)(2,1)S(1)}, u32[]{:S(2)}, u32[]{:S(2)}) collective-permute-start(bf16[5,128,128]{2,1,0:T(8,128)(2,1)S(1)} %pad_maximum_fusion), channel_id=1, source_target_pairs={{0,2},{1,3},{2,0},{3,1},{4,6},{5,7},{6,4},{7,5},{8,10},{9,11},{10,... | collective-permute-start | bytes 491528 | tf_op jit(solution)/shard_map/ppermute | solution.py:86
  11.9 1.3 %copy-start.7 = (bf16[128,128]{1,0:T(8,128)(2,1)}, bf16[128,128]{1,0:T(8,128)(2,1)S(1)}, u32[]{:S(2)}) copy-start(bf16[128,128]{1,0:T(8,128)(2,1)S(1)} %collective-permute-done.2.x1) | copy-start | bytes 98308
  11.9 1.4 %collective-permute-start.5 = (bf16[128,128]{1,0:T(8,128)(2,1)S(1)}, bf16[128,128]{1,0:T(8,128)(2,1)S(1)}, u32[]{:S(2)}, u32[]{:S(2)}) collective-permute-start(bf16[128,128]{1,0:T(8,128)(2,1)S(1)} %collective-permute-done.2.x1), channel_id=1, source_target_pairs={{0,1},{1,0},{2,3},{3,2},{4,5},{5,4},{6,7},{7,6},{8,9},{9,8},{10,11... | collective-permute-start | bytes 98312 | tf_op jit(solution)/shard_map/ppermute | solution.py:90
  11.9 1.3 %copy-start.8 = (bf16[128,128]{1,0:T(8,128)(2,1)}, bf16[128,128]{1,0:T(8,128)(2,1)S(1)}, u32[]{:S(2)}) copy-start(bf16[128,128]{1,0:T(8,128)(2,1)S(1)} %collective-permute-done.1.x0) | copy-start | bytes 98308
  11.9 1.4 %collective-permute-start.4 = (bf16[128,128]{1,0:T(8,128)(2,1)S(1)}, bf16[128,128]{1,0:T(8,128)(2,1)S(1)}, u32[]{:S(2)}, u32[]{:S(2)}) collective-permute-start(bf16[128,128]{1,0:T(8,128)(2,1)S(1)} %collective-permute-done.1.x0), channel_id=1, source_target_pairs={{0,1},{1,0},{2,3},{3,2},{4,5},{5,4},{6,7},{7,6},{8,9},{9,8},{10,11... | collective-permute-start | bytes 98312 | tf_op jit(solution)/shard_map/ppermute | solution.py:90
  12.4 0.8 %copy-start.9 = (bf16[128,128]{1,0:T(8,128)(2,1)}, bf16[128,128]{1,0:T(8,128)(2,1)S(1)}, u32[]{:S(2)}) copy-start(bf16[128,128]{1,0:T(8,128)(2,1)S(1)} %collective-permute-done.3.x2) | copy-start | bytes 98308
  12.4 1.2 %collective-permute-start.6 = (bf16[128,128]{1,0:T(8,128)(2,1)S(1)}, bf16[128,128]{1,0:T(8,128)(2,1)S(1)}, u32[]{:S(2)}, u32[]{:S(2)}) collective-permute-start(bf16[128,128]{1,0:T(8,128)(2,1)S(1)} %collective-permute-done.3.x2), channel_id=1, source_target_pairs={{0,1},{1,0},{2,3},{3,2},{4,5},{5,4},{6,7},{7,6},{8,9},{9,8},{10,11... | collective-permute-start | bytes 98312 | tf_op jit(solution)/shard_map/ppermute | solution.py:90
  13.2 4.2 %copy-start.11 = (bf16[128,128]{1,0:T(8,128)(2,1)}, bf16[128,128]{1,0:T(8,128)(2,1)S(1)}, u32[]{:S(2)}) copy-start(bf16[128,128]{1,0:T(8,128)(2,1)S(1)} %collective-permute-done.9.g_) | copy-start | bytes 98308
  13.2 4.2 %copy-start.12 = (bf16[128,128]{1,0:T(8,128)(2,1)}, bf16[128,128]{1,0:T(8,128)(2,1)S(1)}, u32[]{:S(2)}) copy-start(bf16[128,128]{1,0:T(8,128)(2,1)S(1)} %collective-permute-done.5.y1) | copy-start | bytes 98308
  13.3 4.2 %copy-start.13 = (bf16[128,128]{1,0:T(8,128)(2,1)}, bf16[128,128]{1,0:T(8,128)(2,1)S(1)}, u32[]{:S(2)}) copy-start(bf16[128,128]{1,0:T(8,128)(2,1)S(1)} %collective-permute-done.4.y0) | copy-start | bytes 98308
  13.6 3.9 %copy-start.14 = (bf16[128,128]{1,0:T(8,128)(2,1)}, bf16[128,128]{1,0:T(8,128)(2,1)S(1)}, u32[]{:S(2)}) copy-start(bf16[128,128]{1,0:T(8,128)(2,1)S(1)} %collective-permute-done.6.y2) | copy-start | bytes 98308
  17.5 0.7 %copy-start = (bf16[5,128,128]{2,1,0:T(8,128)(2,1)}, bf16[5,128,128]{2,1,0:T(8,128)(2,1)S(1)}, u32[]{:S(2)}) copy-start(bf16[5,128,128]{2,1,0:T(8,128)(2,1)S(1)} %collective-permute-done.other) | copy-start | bytes 491524
  20.4 8.6 %collective-permute-start.12 = (bf16[384,128]{1,0:T(8,128)(2,1)}, bf16[384,128]{1,0:T(8,128)(2,1)S(1)}, u32[]{:S(2)}, u32[]{:S(2)}) collective-permute-start(bf16[384,128]{1,0:T(8,128)(2,1)} %get-tuple-element.6.m.refs_0_), channel_id=1, source_target_pairs={{0,6},{1,7},{2,4},{3,5},{4,2},{5,3},{6,0},{7,1},{8,14},{9,15},{10,... | collective-permute-start | bytes 294920 | tf_op jit(solution)/shard_map/ppermute | solution.py:86
  22.4 6.7 %collective-permute-start.11 = (bf16[384,128]{1,0:T(8,128)(2,1)}, bf16[384,128]{1,0:T(8,128)(2,1)S(1)}, u32[]{:S(2)}, u32[]{:S(2)}) collective-permute-start(bf16[384,128]{1,0:T(8,128)(2,1)} %get-tuple-element.6.m.refs_0_), channel_id=1, source_target_pairs={{0,4},{1,5},{2,6},{3,7},{4,0},{5,1},{6,2},{7,3},{8,12},{9,13},{10,... | collective-permute-start | bytes 294920 | tf_op jit(solution)/shard_map/ppermute | solution.py:86
  22.7 6.4 %collective-permute-start.10 = (bf16[384,128]{1,0:T(8,128)(2,1)}, bf16[384,128]{1,0:T(8,128)(2,1)S(1)}, u32[]{:S(2)}, u32[]{:S(2)}) collective-permute-start(bf16[384,128]{1,0:T(8,128)(2,1)} %get-tuple-element.6.m.refs_0_), channel_id=1, source_target_pairs={{0,2},{1,3},{2,0},{3,1},{4,6},{5,7},{6,4},{7,5},{8,10},{9,11},{10,... | collective-permute-start | bytes 294920 | tf_op jit(solution)/shard_map/ppermute | solution.py:86
  24.7 8.8 %collective-permute-start.14 = (bf16[128,128]{1,0:T(8,128)(2,1)S(1)}, bf16[128,128]{1,0:T(8,128)(2,1)S(1)}, u32[]{:S(2)}, u32[]{:S(2)}) collective-permute-start(bf16[128,128]{1,0:T(8,128)(2,1)S(1)} %slice.3), channel_id=1, source_target_pairs={{0,8},{1,13},{2,10},{3,15},{4,12},{5,9},{6,14},{7,11},{8,0},{9,5},... | collective-permute-start | bytes 98312 | tf_op jit(solution)/shard_map/ppermute | solution.py:86
  27.8 6.6 %collective-permute-start.13 = (bf16[128,128]{1,0:T(8,128)(2,1)S(1)}, bf16[128,128]{1,0:T(8,128)(2,1)S(1)}, u32[]{:S(2)}, u32[]{:S(2)}) collective-permute-start(bf16[128,128]{1,0:T(8,128)(2,1)S(1)} %slice.3), channel_id=1, source_target_pairs={{0,14},{1,11},{2,12},{3,9},{4,10},{5,15},{6,8},{7,13},{8,6},{9,3},... | collective-permute-start | bytes 98312 | tf_op jit(solution)/shard_map/ppermute | solution.py:86
  29.1 0.6 %copy-start.1 = (bf16[384,128]{1,0:T(8,128)(2,1)}, bf16[384,128]{1,0:T(8,128)(2,1)S(1)}, u32[]{:S(2)}) copy-start(bf16[384,128]{1,0:T(8,128)(2,1)S(1)} %collective-permute-done.12.m2.refs_3_) | copy-start | bytes 294916
  29.1 0.7 %copy-start.2 = (bf16[384,128]{1,0:T(8,128)(2,1)}, bf16[384,128]{1,0:T(8,128)(2,1)S(1)}, u32[]{:S(2)}) copy-start(bf16[384,128]{1,0:T(8,128)(2,1)S(1)} %collective-permute-done.11.m1.refs_2_) | copy-start | bytes 294916
  29.7 0.6 %copy-start.3 = (bf16[384,128]{1,0:T(8,128)(2,1)}, bf16[384,128]{1,0:T(8,128)(2,1)S(1)}, u32[]{:S(2)}) copy-start(bf16[384,128]{1,0:T(8,128)(2,1)S(1)} %collective-permute-done.10.m0.refs_1_) | copy-start | bytes 294916
  32.1 6.2 %copy-start.4 = (f32[128,128]{1,0:T(8,128)S(1)}, f32[128,128]{1,0:T(8,128)}, u32[]{:S(2)}) copy-start(f32[128,128]{1,0:T(8,128)} %shard_map.87) | copy-start | bytes 196612
  32.1 6.2 %collective-permute-start.17 = (f32[128,128]{1,0:T(8,128)}, f32[128,128]{1,0:T(8,128)S(1)}, u32[]{:S(2)}, u32[]{:S(2)}) collective-permute-start(f32[128,128]{1,0:T(8,128)} %shard_map.87), channel_id=1, source_target_pairs={{0,8},{1,9},{2,10},{3,11},{4,12},{5,13},{6,14},{7,15},{8,0},{9,1},... | collective-permute-start | bytes 196616 | tf_op jit(solution)/shard_map/ppermute | solution.py:86
  33.5 2.1 %copy-start.15 = (bf16[128,128]{1,0:T(8,128)(2,1)}, bf16[128,128]{1,0:T(8,128)(2,1)S(1)}, u32[]{:S(2)}) copy-start(bf16[128,128]{1,0:T(8,128)(2,1)S(1)} %collective-permute-done.14.v1) | copy-start | bytes 98308
  33.5 1.2 %collective-permute-start.16 = (bf16[128,128]{1,0:T(8,128)(2,1)S(1)}, bf16[128,128]{1,0:T(8,128)(2,1)S(1)}, u32[]{:S(2)}, u32[]{:S(2)}) collective-permute-start(bf16[128,128]{1,0:T(8,128)(2,1)S(1)} %collective-permute-done.14.v1), channel_id=1, source_target_pairs={{0,1},{1,0},{2,3},{3,2},{4,5},{5,4},{6,7},{7,6},{8,9},{9,8},{10,11... | collective-permute-start | bytes 98312 | tf_op jit(solution)/shard_map/ppermute | solution.py:90
  34.4 1.2 %copy-start.16 = (bf16[128,128]{1,0:T(8,128)(2,1)}, bf16[128,128]{1,0:T(8,128)(2,1)S(1)}, u32[]{:S(2)}) copy-start(bf16[128,128]{1,0:T(8,128)(2,1)S(1)} %collective-permute-done.13.v0) | copy-start | bytes 98308
  34.4 1.2 %collective-permute-start.15 = (bf16[128,128]{1,0:T(8,128)(2,1)S(1)}, bf16[128,128]{1,0:T(8,128)(2,1)S(1)}, u32[]{:S(2)}, u32[]{:S(2)}) collective-permute-start(bf16[128,128]{1,0:T(8,128)(2,1)S(1)} %collective-permute-done.13.v0), channel_id=1, source_target_pairs={{0,1},{1,0},{2,3},{3,2},{4,5},{5,4},{6,7},{7,6},{8,9},{9,8},{10,11... | collective-permute-start | bytes 98312 | tf_op jit(solution)/shard_map/ppermute | solution.py:90
  34.7 0.9 %copy-start.17 = (bf16[128,128]{1,0:T(8,128)(2,1)}, bf16[128,128]{1,0:T(8,128)(2,1)S(1)}, u32[]{:S(2)}) copy-start(bf16[128,128]{1,0:T(8,128)(2,1)S(1)} %collective-permute-done.16.u1) | copy-start | bytes 98308
  35.6 0.6 %copy-start.18 = (bf16[128,128]{1,0:T(8,128)(2,1)}, bf16[128,128]{1,0:T(8,128)(2,1)S(1)}, u32[]{:S(2)}) copy-start(bf16[128,128]{1,0:T(8,128)(2,1)S(1)} %collective-permute-done.15.u0) | copy-start | bytes 98308

commit v2 on v1

v2 whole, which is shorter than its diff:
```python
import math

import jax
import jax.numpy as jnp
from jax import lax
from jax.experimental import pallas as pl
from jax.experimental.pallas import tpu as pltpu
from jax.sharding import PartitionSpec as P

CHIPS = ("dom", "rep")
CORES = ("dom", "rep", "sub")
F32 = jnp.float32
BF16 = jnp.bfloat16


def forward_and_gp(operator, features, weight, bias, cotangent):
    z = jnp.dot(operator, features, preferred_element_type=F32)
    high = z.astype(BF16)
    low = (z - high.astype(F32)).astype(BF16)
    both = jnp.concatenate([high, low], axis=1)
    pre = jnp.dot(both, jnp.concatenate([weight, weight], axis=0), preferred_element_type=F32) + bias
    sigma = jax.nn.sigmoid(pre)
    activation = (pre * sigma).astype(BF16)
    grad_pre = (cotangent.astype(F32) * sigma * (1.0 + pre * (1.0 - sigma))).astype(BF16)
    back = lax.dot_general(
        grad_pre, weight, (((1,), (1,)), ((), ())), preferred_element_type=F32
    ).astype(BF16)
    return high, low, activation, grad_pre, back


def weight_term(high, low, grads):
    return lax.dot_general(
        jnp.concatenate([high, low], axis=0),
        jnp.concatenate([grads, grads], axis=0),
        (((0,), (0,)), ((), ())),
        preferred_element_type=F32,
    )


def masked_rows(adjacency, mask, start, count):
    _, sections, width = adjacency.shape
    extent = adjacency.shape[0] // mask.shape[0]
    rows = lax.dynamic_slice_in_dim(adjacency, start, count, axis=0)
    tall = max(1, count // extent)
    flags = lax.dynamic_slice_in_dim(mask, start // extent, tall, axis=0).astype(BF16)
    flags = jnp.broadcast_to(
        flags[:, None, :, :, None],
        (tall, count // tall, sections, mask.shape[2], width // mask.shape[2]),
    ).reshape(count, sections, width)
    return (rows * flags).transpose(1, 0, 2)


def general(mesh, adjacency, mask, features, weight, bias, cotangent):
    reps = mesh.shape["rep"]
    nodes, width = features.shape[0], adjacency.shape[2]
    sections = adjacency.shape[1]
    pieces = jnp.stack([masked_rows(adjacency, mask, q * nodes, nodes) for q in range(reps)])
    pieces = lax.all_to_all(pieces, "rep", 0, 0, tiled=True)
    operator = pieces.transpose(2, 1, 0, 3).reshape(nodes, sections * reps * width)
    everyone = lax.all_gather(features, CHIPS, axis=0, tiled=True)
    whole_weight = lax.all_gather(weight, "sub", axis=1, tiled=True)
    whole_bias = lax.all_gather(bias, "sub", axis=0, tiled=True)
    whole_cotangent = lax.all_gather(cotangent, "sub", axis=1, tiled=True)
    high, low, activation, grad_pre, back = forward_and_gp(
        operator, everyone, whole_weight, whole_bias[None, :], whole_cotangent
    )
    half = weight.shape[1]
    mine = lax.axis_index("sub") * half
    activation = lax.dynamic_slice_in_dim(activation, mine, half, axis=1)
    grads = lax.dynamic_slice_in_dim(grad_pre, mine, half, axis=1)
    total = lax.psum(weight_term(high, low, grads), CHIPS)
    backs = lax.all_gather(back, CHIPS, axis=0, tiled=True)
    grad_input = jnp.dot(operator, backs, preferred_element_type=F32).astype(BF16)
    return activation, grad_input, total / math.sqrt(sections * reps * width)


SHARED = (((3, 1), (2, 1)), ((2, 0), (3, 0)), ((1, 0), (1, 1)))
ACROSS = ((3, 0), (2, 0), (1, 0))


def fetch(value, first, second=None):
    pairs = []
    for d in range(4):
        for r in range(2):
            for c, off in enumerate((first, first if second is None else second)):
                source = (d * 2 + r) * 2 + c
                pairs.append((source, ((d ^ off[0]) * 2 + (r ^ off[1])) * 2 + c))
    return lax.ppermute(value, CORES, pairs)


def swap(value):
    return lax.ppermute(value, "sub", [(0, 1), (1, 0)])


def vmem(*shape, dtype=BF16):
    return pltpu.VMEM(shape, dtype)


def vmem_call(body, outs, *operands):
    held = [pltpu.with_memory_space_constraint(x, pltpu.VMEM) for x in operands]
    return pl.pallas_call(
        body,
        out_shape=outs,
        in_specs=[pl.BlockSpec(memory_space=pltpu.VMEM)] * len(operands),
        out_specs=[pl.BlockSpec(memory_space=pltpu.VMEM)] * len(outs),
    )(*held)


def load_kernel(count, *refs):
    sources, targets, sems = refs[:count], refs[count : 2 * count], refs[-1]
    copies = [
        pltpu.make_async_copy(source, target, sems.at[i])
        for i, (source, target) in enumerate(zip(sources, targets))
    ]
    for copy in copies:
        copy.start()
    for copy in copies:
        copy.wait()


def load(*arrays):
    return pl.pallas_call(
        lambda *refs: load_kernel(len(arrays), *refs),
        out_shape=[pltpu.VMEM(x.shape, x.dtype) for x in arrays],
        in_specs=[pl.BlockSpec(memory_space=pl.ANY)] * len(arrays),
        out_specs=[pl.BlockSpec(memory_space=pltpu.VMEM)] * len(arrays),
        scratch_shapes=[pltpu.SemaphoreType.DMA((len(arrays),))],
    )(*arrays)


def in_order(first, second):
    zero = lax.axis_index("sub") == 0
    return jnp.where(zero, first, second), jnp.where(zero, second, first)


def forward_kernel(own, p, q, x, x0, x1, x2, y0, y1, y2, w, w_, b, b_, g, g_, act, back, msg, mine, rows, xs):
    n = x.shape[0]
    sections = own.shape[0]
    d, r, c = (lax.axis_index(a) for a in CORES)

    def columns(s, rep):
        return pl.ds(pl.multiple_of((s * 2 + rep) * n, n), n)

    first, second = in_order(p[...], q[...])
    for s in range(sections):
        rows[:, columns(s, r)] = own[s]
        rows[:n, columns(s, 1 - r)] = first[s * n : (s + 1) * n]
        rows[n:, columns(s, 1 - r)] = second[s * n : (s + 1) * n]
    low, high = (sections + 1) * n, (sections + 1) * n + n // 2
    xs[columns(d, r), :] = x[...]
    xs[columns(d, 1 - r), :] = jnp.concatenate([first[low:high], second[low:high]], axis=0)
    for pair, direct, swapped in zip(SHARED, (x0, x1, x2), (y0, y1, y2)):
        for (dx, rx), value in zip(pair, in_order(direct[...], swapped[...])):
            xs[columns(d ^ dx, r ^ rx), :] = value
    mine[...] = rows[pl.ds(pl.multiple_of(r * n, n), n), :]

    weight = jnp.concatenate(in_order(w[...], w_[...]), axis=1)
    bias = jnp.concatenate(in_order(b[...], b_[...]), axis=1)
    here = jnp.concatenate(in_order(g[...], g_[...]), axis=1)
    there = jnp.concatenate([first[sections * n : low], second[sections * n : low]], axis=1)
    zero = r == 0
    cotangent = jnp.concatenate(
        [jnp.where(zero, here, there), jnp.where(zero, there, here)], axis=0
    )
    high, low, activation, grad_pre, v = forward_and_gp(
        rows[...], xs[...], weight, bias, cotangent
    )
    half = w.shape[1]
    zero = c == 0
    activation = jnp.where(r == 0, activation[:n], activation[n:])
    act[...] = jnp.where(zero, activation[:, :half], activation[:, half:])
    grads = jnp.where(zero, grad_pre[:, :half], grad_pre[:, half:])
    back[...] = v
    msg[:n] = jnp.where(zero, v[:n], v[n:])
    msg[n:] = weight_term(high, low, grads).astype(BF16)


def backward_kernel(scale, rows, back, msg, m0, m1, m2, s0, s1, s2, a, gi, gw, act, vs):
    n = rows.shape[0]
    d = lax.axis_index("dom")
    act[...] = a[...]
    terms = {(0, 0): msg[n:].astype(F32)}
    vs[pl.ds(pl.multiple_of(d * 2 * n, n), 2 * n), :] = back[...]
    for off, direct, swapped in zip(ACROSS, (m0, m1, m2), (s0, s1, s2)):
        terms[off] = direct[n:].astype(F32)
        both = jnp.concatenate(in_order(direct[:n], swapped[:n]), axis=0)
        vs[pl.ds(pl.multiple_of((d ^ off[0]) * 2 * n, n), 2 * n), :] = both
    gw[...] = ((terms[0, 0] + terms[1, 0]) + (terms[2, 0] + terms[3, 0])) * scale
    gi[...] = jnp.dot(rows[...], vs[...], preferred_element_type=F32).astype(BF16)


def direct(mesh, adjacency, mask, features, weight, bias, cotangent):
    nodes, feat = features.shape
    sections, width = adjacency.shape[1:]
    total = sections * 2 * width
    half = weight.shape[1]
    c = lax.axis_index("sub")
    few = nodes // 2

    far = fetch(features, *SHARED[0])
    adj, held, grads, flags = load(adjacency, features, cotangent, mask.transpose(0, 2, 1))
    operator = masked_rows(adj, flags.transpose(0, 2, 1), 0, 2 * nodes)
    give = lax.dynamic_slice_in_dim(operator, c * nodes, nodes, axis=1).reshape(sections * nodes, width)
    give = jnp.concatenate([give, grads, lax.dynamic_slice_in_dim(held, c * few, few)], axis=0)
    taken = fetch(give, (0, 1))
    xs = [far] + [fetch(features, *pair) for pair in SHARED[1:]]
    row = bias[None, :]
    w_, b_, g_ = swap(weight), swap(row), swap(cotangent)
    ys = [swap(x) for x in xs]
    act, back, msg, mine = pl.pallas_call(
        forward_kernel,
        out_shape=[vmem(nodes, half), vmem(2 * nodes, feat), vmem(nodes + feat, half), vmem(nodes, total)],
        in_specs=[pl.BlockSpec(memory_space=pltpu.VMEM)] * 16,
        out_specs=[pl.BlockSpec(memory_space=pltpu.VMEM)] * 4,
        scratch_shapes=[vmem(2 * nodes, total), vmem(total, feat)],
    )(
        *(
            pltpu.with_memory_space_constraint(x, pltpu.VMEM)
            for x in (operator, taken, swap(taken), held, *xs, *ys, weight, w_, row, b_, grads, g_)
        )
    )
    ms = [fetch(msg, off) for off in ACROSS]
    ss = [swap(m) for m in ms]
    scale = 1.0 / math.sqrt(total)
    grad_input, grad_weight, activation = pl.pallas_call(
        lambda *refs: backward_kernel(scale, *refs),
        out_shape=[
            jax.ShapeDtypeStruct((nodes, feat), BF16),
            jax.ShapeDtypeStruct((feat, half), F32),
            jax.ShapeDtypeStruct((nodes, half), BF16),
        ],
        in_specs=[pl.BlockSpec(memory_space=pltpu.VMEM)] * 10,
        out_specs=[pl.BlockSpec(memory_space=pltpu.VMEM)] * 3,
        scratch_shapes=[vmem(total, feat)],
    )(
        *(
            pltpu.with_memory_space_constraint(x, pltpu.VMEM)
            for x in (mine, back, msg, *ms, *ss, act)
        )
    )
    return activation, grad_input, grad_weight


def solution(mesh):
    small = dict(mesh.shape) == {"groups": mesh.shape["groups"], "dom": 4, "rep": 2, "sub": 2}
    body = direct if small else general
    return jax.shard_map(
        lambda *arrays: body(mesh, *arrays),
        mesh=mesh,
        in_specs=(
            P(("groups", "dom"), None, "rep"),
            P(("groups", "dom"), None, "rep"),
            P(("groups", "dom", "rep"), None),
            P(None, "sub"),
            P("sub"),
            P(("groups", "dom", "rep"), "sub"),
        ),
        out_specs=(
            P(("groups", "dom", "rep"), "sub"),
            P(("groups", "dom", "rep"), None),
            P("groups", "sub"),
        ),
        check_vma=False,
    )
```

time: 39.3 us -> 29 us (0.74)
  local copies, waits for them, and re-layouts: 6.52 us -> 0.24 us
  waiting for transfers between devices: 6.26 us -> 10.9 us
  starting transfers between devices: 17.8 us -> 13.8 us
  Pallas kernels: 6.03 us -> 2.7 us
  other arithmetic: 1.47 us -> 0.42 us
    ppermute x10 -> x7, starting transfers between devices: 16.6 us -> 11.9 us  [fetch(): return lax.ppermute(value, CORES, pairs)]
    unnamed x44 -> x10, local copies, waits for them, and re-layouts: 4.67 us -> 0.11 us
    ppermute x10 -> x7, waiting for transfers between devices: 4.73 us -> 8.79 us  [fetch(): return lax.ppermute(value, CORES, pairs)]
    pallas_call x3, Pallas kernels: 6.03 us -> 2.7 us  [the longest x1 0.99 us: load(): pl.pallas_call(lambda *refs: load_kernel(len(arrays), *refs), out_shape=[...]
    dynamic_slice x1, local copies, waits for them, and re-layouts: 1.06 us -> 0.01 us  [direct(): lax.dynamic_slice_in_dim(held, c * few, few)]
    ppermute x8 -> x10, starting transfers between devices: 1.16 us -> 1.98 us  [swap(): return lax.ppermute(value, 'sub', [(0, 1), (1, 0)])]
    slice x1 -> x0, local copies, waits for them, and re-layouts: 0.79 us -> none  [direct(): back = msg[:nodes]]
    div x1 -> x0, other arithmetic: 0.64 us -> none  [direct(): total = (plane + across) / math.sqrt(sections * 2 * width)]
  transfers between devices with their start and end apart: 18 -> 17, of which waited for: 5 -> 8; matrix products, arithmetic and copies ran while one was open for 7% -> 1% of each run, Pallas kernels for 10% -> 0%
where the time goes in v2:
time: 29 us; the launch traced here: 28.8 us
  starting transfers between devices  13.8 us (48%)
  waiting for transfers between devices  10.9 us (38%)
  Pallas kernels  2.7 us (9%)
  between operations  0.76 us (3%)
  other arithmetic  0.42 us (1%)
    ppermute x7, starting transfers between devices, fetch(): return lax.ppermute(value, CORES, pairs)  11.9 us
    ppermute x7, waiting for transfers between devices, fetch(): return lax.ppermute(value, CORES, pairs)  8.79 us
    ppermute x10, waiting for transfers between devices, swap(): return lax.ppermute(value, 'sub', [(0, 1), (1, 0)])  2.09 us
    ppermute x10, starting transfers between devices, swap(): return lax.ppermute(value, 'sub', [(0, 1), (1, 0)])  1.98 us
    pallas_call x1, Pallas kernels, load(): pl.pallas_call(lambda *refs: load_kernel(len(arrays), *refs), out_shape=[...  0.99 us
    pallas_call x1, Pallas kernels, direct(): pl.pallas_call(lambda *refs: backward_kernel(scale, *refs), out_shape=[ja...  0.89 us
    pallas_call x1, Pallas kernels, direct(): pl.pallas_call(forward_kernel, out_shape=[vmem(nodes, half), vmem(2 * nod...  0.81 us
  transfers between devices with their start and end apart: 17, of which 8 were waited for; matrix products, arithmetic and copies ran while one was open for 1% of the time, Pallas kernels for 0%

profile of v2, /device:TPU:0, one launch (start us, length us, event | category | flops | bytes accessed | tf_op | source)
XLA Modules:
  0.0 28.8 jit_solution(16579883288766753748)
XLA Ops:
  0.6 1.0 %shard_map.85 = (bf16[256,4,128]{2,1,0:T(4,128)(2,1)S(1)}, bf16[128,128]{1,0:T(8,128)(2,1)S(1)}, bf16[128,128]{1,0:T(8,128)(2,1)S(1)}, s32[2,1,4]{2,1,0:T(1,128)S(1)}) custom-call(bf16[256,4,128]{2,1,0:T(4,128)(2,1)} %refs_0_.1, bf16[128,128]{1,0:T(8,128)(2,1)} %refs_1_.1, bf16[128,128]{1,0:T(8,128)(2,1)} %refs_2_.1, s32[2,1,4]{2,1,0:T(1,128)} %bitcast.23), custom_call_target="tpu_custom_call" | custom-call | tf_op jit(solution)/shard_map/pallas_call | solution.py:122
  1.6 0.1 copy.15
  1.8 0.1 broadcast_bitcast_fusion
  1.8 0.2 copy_multiply_fusion
  2.1 0.0 copy-start
  2.1 0.0 copy-start.2
  2.1 0.0 copy-start.3
  2.1 0.0 copy-start.1
  2.1 3.0 %collective-permute-start = (bf16[704,128]{1,0:T(8,128)(2,1)S(1)}, bf16[704,128]{1,0:T(8,128)(2,1)S(1)}, u32[]{:S(2)}, u32[]{:S(2)}) collective-permute-start(bf16[704,128]{1,0:T(8,128)(2,1)S(1)} %pad_maximum_fusion), channel_id=1, source_target_pairs={{0,2},{1,3},{2,0},{3,1},{4,6},{5,7},{6,4},{7,5},{8,10},{9,11},{10,... | collective-permute-start | bytes 540680 | tf_op jit(solution)/shard_map/ppermute | solution.py:88
  5.1 0.0 copy-done.1
  5.2 0.0 collective-permute-start.9
  5.2 0.0 copy-done
  5.2 0.5 %collective-permute-start.8 = (bf16[128,128]{1,0:T(8,128)(2,1)S(1)}, bf16[128,128]{1,0:T(8,128)(2,1)S(1)}, u32[]{:S(2)}, u32[]{:S(2)}) collective-permute-start(bf16[128,128]{1,0:T(8,128)(2,1)S(1)} %copy-done), channel_id=1, source_target_pairs={{0,1},{1,0},{2,3},{3,2},{4,5},{5,4},{6,7},{7,6},{8,9},{9,8},{10,11... | collective-permute-start | bytes 98312 | tf_op jit(solution)/shard_map/ppermute | solution.py:92
  5.7 0.0 copy-done.2
  5.7 3.6 %collective-permute-start.2 = (bf16[128,128]{1,0:T(8,128)(2,1)S(1)}, bf16[128,128]{1,0:T(8,128)(2,1)S(1)}, u32[]{:S(2)}, u32[]{:S(2)}) collective-permute-start(bf16[128,128]{1,0:T(8,128)(2,1)S(1)} %copy-done.2), channel_id=1, source_target_pairs={{0,14},{1,11},{2,12},{3,9},{4,10},{5,15},{6,8},{7,13},{8,6},{9,3},... | collective-permute-start | bytes 98312 | tf_op jit(solution)/shard_map/ppermute | solution.py:88
  9.3 0.0 collective-permute-start.4
  9.3 0.0 collective-permute-done.9.b_
  9.3 0.8 %collective-permute-start.3 = (bf16[128,128]{1,0:T(8,128)(2,1)S(1)}, bf16[128,128]{1,0:T(8,128)(2,1)S(1)}, u32[]{:S(2)}, u32[]{:S(2)}) collective-permute-start(bf16[128,128]{1,0:T(8,128)(2,1)S(1)} %copy-done.2), channel_id=1, source_target_pairs={{0,8},{1,13},{2,10},{3,15},{4,12},{5,9},{6,14},{7,11},{8,0},{9,5},... | collective-permute-start | bytes 98312 | tf_op jit(solution)/shard_map/ppermute | solution.py:88
  10.1 0.0 collective-permute-done.8.w_
  10.1 0.0 copy-done.3
  10.1 0.2 collective-permute-start.10
  10.3 1.9 %collective-permute-done.2.x0 = bf16[128,128]{1,0:T(8,128)(2,1)S(1)} collective-permute-done((bf16[128,128]{1,0:T(8,128)(2,1)S(1)}, bf16[128,128]{1,0:T(8,128)(2,1)S(1)}, u32[]{:S(2)}, u32[]{:S(2)}) %collective-permute-start.2) | collective-permute-done | bytes 32800 | tf_op jit(solution)/shard_map/ppermute | solution.py:88
  12.3 0.0 collective-permute-start.5
  12.3 0.9 %collective-permute-done.4.x2 = bf16[128,128]{1,0:T(8,128)(2,1)S(1)} collective-permute-done((bf16[128,128]{1,0:T(8,128)(2,1)S(1)}, bf16[128,128]{1,0:T(8,128)(2,1)S(1)}, u32[]{:S(2)}, u32[]{:S(2)}) %collective-permute-start.4) | collective-permute-done | bytes 32800 | tf_op jit(solution)/shard_map/ppermute | solution.py:88
  13.2 0.0 collective-permute-start.7
  13.2 0.9 %collective-permute-done.3.x1 = bf16[128,128]{1,0:T(8,128)(2,1)S(1)} collective-permute-done((bf16[128,128]{1,0:T(8,128)(2,1)S(1)}, bf16[128,128]{1,0:T(8,128)(2,1)S(1)}, u32[]{:S(2)}, u32[]{:S(2)}) %collective-permute-start.3) | collective-permute-done | bytes 32800 | tf_op jit(solution)/shard_map/ppermute | solution.py:88
  14.1 0.7 %collective-permute-start.6 = (bf16[128,128]{1,0:T(8,128)(2,1)S(1)}, bf16[128,128]{1,0:T(8,128)(2,1)S(1)}, u32[]{:S(2)}, u32[]{:S(2)}) collective-permute-start(bf16[128,128]{1,0:T(8,128)(2,1)S(1)} %collective-permute-done.3.x1), channel_id=1, source_target_pairs={{0,1},{1,0},{2,3},{3,2},{4,5},{5,4},{6,7},{7,6},{8,9},{9,8},{10,11... | collective-permute-start | bytes 98312 | tf_op jit(solution)/shard_map/ppermute | solution.py:92
  14.8 0.0 collective-permute-done.p
  14.8 0.0 collective-permute-start.1
  14.8 0.2 fusion.own
  15.0 0.0 collective-permute-done.10.g_
  15.0 0.0 collective-permute-done.5.y0
  15.0 0.0 collective-permute-done.7.y2
  15.1 0.6 %collective-permute-done.6.y1 = bf16[128,128]{1,0:T(8,128)(2,1)S(1)} collective-permute-done((bf16[128,128]{1,0:T(8,128)(2,1)S(1)}, bf16[128,128]{1,0:T(8,128)(2,1)S(1)}, u32[]{:S(2)}, u32[]{:S(2)}) %collective-permute-start.6) | collective-permute-done | bytes 32800 | tf_op jit(solution)/shard_map/ppermute | solution.py:92
  15.7 0.6 %collective-permute-done.1.q = bf16[704,128]{1,0:T(8,128)(2,1)S(1)} collective-permute-done((bf16[704,128]{1,0:T(8,128)(2,1)S(1)}, bf16[704,128]{1,0:T(8,128)(2,1)S(1)}, u32[]{:S(2)}, u32[]{:S(2)}) %collective-permute-start.1) | collective-permute-done | bytes 180256 | tf_op jit(solution)/shard_map/ppermute | solution.py:92
  16.2 0.8 %shard_map.86 = (bf16[128,128]{1,0:T(8,128)(2,1)S(1)}, bf16[256,128]{1,0:T(8,128)(2,1)S(1)}, bf16[256,128]{1,0:T(8,128)(2,1)S(1)}, bf16[128,1024]{1,0:T(8,128)(2,1)S(1)}) custom-call(bf16[4,256,128]{2,1,0:T(8,128)(2,1)S(1)} %fusion.own, bf16[704,128]{1,0:T(8,128)(2,1)S(1)} %collective-permute-done.p, bf16[704,128]{1,0:T(8,128)(2,1)S(1)} %collective-permute-done.1.q, ...), custom_call_target="tpu_custom_call" | custom-call | tf_op jit(solution)/shard_map/pallas_call | solution.py:210
  17.1 1.5 %collective-permute-start.13 = (bf16[256,128]{1,0:T(8,128)(2,1)S(1)}, bf16[256,128]{1,0:T(8,128)(2,1)S(1)}, u32[]{:S(2)}, u32[]{:S(2)}) collective-permute-start(bf16[256,128]{1,0:T(8,128)(2,1)S(1)} %get-tuple-element.20.refs_2_), channel_id=1, source_target_pairs={{0,4},{1,5},{2,6},{3,7},{4,0},{5,1},{6,2},{7,3},{8,12},{9,13},{10,... | collective-permute-start | bytes 196616 | tf_op jit(solution)/shard_map/ppermute | solution.py:88
  18.6 0.9 %collective-permute-start.12 = (bf16[256,128]{1,0:T(8,128)(2,1)S(1)}, bf16[256,128]{1,0:T(8,128)(2,1)S(1)}, u32[]{:S(2)}, u32[]{:S(2)}) collective-permute-start(bf16[256,128]{1,0:T(8,128)(2,1)S(1)} %get-tuple-element.20.refs_2_), channel_id=1, source_target_pairs={{0,8},{1,9},{2,10},{3,11},{4,12},{5,13},{6,14},{7,15},{8,0},{9,1},... | collective-permute-start | bytes 196616 | tf_op jit(solution)/shard_map/ppermute | solution.py:88
  19.5 2.0 %collective-permute-start.11 = (bf16[256,128]{1,0:T(8,128)(2,1)S(1)}, bf16[256,128]{1,0:T(8,128)(2,1)S(1)}, u32[]{:S(2)}, u32[]{:S(2)}) collective-permute-start(bf16[256,128]{1,0:T(8,128)(2,1)S(1)} %get-tuple-element.20.refs_2_), channel_id=1, source_target_pairs={{0,12},{1,13},{2,14},{3,15},{4,8},{5,9},{6,10},{7,11},{8,4},{9,5},... | collective-permute-start | bytes 196616 | tf_op jit(solution)/shard_map/ppermute | solution.py:88
  21.5 0.0 collective-permute-done.13.refs_5_
  21.5 0.0 collective-permute-start.16
  21.5 5.0 %collective-permute-done.12.refs_4_ = bf16[256,128]{1,0:T(8,128)(2,1)S(1)} collective-permute-done((bf16[256,128]{1,0:T(8,128)(2,1)S(1)}, bf16[256,128]{1,0:T(8,128)(2,1)S(1)}, u32[]{:S(2)}, u32[]{:S(2)}) %collective-permute-start.12) | collective-permute-done | bytes 65568 | tf_op jit(solution)/shard_map/ppermute | solution.py:88
  26.5 0.0 collective-permute-start.15
  26.5 0.0 collective-permute-done.11.refs_3_
  26.5 0.5 %collective-permute-start.14 = (bf16[256,128]{1,0:T(8,128)(2,1)S(1)}, bf16[256,128]{1,0:T(8,128)(2,1)S(1)}, u32[]{:S(2)}, u32[]{:S(2)}) collective-permute-start(bf16[256,128]{1,0:T(8,128)(2,1)S(1)} %collective-permute-done.11.refs_3_), channel_id=1, source_target_pairs={{0,1},{1,0},{2,3},{3,2},{4,5},{5,4},{6,7},{7,6},{8,9},{9,8},{10,11... | collective-permute-start | bytes 196616 | tf_op jit(solution)/shard_map/ppermute | solution.py:92
  27.0 0.0 collective-permute-done.16.refs_8_
  27.1 0.7 %collective-permute-done.15.refs_7_ = bf16[256,128]{1,0:T(8,128)(2,1)S(1)} collective-permute-done((bf16[256,128]{1,0:T(8,128)(2,1)S(1)}, bf16[256,128]{1,0:T(8,128)(2,1)S(1)}, u32[]{:S(2)}, u32[]{:S(2)}) %collective-permute-start.15) | collective-permute-done | bytes 65568 | tf_op jit(solution)/shard_map/ppermute | solution.py:92
  27.8 0.2 collective-permute-done.14.refs_6_
  28.0 0.9 %shard_map.87 = (bf16[128,128]{1,0:T(8,128)(2,1)}, f32[128,128]{1,0:T(8,128)}, bf16[128,128]{1,0:T(8,128)(2,1)}) custom-call(bf16[128,1024]{1,0:T(8,128)(2,1)S(1)} %get-tuple-element.18.refs_0_, bf16[256,128]{1,0:T(8,128)(2,1)S(1)} %get-tuple-element.19.refs_1_, bf16[256,128]{1,0:T(8,128)(2,1)S(1)} %get-tuple-element.20.refs_2_, ...), custom_call_target="tpu_custom_call" | custom-call | tf_op jit(solution)/shard_map/pallas_call | solution.py:225
  (5 shorter events, 0.0 us)
Async XLA Ops:
  2.1 3.1 %copy-start = (bf16[128,128]{1,0:T(8,128)(2,1)S(1)}, bf16[128,128]{1,0:T(8,128)(2,1)}, u32[]{:S(2)}) copy-start(bf16[128,128]{1,0:T(8,128)(2,1)} %w.1) | copy-start | bytes 98308
  2.1 3.6 %copy-start.2 = (bf16[128,128]{1,0:T(8,128)(2,1)S(1)}, bf16[128,128]{1,0:T(8,128)(2,1)}, u32[]{:S(2)}) copy-start(bf16[128,128]{1,0:T(8,128)(2,1)} %refs_1_.1) | copy-start | bytes 98308
  2.1 8.0 %copy-start.3 = (bf16[128,128]{1,0:T(8,128)(2,1)S(1)}, bf16[128,128]{1,0:T(8,128)(2,1)}, u32[]{:S(2)}) copy-start(bf16[128,128]{1,0:T(8,128)(2,1)} %refs_2_.1) | copy-start | bytes 98308
  2.1 3.0 %copy-start.1 = (f32[128]{0:T(128)S(1)}, f32[128]{0:T(128)}, u32[]{:S(2)}) copy-start(f32[128]{0:T(128)} %param.10) | copy-start | bytes 1540
  2.1 12.7 %collective-permute-start = (bf16[704,128]{1,0:T(8,128)(2,1)S(1)}, bf16[704,128]{1,0:T(8,128)(2,1)S(1)}, u32[]{:S(2)}, u32[]{:S(2)}) collective-permute-start(bf16[704,128]{1,0:T(8,128)(2,1)S(1)} %pad_maximum_fusion), channel_id=1, source_target_pairs={{0,2},{1,3},{2,0},{3,1},{4,6},{5,7},{6,4},{7,5},{8,10},{9,11},{10,... | collective-permute-start | bytes 540680 | tf_op jit(solution)/shard_map/ppermute | solution.py:88
  5.2 4.1 %collective-permute-start.9 = (f32[1,128]{1,0:T(1,128)S(1)}, f32[1,128]{1,0:T(1,128)S(1)}, u32[]{:S(2)}, u32[]{:S(2)}) collective-permute-start(f32[1,128]{1,0:T(1,128)S(1)} %bitcast.17), channel_id=1, source_target_pairs={{0,1},{1,0},{2,3},{3,2},{4,5},{5,4},{6,7},{7,6},{8,9},{9,8},{10,11... | collective-permute-start | bytes 1544 | tf_op jit(solution)/shard_map/ppermute | solution.py:92
  5.2 4.9 %collective-permute-start.8 = (bf16[128,128]{1,0:T(8,128)(2,1)S(1)}, bf16[128,128]{1,0:T(8,128)(2,1)S(1)}, u32[]{:S(2)}, u32[]{:S(2)}) collective-permute-start(bf16[128,128]{1,0:T(8,128)(2,1)S(1)} %copy-done), channel_id=1, source_target_pairs={{0,1},{1,0},{2,3},{3,2},{4,5},{5,4},{6,7},{7,6},{8,9},{9,8},{10,11... | collective-permute-start | bytes 98312 | tf_op jit(solution)/shard_map/ppermute | solution.py:92
  5.7 6.6 %collective-permute-start.2 = (bf16[128,128]{1,0:T(8,128)(2,1)S(1)}, bf16[128,128]{1,0:T(8,128)(2,1)S(1)}, u32[]{:S(2)}, u32[]{:S(2)}) collective-permute-start(bf16[128,128]{1,0:T(8,128)(2,1)S(1)} %copy-done.2), channel_id=1, source_target_pairs={{0,14},{1,11},{2,12},{3,9},{4,10},{5,15},{6,8},{7,13},{8,6},{9,3},... | collective-permute-start | bytes 98312 | tf_op jit(solution)/shard_map/ppermute | solution.py:88
  9.3 3.9 %collective-permute-start.4 = (bf16[128,128]{1,0:T(8,128)(2,1)S(1)}, bf16[128,128]{1,0:T(8,128)(2,1)S(1)}, u32[]{:S(2)}, u32[]{:S(2)}) collective-permute-start(bf16[128,128]{1,0:T(8,128)(2,1)S(1)} %copy-done.2), channel_id=1, source_target_pairs={{0,4},{1,7},{2,6},{3,5},{4,0},{5,3},{6,2},{7,1},{8,12},{9,15},{10,... | collective-permute-start | bytes 98312 | tf_op jit(solution)/shard_map/ppermute | solution.py:88
  9.3 4.8 %collective-permute-start.3 = (bf16[128,128]{1,0:T(8,128)(2,1)S(1)}, bf16[128,128]{1,0:T(8,128)(2,1)S(1)}, u32[]{:S(2)}, u32[]{:S(2)}) collective-permute-start(bf16[128,128]{1,0:T(8,128)(2,1)S(1)} %copy-done.2), channel_id=1, source_target_pairs={{0,8},{1,13},{2,10},{3,15},{4,12},{5,9},{6,14},{7,11},{8,0},{9,5},... | collective-permute-start | bytes 98312 | tf_op jit(solution)/shard_map/ppermute | solution.py:88
  10.1 4.9 %collective-permute-start.10 = (bf16[128,128]{1,0:T(8,128)(2,1)S(1)}, bf16[128,128]{1,0:T(8,128)(2,1)S(1)}, u32[]{:S(2)}, u32[]{:S(2)}) collective-permute-start(bf16[128,128]{1,0:T(8,128)(2,1)S(1)} %copy-done.3), channel_id=1, source_target_pairs={{0,1},{1,0},{2,3},{3,2},{4,5},{5,4},{6,7},{7,6},{8,9},{9,8},{10,11... | collective-permute-start | bytes 98312 | tf_op jit(solution)/shard_map/ppermute | solution.py:92
  12.3 2.8 %collective-permute-start.5 = (bf16[128,128]{1,0:T(8,128)(2,1)S(1)}, bf16[128,128]{1,0:T(8,128)(2,1)S(1)}, u32[]{:S(2)}, u32[]{:S(2)}) collective-permute-start(bf16[128,128]{1,0:T(8,128)(2,1)S(1)} %collective-permute-done.2.x0), channel_id=1, source_target_pairs={{0,1},{1,0},{2,3},{3,2},{4,5},{5,4},{6,7},{7,6},{8,9},{9,8},{10,11... | collective-permute-start | bytes 98312 | tf_op jit(solution)/shard_map/ppermute | solution.py:92
  13.2 1.8 %collective-permute-start.7 = (bf16[128,128]{1,0:T(8,128)(2,1)S(1)}, bf16[128,128]{1,0:T(8,128)(2,1)S(1)}, u32[]{:S(2)}, u32[]{:S(2)}) collective-permute-start(bf16[128,128]{1,0:T(8,128)(2,1)S(1)} %collective-permute-done.4.x2), channel_id=1, source_target_pairs={{0,1},{1,0},{2,3},{3,2},{4,5},{5,4},{6,7},{7,6},{8,9},{9,8},{10,11... | collective-permute-start | bytes 98312 | tf_op jit(solution)/shard_map/ppermute | solution.py:92
  14.1 1.6 %collective-permute-start.6 = (bf16[128,128]{1,0:T(8,128)(2,1)S(1)}, bf16[128,128]{1,0:T(8,128)(2,1)S(1)}, u32[]{:S(2)}, u32[]{:S(2)}) collective-permute-start(bf16[128,128]{1,0:T(8,128)(2,1)S(1)} %collective-permute-done.3.x1), channel_id=1, source_target_pairs={{0,1},{1,0},{2,3},{3,2},{4,5},{5,4},{6,7},{7,6},{8,9},{9,8},{10,11... | collective-permute-start | bytes 98312 | tf_op jit(solution)/shard_map/ppermute | solution.py:92
  14.8 1.4 %collective-permute-start.1 = (bf16[704,128]{1,0:T(8,128)(2,1)S(1)}, bf16[704,128]{1,0:T(8,128)(2,1)S(1)}, u32[]{:S(2)}, u32[]{:S(2)}) collective-permute-start(bf16[704,128]{1,0:T(8,128)(2,1)S(1)} %collective-permute-done.p), channel_id=1, source_target_pairs={{0,1},{1,0},{2,3},{3,2},{4,5},{5,4},{6,7},{7,6},{8,9},{9,8},{10,11... | collective-permute-start | bytes 540680 | tf_op jit(solution)/shard_map/ppermute | solution.py:92
  17.1 4.5 %collective-permute-start.13 = (bf16[256,128]{1,0:T(8,128)(2,1)S(1)}, bf16[256,128]{1,0:T(8,128)(2,1)S(1)}, u32[]{:S(2)}, u32[]{:S(2)}) collective-permute-start(bf16[256,128]{1,0:T(8,128)(2,1)S(1)} %get-tuple-element.20.refs_2_), channel_id=1, source_target_pairs={{0,4},{1,5},{2,6},{3,7},{4,0},{5,1},{6,2},{7,3},{8,12},{9,13},{10,... | collective-permute-start | bytes 196616 | tf_op jit(solution)/shard_map/ppermute | solution.py:88
  18.6 7.9 %collective-permute-start.12 = (bf16[256,128]{1,0:T(8,128)(2,1)S(1)}, bf16[256,128]{1,0:T(8,128)(2,1)S(1)}, u32[]{:S(2)}, u32[]{:S(2)}) collective-permute-start(bf16[256,128]{1,0:T(8,128)(2,1)S(1)} %get-tuple-element.20.refs_2_), channel_id=1, source_target_pairs={{0,8},{1,9},{2,10},{3,11},{4,12},{5,13},{6,14},{7,15},{8,0},{9,1},... | collective-permute-start | bytes 196616 | tf_op jit(solution)/shard_map/ppermute | solution.py:88
  19.5 7.0 %collective-permute-start.11 = (bf16[256,128]{1,0:T(8,128)(2,1)S(1)}, bf16[256,128]{1,0:T(8,128)(2,1)S(1)}, u32[]{:S(2)}, u32[]{:S(2)}) collective-permute-start(bf16[256,128]{1,0:T(8,128)(2,1)S(1)} %get-tuple-element.20.refs_2_), channel_id=1, source_target_pairs={{0,12},{1,13},{2,14},{3,15},{4,8},{5,9},{6,10},{7,11},{8,4},{9,5},... | collective-permute-start | bytes 196616 | tf_op jit(solution)/shard_map/ppermute | solution.py:88
  21.5 5.5 %collective-permute-start.16 = (bf16[256,128]{1,0:T(8,128)(2,1)S(1)}, bf16[256,128]{1,0:T(8,128)(2,1)S(1)}, u32[]{:S(2)}, u32[]{:S(2)}) collective-permute-start(bf16[256,128]{1,0:T(8,128)(2,1)S(1)} %collective-permute-done.13.refs_5_), channel_id=1, source_target_pairs={{0,1},{1,0},{2,3},{3,2},{4,5},{5,4},{6,7},{7,6},{8,9},{9,8},{10,11... | collective-permute-start | bytes 196616 | tf_op jit(solution)/shard_map/ppermute | solution.py:92
  26.5 1.3 %collective-permute-start.15 = (bf16[256,128]{1,0:T(8,128)(2,1)S(1)}, bf16[256,128]{1,0:T(8,128)(2,1)S(1)}, u32[]{:S(2)}, u32[]{:S(2)}) collective-permute-start(bf16[256,128]{1,0:T(8,128)(2,1)S(1)} %collective-permute-done.12.refs_4_), channel_id=1, source_target_pairs={{0,1},{1,0},{2,3},{3,2},{4,5},{5,4},{6,7},{7,6},{8,9},{9,8},{10,11... | collective-permute-start | bytes 196616 | tf_op jit(solution)/shard_map/ppermute | solution.py:92
  26.5 1.4 %collective-permute-start.14 = (bf16[256,128]{1,0:T(8,128)(2,1)S(1)}, bf16[256,128]{1,0:T(8,128)(2,1)S(1)}, u32[]{:S(2)}, u32[]{:S(2)}) collective-permute-start(bf16[256,128]{1,0:T(8,128)(2,1)S(1)} %collective-permute-done.11.refs_3_), channel_id=1, source_target_pairs={{0,1},{1,0},{2,3},{3,2},{4,5},{5,4},{6,7},{7,6},{8,9},{9,8},{10,11... | collective-permute-start | bytes 196616 | tf_op jit(solution)/shard_map/ppermute | solution.py:92

commit v3 on v2

--- a/solution.py
+++ b/solution.py
@@ -74,8 +74,8 @@
     return activation, grad_input, total / math.sqrt(sections * reps * width)
 
 
-SHARED = (((3, 1), (2, 1)), ((2, 0), (3, 0)), ((1, 0), (1, 1)))
-ACROSS = ((3, 0), (2, 0), (1, 0))
+SHARED = (((3, 1), (3, 0)), ((1, 0), (1, 1)), ((2, 0), (2, 1)))
+ACROSS = ((3, 0), (1, 0), (2, 0))
 
 
 def fetch(value, first, second=None):
@@ -106,25 +106,33 @@
     )(*held)
 
 
-def load_kernel(count, *refs):
-    sources, targets, sems = refs[:count], refs[count : 2 * count], refs[-1]
-    copies = [
-        pltpu.make_async_copy(source, target, sems.at[i])
-        for i, (source, target) in enumerate(zip(sources, targets))
-    ]
+def load_kernel(a, x, g, w, m, b, ao, xo, go, wo, mo, parts, held, sems):
+    pairs = ((a, ao), (x, xo), (g, go), (w, wo), (m, mo), (b, held))
+    copies = [pltpu.make_async_copy(p, q, sems.at[i]) for i, (p, q) in enumerate(pairs)]
     for copy in copies:
         copy.start()
-    for copy in copies:
+    for copy in copies[::-1]:
         copy.wait()
+        if copy is copies[-1]:
+            rest = held[...]
+            for i in range(3):
+                part = rest.astype(BF16)
+                parts[i : i + 1] = part
+                rest = rest - part.astype(F32)
 
 
 def load(*arrays):
+    row = arrays[-1]
+    outs = [pltpu.VMEM(x.shape, x.dtype) for x in arrays[:-1]] + [vmem(16, row.shape[1])]
     return pl.pallas_call(
-        lambda *refs: load_kernel(len(arrays), *refs),
-        out_shape=[pltpu.VMEM(x.shape, x.dtype) for x in arrays],
+        load_kernel,
+        out_shape=outs,
         in_specs=[pl.BlockSpec(memory_space=pl.ANY)] * len(arrays),
-        out_specs=[pl.BlockSpec(memory_space=pltpu.VMEM)] * len(arrays),
-        scratch_shapes=[pltpu.SemaphoreType.DMA((len(arrays),))],
+        out_specs=[pl.BlockSpec(memory_space=pltpu.VMEM)] * len(outs),
+        scratch_shapes=[
+            pltpu.VMEM(row.shape, row.dtype),
+            pltpu.SemaphoreType.DMA((len(arrays),)),
+        ],
     )(*arrays)
 
 
@@ -133,7 +141,25 @@
     return jnp.where(zero, first, second), jnp.where(zero, second, first)
 
 
-def forward_kernel(own, p, q, x, x0, x1, x2, y0, y1, y2, w, w_, b, b_, g, g_, act, back, msg, mine, rows, xs):
+def mask_rows(entries, blocks, sections):
+    row = lax.broadcasted_iota(jnp.int32, entries.shape, 0)
+    lane = lax.broadcasted_iota(jnp.int32, entries.shape, 1)
+    picked = jnp.zeros(entries.shape, F32)
+    for q in range(blocks):
+        here = (row // sections == q) & (lane == row % sections)
+        picked = jnp.where(here, entries[q : q + 1].astype(F32), picked)
+    ones = jnp.ones((entries.shape[1],) * 2, BF16)
+    return jnp.dot(picked.astype(BF16), ones, preferred_element_type=F32).astype(BF16)
+
+
+def pack_kernel(*refs):
+    at = 0
+    for ref in refs[:-1]:
+        refs[-1][at : at + ref.shape[0]] = ref[...]
+        at += ref.shape[0]
+
+
+def forward_kernel(own, give, x, here, there, act, back, msg, mine, rows, xs):
     n = x.shape[0]
     sections = own.shape[0]
     d, r, c = (lax.axis_index(a) for a in CORES)
@@ -141,31 +167,43 @@
     def columns(s, rep):
         return pl.ds(pl.multiple_of((s * 2 + rep) * n, n), n)
 
-    first, second = in_order(p[...], q[...])
+    low, high = (sections + 1) * n, (sections + 1) * n + n // 2
+    end = give.shape[0]
+    flags = mask_rows(give[high:end], 2, sections)
+    flags_ = mask_rows(here[high:end], 2, sections)
+    first, second = in_order(here[...], there[...])
     for s in range(sections):
-        rows[:, columns(s, r)] = own[s]
-        rows[:n, columns(s, 1 - r)] = first[s * n : (s + 1) * n]
-        rows[n:, columns(s, 1 - r)] = second[s * n : (s + 1) * n]
-    low, high = (sections + 1) * n, (sections + 1) * n + n // 2
+        for k, part in enumerate((first, second)):
+            at = slice(k * n, (k + 1) * n)
+            entry = slice(k * sections + s, k * sections + s + 1)
+            rows[at, columns(s, r)] = own[s, at] * flags[entry]
+            rows[at, columns(s, 1 - r)] = part[s * n : (s + 1) * n] * flags_[entry]
     xs[columns(d, r), :] = x[...]
     xs[columns(d, 1 - r), :] = jnp.concatenate([first[low:high], second[low:high]], axis=0)
-    for pair, direct, swapped in zip(SHARED, (x0, x1, x2), (y0, y1, y2)):
-        for (dx, rx), value in zip(pair, in_order(direct[...], swapped[...])):
-            xs[columns(d ^ dx, r ^ rx), :] = value
+    for i, pair in enumerate(SHARED):
+        for (dx, rx), part in zip(pair, (first, second)):
+            xs[columns(d ^ dx, r ^ rx), :] = part[end + i * n : end + (i + 1) * n]
+    end += len(SHARED) * n
     mine[...] = rows[pl.ds(pl.multiple_of(r * n, n), n), :]
 
-    weight = jnp.concatenate(in_order(w[...], w_[...]), axis=1)
-    bias = jnp.concatenate(in_order(b[...], b_[...]), axis=1)
-    here = jnp.concatenate(in_order(g[...], g_[...]), axis=1)
-    there = jnp.concatenate([first[sections * n : low], second[sections * n : low]], axis=1)
+    weight, ours = (
+        jnp.concatenate([part[k : k + n] for part in (first, second)], axis=1)
+        for k in (end, end + n)
+    )
+    end += 2 * n
+    bias = jnp.concatenate(
+        [jnp.sum(part[end : end + 3].astype(F32), axis=0, keepdims=True) for part in (first, second)],
+        axis=1,
+    )
+    theirs = jnp.concatenate([part[sections * n : low] for part in (first, second)], axis=1)
     zero = r == 0
     cotangent = jnp.concatenate(
-        [jnp.where(zero, here, there), jnp.where(zero, there, here)], axis=0
+        [jnp.where(zero, ours, theirs), jnp.where(zero, theirs, ours)], axis=0
     )
     high, low, activation, grad_pre, v = forward_and_gp(
         rows[...], xs[...], weight, bias, cotangent
     )
-    half = w.shape[1]
+    half = msg.shape[1]
     zero = c == 0
     activation = jnp.where(r == 0, activation[:n], activation[n:])
     act[...] = jnp.where(zero, activation[:, :half], activation[:, half:])
@@ -197,26 +235,32 @@
     c = lax.axis_index("sub")
     few = nodes // 2
 
-    far = fetch(features, *SHARED[0])
-    adj, held, grads, flags = load(adjacency, features, cotangent, mask.transpose(0, 2, 1))
-    operator = masked_rows(adj, flags.transpose(0, 2, 1), 0, 2 * nodes)
-    give = lax.dynamic_slice_in_dim(operator, c * nodes, nodes, axis=1).reshape(sections * nodes, width)
-    give = jnp.concatenate([give, grads, lax.dynamic_slice_in_dim(held, c * few, few)], axis=0)
+
+    adj, held, grads, wide, flat, row = load(
+        adjacency, features, cotangent, weight, mask.transpose(0, 2, 1), bias[None, :]
+    )
+    own = adj.transpose(1, 0, 2)
+    give = lax.dynamic_slice_in_dim(adj, c * nodes, nodes, axis=0).transpose(1, 0, 2)
+    flat = jnp.pad(flat[:, 0].astype(BF16), ((0, 14), (0, width - sections)))
+    give = jnp.concatenate(
+        [give.reshape(sections * nodes, width), grads, lax.dynamic_slice_in_dim(held, c * few, few), flat],
+        axis=0,
+    )
     taken = fetch(give, (0, 1))
-    xs = [far] + [fetch(features, *pair) for pair in SHARED[1:]]
-    row = bias[None, :]
-    w_, b_, g_ = swap(weight), swap(row), swap(cotangent)
-    ys = [swap(x) for x in xs]
+    xs = [fetch(features, *pair) for pair in SHARED]
+    parts = (taken, *xs, wide, grads, row)
+    (here,) = vmem_call(pack_kernel, [vmem(sum(x.shape[0] for x in parts), width)], *parts)
+    there = swap(here)
     act, back, msg, mine = pl.pallas_call(
         forward_kernel,
         out_shape=[vmem(nodes, half), vmem(2 * nodes, feat), vmem(nodes + feat, half), vmem(nodes, total)],
-        in_specs=[pl.BlockSpec(memory_space=pltpu.VMEM)] * 16,
+        in_specs=[pl.BlockSpec(memory_space=pltpu.VMEM)] * 5,
         out_specs=[pl.BlockSpec(memory_space=pltpu.VMEM)] * 4,
         scratch_shapes=[vmem(2 * nodes, total), vmem(total, feat)],
     )(
         *(
             pltpu.with_memory_space_constraint(x, pltpu.VMEM)
-            for x in (operator, taken, swap(taken), held, *xs, *ys, weight, w_, row, b_, grads, g_)
+            for x in (own, give, held, here, there)
         )
     )
     ms = [fetch(msg, off) for off in ACROSS]

time: 29 us -> 27.1 us (0.934)
  starting transfers between devices: 13.8 us -> 12.5 us
  other arithmetic: 0.42 us -> 0.02 us
    ppermute x10 -> x4, starting transfers between devices: 1.98 us -> 0.58 us  [swap(): return lax.ppermute(value, 'sub', [(0, 1), (1, 0)])]
    ppermute x7, waiting for transfers between devices: 8.79 us -> 8.19 us  [fetch(): return lax.ppermute(value, CORES, pairs)]
    ppermute x10 -> x4, waiting for transfers between devices: 2.09 us -> 2.51 us  [swap(): return lax.ppermute(value, 'sub', [(0, 1), (1, 0)])]
    pallas_call x1 -> x2, Pallas kernels: 0.99 us -> 1.03 us  [the longest x1 1.01 us: load(): pl.pallas_call(load_kernel, out_shape=outs, in_specs=[pl.BlockSpec(memory...]
  transfers between devices with their start and end apart: 17 -> 11, of which waited for: 8 -> 7; matrix products, arithmetic and copies ran while one was open for 1% -> 0% of each run, Pallas kernels for 0% -> 0%
where the time goes in v3:
time: 27.1 us; the launch traced here: 26.9 us
  starting transfers between devices  12.5 us (46%)
  waiting for transfers between devices  10.7 us (39%)
  Pallas kernels  2.8 us (10%)
  between operations  0.74 us (3%)
    ppermute x7, starting transfers between devices, fetch(): return lax.ppermute(value, CORES, pairs)  11.9 us
    ppermute x7, waiting for transfers between devices, fetch(): return lax.ppermute(value, CORES, pairs)  8.19 us
    ppermute x4, waiting for transfers between devices, swap(): return lax.ppermute(value, 'sub', [(0, 1), (1, 0)])  2.51 us
    pallas_call x1, Pallas kernels, load(): pl.pallas_call(load_kernel, out_shape=outs, in_specs=[pl.BlockSpec(memory...  1.01 us
    pallas_call x1, Pallas kernels, direct(): pl.pallas_call(lambda *refs: backward_kernel(scale, *refs), out_shape=[ja...  0.89 us
    pallas_call x1, Pallas kernels, direct(): pl.pallas_call(forward_kernel, out_shape=[vmem(nodes, half), vmem(2 * nod...  0.89 us
    ppermute x4, starting transfers between devices, swap(): return lax.ppermute(value, 'sub', [(0, 1), (1, 0)])  0.58 us
  transfers between devices with their start and end apart: 11, of which 7 were waited for; matrix products, arithmetic and copies ran while one was open for 0% of the time, Pallas kernels for 0%

profile of v3, /device:TPU:0, one launch (start us, length us, event | category | flops | bytes accessed | tf_op | source)
XLA Modules:
  0.0 26.9 jit_solution(11643021470639831090)
XLA Ops:
  0.6 1.0 %shard_map.85 = (bf16[256,4,128]{2,1,0:T(4,128)(2,1)S(1)}, bf16[128,128]{1,0:T(8,128)(2,1)S(1)}, bf16[128,128]{1,0:T(8,128)(2,1)S(1)}, bf16[128,128]{1,0:T(8,128...) custom-call(bf16[256,4,128]{2,1,0:T(4,128)(2,1)} %a.1, bf16[128,128]{1,0:T(8,128)(2,1)} %x.3, ...), custom_call_target="tpu_custom_call" | custom-call | tf_op jit(solution)/shard_map/pallas_call | solution.py:127
  1.7 0.1 dynamic-slice_bitcast_fusion
  1.8 0.0 copy-start
  1.8 3.0 %collective-permute-start = (bf16[720,128]{1,0:T(8,128)(2,1)S(1)}, bf16[720,128]{1,0:T(8,128)(2,1)S(1)}, u32[]{:S(2)}, u32[]{:S(2)}) collective-permute-start(bf16[720,128]{1,0:T(8,128)(2,1)S(1)} %fusion.1.give), channel_id=1, source_target_pairs={{0,2},{1,3},{2,0},{3,1},{4,6},{5,7},{6,4},{7,5},{8,10},{9,11},{10,... | collective-permute-start | bytes 552968 | tf_op jit(solution)/shard_map/ppermute | solution.py:88
  4.8 0.0 copy-done
  4.8 3.7 %collective-permute-start.1 = (bf16[128,128]{1,0:T(8,128)(2,1)S(1)}, bf16[128,128]{1,0:T(8,128)(2,1)S(1)}, u32[]{:S(2)}, u32[]{:S(2)}) collective-permute-start(bf16[128,128]{1,0:T(8,128)(2,1)S(1)} %copy-done), channel_id=1, source_target_pairs={{0,14},{1,13},{2,12},{3,15},{4,10},{5,9},{6,8},{7,11},{8,6},{9,5},... | collective-permute-start | bytes 98312 | tf_op jit(solution)/shard_map/ppermute | solution.py:88
  8.5 0.0 collective-permute-start.3
  8.5 0.8 %collective-permute-start.2 = (bf16[128,128]{1,0:T(8,128)(2,1)S(1)}, bf16[128,128]{1,0:T(8,128)(2,1)S(1)}, u32[]{:S(2)}, u32[]{:S(2)}) collective-permute-start(bf16[128,128]{1,0:T(8,128)(2,1)S(1)} %copy-done), channel_id=1, source_target_pairs={{0,4},{1,7},{2,6},{3,5},{4,0},{5,3},{6,2},{7,1},{8,12},{9,15},{10,... | collective-permute-start | bytes 98312 | tf_op jit(solution)/shard_map/ppermute | solution.py:88
  9.3 2.5 %collective-permute-done.1.refs_1_ = bf16[128,128]{1,0:T(8,128)(2,1)S(1)} collective-permute-done((bf16[128,128]{1,0:T(8,128)(2,1)S(1)}, bf16[128,128]{1,0:T(8,128)(2,1)S(1)}, u32[]{:S(2)}, u32[]{:S(2)}) %collective-permute-start.1) | collective-permute-done | bytes 32800 | tf_op jit(solution)/shard_map/ppermute | solution.py:88
  11.8 1.6 %collective-permute-done.3.refs_3_ = bf16[128,128]{1,0:T(8,128)(2,1)S(1)} collective-permute-done((bf16[128,128]{1,0:T(8,128)(2,1)S(1)}, bf16[128,128]{1,0:T(8,128)(2,1)S(1)}, u32[]{:S(2)}, u32[]{:S(2)}) %collective-permute-start.3) | collective-permute-done | bytes 32800 | tf_op jit(solution)/shard_map/ppermute | solution.py:88
  13.3 0.0 collective-permute-done.2.refs_2_
  13.3 0.0 collective-permute-done.refs_0_
  13.4 0.1 collective-permute-start.4
  13.5 1.6 %collective-permute-done.4.there = bf16[1376,128]{1,0:T(8,128)(2,1)S(1)} collective-permute-done((bf16[1376,128]{1,0:T(8,128)(2,1)S(1)}, bf16[1376,128]{1,0:T(8,128)(2,1)S(1)}, u32[]{:S(2)}, u32[]{:S(2)}) %collective-permute-start.4) | collective-permute-done | bytes 352288 | tf_op jit(solution)/shard_map/ppermute | solution.py:92
  15.1 0.9 %shard_map.87 = (bf16[128,128]{1,0:T(8,128)(2,1)S(1)}, bf16[256,128]{1,0:T(8,128)(2,1)S(1)}, bf16[256,128]{1,0:T(8,128)(2,1)S(1)}, bf16[128,1024]{1,0:T(8,128)(2,1)S(1)}) custom-call(bf16[4,256,128]{2,1,0:T(8,128)(2,1)S(1)} %bitcast.13, bf16[720,128]{1,0:T(8,128)(2,1)S(1)} %fusion.1.give, bf16[128,128]{1,0:T(8,128)(2,1)S(1)} %get-tuple-element.18.x, ...), custom_call_target="tpu_custom_call" | custom-call | tf_op jit(solution)/shard_map/pallas_call | solution.py:254
  16.0 2.1 %collective-permute-start.7 = (bf16[256,128]{1,0:T(8,128)(2,1)S(1)}, bf16[256,128]{1,0:T(8,128)(2,1)S(1)}, u32[]{:S(2)}, u32[]{:S(2)}) collective-permute-start(bf16[256,128]{1,0:T(8,128)(2,1)S(1)} %get-tuple-element.24.refs_2_), channel_id=1, source_target_pairs={{0,8},{1,9},{2,10},{3,11},{4,12},{5,13},{6,14},{7,15},{8,0},{9,1},... | collective-permute-start | bytes 196616 | tf_op jit(solution)/shard_map/ppermute | solution.py:88
  18.1 0.3 collective-permute-start.6
  18.3 2.1 %collective-permute-start.5 = (bf16[256,128]{1,0:T(8,128)(2,1)S(1)}, bf16[256,128]{1,0:T(8,128)(2,1)S(1)}, u32[]{:S(2)}, u32[]{:S(2)}) collective-permute-start(bf16[256,128]{1,0:T(8,128)(2,1)S(1)} %get-tuple-element.24.refs_2_), channel_id=1, source_target_pairs={{0,12},{1,13},{2,14},{3,15},{4,8},{5,9},{6,10},{7,11},{8,4},{9,5},... | collective-permute-start | bytes 196616 | tf_op jit(solution)/shard_map/ppermute | solution.py:88
  20.4 1.6 %collective-permute-done.7.refs_5_ = bf16[256,128]{1,0:T(8,128)(2,1)S(1)} collective-permute-done((bf16[256,128]{1,0:T(8,128)(2,1)S(1)}, bf16[256,128]{1,0:T(8,128)(2,1)S(1)}, u32[]{:S(2)}, u32[]{:S(2)}) %collective-permute-start.7) | collective-permute-done | bytes 65568 | tf_op jit(solution)/shard_map/ppermute | solution.py:88
  22.0 0.0 collective-permute-start.10
  22.0 2.6 %collective-permute-done.6.refs_4_ = bf16[256,128]{1,0:T(8,128)(2,1)S(1)} collective-permute-done((bf16[256,128]{1,0:T(8,128)(2,1)S(1)}, bf16[256,128]{1,0:T(8,128)(2,1)S(1)}, u32[]{:S(2)}, u32[]{:S(2)}) %collective-permute-start.6) | collective-permute-done | bytes 65568 | tf_op jit(solution)/shard_map/ppermute | solution.py:88
  24.6 0.0 collective-permute-start.9
  24.6 0.0 collective-permute-done.5.refs_3_
  24.6 0.5 %collective-permute-start.8 = (bf16[256,128]{1,0:T(8,128)(2,1)S(1)}, bf16[256,128]{1,0:T(8,128)(2,1)S(1)}, u32[]{:S(2)}, u32[]{:S(2)}) collective-permute-start(bf16[256,128]{1,0:T(8,128)(2,1)S(1)} %collective-permute-done.5.refs_3_), channel_id=1, source_target_pairs={{0,1},{1,0},{2,3},{3,2},{4,5},{5,4},{6,7},{7,6},{8,9},{9,8},{10,11... | collective-permute-start | bytes 196616 | tf_op jit(solution)/shard_map/ppermute | solution.py:92
  25.1 0.0 collective-permute-done.10.refs_8_
  25.1 0.7 %collective-permute-done.9.refs_7_ = bf16[256,128]{1,0:T(8,128)(2,1)S(1)} collective-permute-done((bf16[256,128]{1,0:T(8,128)(2,1)S(1)}, bf16[256,128]{1,0:T(8,128)(2,1)S(1)}, u32[]{:S(2)}, u32[]{:S(2)}) %collective-permute-start.9) | collective-permute-done | bytes 65568 | tf_op jit(solution)/shard_map/ppermute | solution.py:92
  25.9 0.2 collective-permute-done.8.refs_6_
  26.0 0.9 %shard_map.88 = (bf16[128,128]{1,0:T(8,128)(2,1)}, f32[128,128]{1,0:T(8,128)}, bf16[128,128]{1,0:T(8,128)(2,1)}) custom-call(bf16[128,1024]{1,0:T(8,128)(2,1)S(1)} %get-tuple-element.22.refs_0_, bf16[256,128]{1,0:T(8,128)(2,1)S(1)} %get-tuple-element.23.refs_1_, bf16[256,128]{1,0:T(8,128)(2,1)S(1)} %get-tuple-element.24.refs_2_, ...), custom_call_target="tpu_custom_call" | custom-call | tf_op jit(solution)/shard_map/pallas_call | solution.py:269
  (7 shorter events, 0.1 us)
Async XLA Ops:
  1.8 3.0 %copy-start = (bf16[128,128]{1,0:T(8,128)(2,1)S(1)}, bf16[128,128]{1,0:T(8,128)(2,1)}, u32[]{:S(2)}) copy-start(bf16[128,128]{1,0:T(8,128)(2,1)} %x.3) | copy-start | bytes 98308
  1.8 11.5 %collective-permute-start = (bf16[720,128]{1,0:T(8,128)(2,1)S(1)}, bf16[720,128]{1,0:T(8,128)(2,1)S(1)}, u32[]{:S(2)}, u32[]{:S(2)}) collective-permute-start(bf16[720,128]{1,0:T(8,128)(2,1)S(1)} %fusion.1.give), channel_id=1, source_target_pairs={{0,2},{1,3},{2,0},{3,1},{4,6},{5,7},{6,4},{7,5},{8,10},{9,11},{10,... | collective-permute-start | bytes 552968 | tf_op jit(solution)/shard_map/ppermute | solution.py:88
  4.8 7.0 %collective-permute-start.1 = (bf16[128,128]{1,0:T(8,128)(2,1)S(1)}, bf16[128,128]{1,0:T(8,128)(2,1)S(1)}, u32[]{:S(2)}, u32[]{:S(2)}) collective-permute-start(bf16[128,128]{1,0:T(8,128)(2,1)S(1)} %copy-done), channel_id=1, source_target_pairs={{0,14},{1,13},{2,12},{3,15},{4,10},{5,9},{6,8},{7,11},{8,6},{9,5},... | collective-permute-start | bytes 98312 | tf_op jit(solution)/shard_map/ppermute | solution.py:88
  8.5 4.8 %collective-permute-start.3 = (bf16[128,128]{1,0:T(8,128)(2,1)S(1)}, bf16[128,128]{1,0:T(8,128)(2,1)S(1)}, u32[]{:S(2)}, u32[]{:S(2)}) collective-permute-start(bf16[128,128]{1,0:T(8,128)(2,1)S(1)} %copy-done), channel_id=1, source_target_pairs={{0,8},{1,11},{2,10},{3,9},{4,12},{5,15},{6,14},{7,13},{8,0},{9,3},... | collective-permute-start | bytes 98312 | tf_op jit(solution)/shard_map/ppermute | solution.py:88
  8.5 4.8 %collective-permute-start.2 = (bf16[128,128]{1,0:T(8,128)(2,1)S(1)}, bf16[128,128]{1,0:T(8,128)(2,1)S(1)}, u32[]{:S(2)}, u32[]{:S(2)}) collective-permute-start(bf16[128,128]{1,0:T(8,128)(2,1)S(1)} %copy-done), channel_id=1, source_target_pairs={{0,4},{1,7},{2,6},{3,5},{4,0},{5,3},{6,2},{7,1},{8,12},{9,15},{10,... | collective-permute-start | bytes 98312 | tf_op jit(solution)/shard_map/ppermute | solution.py:88
  13.4 1.7 %collective-permute-start.4 = (bf16[1376,128]{1,0:T(8,128)(2,1)S(1)}, bf16[1376,128]{1,0:T(8,128)(2,1)S(1)}, u32[]{:S(2)}, u32[]{:S(2)}) collective-permute-start(bf16[1376,128]{1,0:T(8,128)(2,1)S(1)} %shard_map.86.here), channel_id=1, source_target_pairs={{0,1},{1,0},{2,3},{3,2},{4,5},{5,4},{6,7},{7,6},{8,9},{9,8},{10,11... | collective-permute-start | bytes 1056776 | tf_op jit(solution)/shard_map/ppermute | solution.py:92
  16.0 6.0 %collective-permute-start.7 = (bf16[256,128]{1,0:T(8,128)(2,1)S(1)}, bf16[256,128]{1,0:T(8,128)(2,1)S(1)}, u32[]{:S(2)}, u32[]{:S(2)}) collective-permute-start(bf16[256,128]{1,0:T(8,128)(2,1)S(1)} %get-tuple-element.24.refs_2_), channel_id=1, source_target_pairs={{0,8},{1,9},{2,10},{3,11},{4,12},{5,13},{6,14},{7,15},{8,0},{9,1},... | collective-permute-start | bytes 196616 | tf_op jit(solution)/shard_map/ppermute | solution.py:88
  18.1 6.5 %collective-permute-start.6 = (bf16[256,128]{1,0:T(8,128)(2,1)S(1)}, bf16[256,128]{1,0:T(8,128)(2,1)S(1)}, u32[]{:S(2)}, u32[]{:S(2)}) collective-permute-start(bf16[256,128]{1,0:T(8,128)(2,1)S(1)} %get-tuple-element.24.refs_2_), channel_id=1, source_target_pairs={{0,4},{1,5},{2,6},{3,7},{4,0},{5,1},{6,2},{7,3},{8,12},{9,13},{10,... | collective-permute-start | bytes 196616 | tf_op jit(solution)/shard_map/ppermute | solution.py:88
  18.3 6.3 %collective-permute-start.5 = (bf16[256,128]{1,0:T(8,128)(2,1)S(1)}, bf16[256,128]{1,0:T(8,128)(2,1)S(1)}, u32[]{:S(2)}, u32[]{:S(2)}) collective-permute-start(bf16[256,128]{1,0:T(8,128)(2,1)S(1)} %get-tuple-element.24.refs_2_), channel_id=1, source_target_pairs={{0,12},{1,13},{2,14},{3,15},{4,8},{5,9},{6,10},{7,11},{8,4},{9,5},... | collective-permute-start | bytes 196616 | tf_op jit(solution)/shard_map/ppermute | solution.py:88
  22.0 3.1 %collective-permute-start.10 = (bf16[256,128]{1,0:T(8,128)(2,1)S(1)}, bf16[256,128]{1,0:T(8,128)(2,1)S(1)}, u32[]{:S(2)}, u32[]{:S(2)}) collective-permute-start(bf16[256,128]{1,0:T(8,128)(2,1)S(1)} %collective-permute-done.7.refs_5_), channel_id=1, source_target_pairs={{0,1},{1,0},{2,3},{3,2},{4,5},{5,4},{6,7},{7,6},{8,9},{9,8},{10,11... | collective-permute-start | bytes 196616 | tf_op jit(solution)/shard_map/ppermute | solution.py:92
  24.6 1.3 %collective-permute-start.9 = (bf16[256,128]{1,0:T(8,128)(2,1)S(1)}, bf16[256,128]{1,0:T(8,128)(2,1)S(1)}, u32[]{:S(2)}, u32[]{:S(2)}) collective-permute-start(bf16[256,128]{1,0:T(8,128)(2,1)S(1)} %collective-permute-done.6.refs_4_), channel_id=1, source_target_pairs={{0,1},{1,0},{2,3},{3,2},{4,5},{5,4},{6,7},{7,6},{8,9},{9,8},{10,11... | collective-permute-start | bytes 196616 | tf_op jit(solution)/shard_map/ppermute | solution.py:92
  24.6 1.4 %collective-permute-start.8 = (bf16[256,128]{1,0:T(8,128)(2,1)S(1)}, bf16[256,128]{1,0:T(8,128)(2,1)S(1)}, u32[]{:S(2)}, u32[]{:S(2)}) collective-permute-start(bf16[256,128]{1,0:T(8,128)(2,1)S(1)} %collective-permute-done.5.refs_3_), channel_id=1, source_target_pairs={{0,1},{1,0},{2,3},{3,2},{4,5},{5,4},{6,7},{7,6},{8,9},{9,8},{10,11... | collective-permute-start | bytes 196616 | tf_op jit(solution)/shard_map/ppermute | solution.py:92

commit v4 on v3

--- a/solution.py
+++ b/solution.py
@@ -24,16 +24,17 @@
     grad_pre = (cotangent.astype(F32) * sigma * (1.0 + pre * (1.0 - sigma))).astype(BF16)
     back = lax.dot_general(
         grad_pre, weight, (((1,), (1,)), ((), ())), preferred_element_type=F32
-    ).astype(BF16)
+    )
     return high, low, activation, grad_pre, back
 
 
+def transposed_dot(a, b):
+    return lax.dot_general(a, b, (((0,), (0,)), ((), ())), preferred_element_type=F32)
+
+
 def weight_term(high, low, grads):
-    return lax.dot_general(
-        jnp.concatenate([high, low], axis=0),
-        jnp.concatenate([grads, grads], axis=0),
-        (((0,), (0,)), ((), ())),
-        preferred_element_type=F32,
+    return transposed_dot(
+        jnp.concatenate([high, low], axis=0), jnp.concatenate([grads, grads], axis=0)
     )
 
 
@@ -69,13 +70,13 @@
     activation = lax.dynamic_slice_in_dim(activation, mine, half, axis=1)
     grads = lax.dynamic_slice_in_dim(grad_pre, mine, half, axis=1)
     total = lax.psum(weight_term(high, low, grads), CHIPS)
-    backs = lax.all_gather(back, CHIPS, axis=0, tiled=True)
+    backs = lax.all_gather(back.astype(BF16), CHIPS, axis=0, tiled=True)
     grad_input = jnp.dot(operator, backs, preferred_element_type=F32).astype(BF16)
     return activation, grad_input, total / math.sqrt(sections * reps * width)
 
 
 SHARED = (((3, 1), (3, 0)), ((1, 0), (1, 1)), ((2, 0), (2, 1)))
-ACROSS = ((3, 0), (1, 0), (2, 0))
+ACROSS = ((3, 0), (2, 0))
 
 
 def fetch(value, first, second=None):
@@ -106,33 +107,31 @@
     )(*held)
 
 
-def load_kernel(a, x, g, w, m, b, ao, xo, go, wo, mo, parts, held, sems):
-    pairs = ((a, ao), (x, xo), (g, go), (w, wo), (m, mo), (b, held))
+def load_kernel(a, x, g, m, ao, fo, go, mo, sems):
+    c = lax.axis_index("sub")
+    pairs = (
+        (a.at[pl.ds(c * ao.shape[0], ao.shape[0])], ao),
+        (x.at[pl.ds(pl.multiple_of(c * fo.shape[0], 16), fo.shape[0])], fo),
+        (g, go),
+        (m, mo),
+    )
     copies = [pltpu.make_async_copy(p, q, sems.at[i]) for i, (p, q) in enumerate(pairs)]
     for copy in copies:
         copy.start()
-    for copy in copies[::-1]:
+    for copy in copies:
         copy.wait()
-        if copy is copies[-1]:
-            rest = held[...]
-            for i in range(3):
-                part = rest.astype(BF16)
-                parts[i : i + 1] = part
-                rest = rest - part.astype(F32)
-
-
-def load(*arrays):
-    row = arrays[-1]
-    outs = [pltpu.VMEM(x.shape, x.dtype) for x in arrays[:-1]] + [vmem(16, row.shape[1])]
+
+
+def load(adjacency, features, cotangent, mask):
+    arrays = (adjacency, features, cotangent, mask)
+    outs = [vmem(x.shape[0] // 2, *x.shape[1:]) for x in arrays[:2]]
+    outs += [pltpu.VMEM(x.shape, x.dtype) for x in arrays[2:]]
     return pl.pallas_call(
         load_kernel,
         out_shape=outs,
         in_specs=[pl.BlockSpec(memory_space=pl.ANY)] * len(arrays),
         out_specs=[pl.BlockSpec(memory_space=pltpu.VMEM)] * len(outs),
-        scratch_shapes=[
-            pltpu.VMEM(row.shape, row.dtype),
-            pltpu.SemaphoreType.DMA((len(arrays),)),
-        ],
+        scratch_shapes=[pltpu.SemaphoreType.DMA((len(outs),))],
     )(*arrays)
 
 
@@ -153,13 +152,19 @@
 
 
 def pack_kernel(*refs):
+    *arrays, row, out = refs
     at = 0
-    for ref in refs[:-1]:
-        refs[-1][at : at + ref.shape[0]] = ref[...]
+    for ref in arrays:
+        out[at : at + ref.shape[0]] = ref[...]
         at += ref.shape[0]
-
-
-def forward_kernel(own, give, x, here, there, act, back, msg, mine, rows, xs):
+    rest = row[...]
+    for i in range(3):
+        part = rest.astype(BF16)
+        out[at + i : at + i + 1] = part
+        rest = rest - part.astype(F32)
+
+
+def forward_kernel(own, give, x, here, there, act, far, near, kept, rows, xs):
     n = x.shape[0]
     sections = own.shape[0]
     d, r, c = (lax.axis_index(a) for a in CORES)
@@ -184,7 +189,6 @@
         for (dx, rx), part in zip(pair, (first, second)):
             xs[columns(d ^ dx, r ^ rx), :] = part[end + i * n : end + (i + 1) * n]
     end += len(SHARED) * n
-    mine[...] = rows[pl.ds(pl.multiple_of(r * n, n), n), :]
 
     weight, ours = (
         jnp.concatenate([part[k : k + n] for part in (first, second)], axis=1)
@@ -203,28 +207,57 @@
     high, low, activation, grad_pre, v = forward_and_gp(
         rows[...], xs[...], weight, bias, cotangent
     )
-    half = msg.shape[1]
+    half = far.shape[1]
     zero = c == 0
     activation = jnp.where(r == 0, activation[:n], activation[n:])
     act[...] = jnp.where(zero, activation[:, :half], activation[:, half:])
-    grads = jnp.where(zero, grad_pre[:, :half], grad_pre[:, half:])
-    back[...] = v
-    msg[:n] = jnp.where(zero, v[:n], v[n:])
-    msg[n:] = weight_term(high, low, grads).astype(BF16)
-
-
-def backward_kernel(scale, rows, back, msg, m0, m1, m2, s0, s1, s2, a, gi, gw, act, vs):
-    n = rows.shape[0]
-    d = lax.axis_index("dom")
+    term = weight_term(high, low, grad_pre).astype(BF16)
+    far[n : 2 * n] = term[:, :half]
+    far[2 * n :] = term[:, half:]
+    near[n // 2 :] = jnp.where(zero, term[:, :half], term[:, half:])
+
+    upper = v.astype(BF16)
+    lower = (v - upper.astype(F32)).astype(BF16)
+    v = jnp.concatenate([upper, lower], axis=0)
+
+    def give_back(s):
+        block = rows[:, columns(s, r)]
+        return transposed_dot(jnp.concatenate([block, block], axis=0), v)
+
+    kept[...] = give_back(d)
+    aside = give_back(d ^ 1).astype(BF16)
+    near[: n // 2] = jnp.where(zero, aside[: n // 2], aside[n // 2 :])
+    far[:n] = give_back(d ^ jnp.where(zero, ACROSS[0][0], ACROSS[1][0])).astype(BF16)
+
+
+def far_term(ref, core, n):
+    return ref[pl.ds(pl.multiple_of((1 + core) * n, n), n), :]
+
+
+def pack_back_kernel(far, near, out):
+    n = far.shape[0] // 3
+    out[:n] = far[:n]
+    out[n : 2 * n] = far_term(far, 1 - lax.axis_index("sub"), n)
+    out[2 * n :] = near[: n // 2]
+
+
+def backward_kernel(scale, kept, mine, far, near, there, a, gi, gw, act):
+    n = kept.shape[0]
+    c = lax.axis_index("sub")
     act[...] = a[...]
-    terms = {(0, 0): msg[n:].astype(F32)}
-    vs[pl.ds(pl.multiple_of(d * 2 * n, n), 2 * n), :] = back[...]
-    for off, direct, swapped in zip(ACROSS, (m0, m1, m2), (s0, s1, s2)):
-        terms[off] = direct[n:].astype(F32)
-        both = jnp.concatenate(in_order(direct[:n], swapped[:n]), axis=0)
-        vs[pl.ds(pl.multiple_of((d ^ off[0]) * 2 * n, n), 2 * n), :] = both
-    gw[...] = ((terms[0, 0] + terms[1, 0]) + (terms[2, 0] + terms[3, 0])) * scale
-    gi[...] = jnp.dot(rows[...], vs[...], preferred_element_type=F32).astype(BF16)
+    parts = {0: kept[...], 1: jnp.concatenate(in_order(near[: n // 2], there[2 * n :]), axis=0)}
+    terms = {0: far_term(mine, c, n), 1: near[n // 2 :]}
+    for (dx, _), part, term in zip(
+        ACROSS, in_order(far[:n], there[:n]), in_order(far_term(far, c, n), there[n : 2 * n])
+    ):
+        parts[dx], terms[dx] = part, term
+
+    def total(values):
+        values = [values[dx].astype(F32) for dx in range(4)]
+        return (values[0] + values[1]) + (values[2] + values[3])
+
+    gw[...] = total(terms) * scale
+    gi[...] = total(parts).astype(BF16)
 
 
 def direct(mesh, adjacency, mask, features, weight, bias, cotangent):
@@ -233,38 +266,45 @@
     total = sections * 2 * width
     half = weight.shape[1]
     c = lax.axis_index("sub")
-    few = nodes // 2
-
-
-    adj, held, grads, wide, flat, row = load(
-        adjacency, features, cotangent, weight, mask.transpose(0, 2, 1), bias[None, :]
-    )
-    own = adj.transpose(1, 0, 2)
-    give = lax.dynamic_slice_in_dim(adj, c * nodes, nodes, axis=0).transpose(1, 0, 2)
+
+
+    x0 = fetch(features, *SHARED[0])
+    x2 = fetch(features, *SHARED[2])
+    give, few, grads, flat = load(adjacency, features, cotangent, mask.transpose(0, 2, 1))
+    own = adjacency.transpose(1, 0, 2)
+    give = give.transpose(1, 0, 2)
     flat = jnp.pad(flat[:, 0].astype(BF16), ((0, 14), (0, width - sections)))
     give = jnp.concatenate(
-        [give.reshape(sections * nodes, width), grads, lax.dynamic_slice_in_dim(held, c * few, few), flat],
+        [give.reshape(sections * nodes, width), grads, few, flat],
         axis=0,
     )
+    late, give = lax.optimization_barrier((features, give))
+    x1 = fetch(late, *SHARED[1])
     taken = fetch(give, (0, 1))
-    xs = [fetch(features, *pair) for pair in SHARED]
-    parts = (taken, *xs, wide, grads, row)
-    (here,) = vmem_call(pack_kernel, [vmem(sum(x.shape[0] for x in parts), width)], *parts)
+    xs = [x0, x1, x2]
+    parts = (taken, *xs, weight, grads, bias[None, :])
+    (here,) = vmem_call(pack_kernel, [vmem(sum(x.shape[0] for x in parts) + 15, width)], *parts)
     there = swap(here)
-    act, back, msg, mine = pl.pallas_call(
+    act, far, near, kept = pl.pallas_call(
         forward_kernel,
-        out_shape=[vmem(nodes, half), vmem(2 * nodes, feat), vmem(nodes + feat, half), vmem(nodes, total)],
+        out_shape=[
+            vmem(nodes, half),
+            vmem(3 * nodes, feat),
+            vmem(nodes + nodes // 2, feat),
+            vmem(nodes, feat, dtype=F32),
+        ],
         in_specs=[pl.BlockSpec(memory_space=pltpu.VMEM)] * 5,
         out_specs=[pl.BlockSpec(memory_space=pltpu.VMEM)] * 4,
         scratch_shapes=[vmem(2 * nodes, total), vmem(total, feat)],
     )(
         *(
             pltpu.with_memory_space_constraint(x, pltpu.VMEM)
-            for x in (own, give, held, here, there)
+            for x in (own, give, features, here, there)
         )
     )
-    ms = [fetch(msg, off) for off in ACROSS]
-    ss = [swap(m) for m in ms]
+    far_, near_ = fetch(far, *ACROSS), fetch(near, (1, 0))
+    (packed,) = vmem_call(pack_back_kernel, [vmem(2 * nodes + nodes // 2, feat)], far_, near_)
+    packed = swap(packed)
     scale = 1.0 / math.sqrt(total)
     grad_input, grad_weight, activation = pl.pallas_call(
         lambda *refs: backward_kernel(scale, *refs),
@@ -273,13 +313,12 @@
             jax.ShapeDtypeStruct((feat, half), F32),
             jax.ShapeDtypeStruct((nodes, half), BF16),
         ],
-        in_specs=[pl.BlockSpec(memory_space=pltpu.VMEM)] * 10,
+        in_specs=[pl.BlockSpec(memory_space=pltpu.VMEM)] * 6,
         out_specs=[pl.BlockSpec(memory_space=pltpu.VMEM)] * 3,
-        scratch_shapes=[vmem(total, feat)],
     )(
         *(
             pltpu.with_memory_space_constraint(x, pltpu.VMEM)
-            for x in (mine, back, msg, *ms, *ss, act)
+            for x in (kept, far, far_, near_, packed, act)
         )
     )
     return activation, grad_input, grad_weight

time: 27.1 us -> 25.8 us (0.952)
  starting transfers between devices: 12.5 us -> 10.2 us
  local copies, waits for them, and re-layouts: 0.14 us -> 0.9 us
    ppermute x7 -> x6, starting transfers between devices: 11.9 us -> 10.1 us  [fetch(): return lax.ppermute(value, CORES, pairs)]
    unnamed x3 -> x10, local copies, waits for them, and re-layouts: 0.01 us -> 0.88 us
    ppermute x7 -> x6, waiting for transfers between devices: 8.19 us -> 8.85 us  [fetch(): return lax.ppermute(value, CORES, pairs)]
    ppermute x4 -> x2, waiting for transfers between devices: 2.51 us -> 2.05 us  [swap(): return lax.ppermute(value, 'sub', [(0, 1), (1, 0)])]
    ppermute x4 -> x2, starting transfers between devices: 0.58 us -> 0.14 us  [swap(): return lax.ppermute(value, 'sub', [(0, 1), (1, 0)])]
  transfers between devices with their start and end apart: 11 -> 8, of which waited for: 7 -> 5; matrix products, arithmetic and copies ran while one was open for 0% -> 0% of each run, Pallas kernels for 0% -> 0%
where the time goes in v4:
time: 25.8 us; the launch traced here: 25.6 us
  waiting for transfers between devices  10.9 us (42%)
  starting transfers between devices  10.2 us (40%)
  Pallas kernels  2.77 us (11%)
  local copies, waits for them, and re-layouts  0.9 us (3%)
  between operations  0.75 us (3%)
    ppermute x6, starting transfers between devices, fetch(): return lax.ppermute(value, CORES, pairs)  10.1 us
    ppermute x6, waiting for transfers between devices, fetch(): return lax.ppermute(value, CORES, pairs)  8.85 us
    ppermute x2, waiting for transfers between devices, swap(): return lax.ppermute(value, 'sub', [(0, 1), (1, 0)])  2.05 us
    pallas_call x1, Pallas kernels, direct(): pl.pallas_call(forward_kernel, out_shape=[vmem(nodes, half), vmem(3 * nod...  1.09 us
    pallas_call x1, Pallas kernels, load(): pl.pallas_call(load_kernel, out_shape=outs, in_specs=[pl.BlockSpec(memory...  0.95 us
    unnamed x10, local copies, waits for them, and re-layouts  0.88 us
    pallas_call x1, Pallas kernels, direct(): pl.pallas_call(lambda *refs: backward_kernel(scale, *refs), out_shape=[ja...  0.68 us
  transfers between devices with their start and end apart: 8, of which 5 were waited for; matrix products, arithmetic and copies ran while one was open for 0% of the time, Pallas kernels for 0%

profile of v4, /device:TPU:0, one launch (start us, length us, event | category | flops | bytes accessed | tf_op | source)
XLA Modules:
  0.0 25.6 jit_solution(2078884004835843189)
XLA Ops:
  0.6 1.0 %shard_map.85 = (bf16[128,4,128]{2,1,0:T(4,128)(2,1)S(1)}, bf16[64,128]{1,0:T(8,128)(2,1)S(1)}, bf16[128,128]{1,0:T(8,128)(2,1)S(1)}, s32[2,1,4]{2,1,0:T(1,128)S(1)}) custom-call(bf16[256,4,128]{2,1,0:T(4,128)(2,1)} %a.1, bf16[128,128]{1,0:T(8,128)(2,1)} %x.5, bf16[128,128]{1,0:T(8,128)(2,1)} %g.1, s32[2,1,4]{2,1,0:T(1,128)} %bitcast.16), custom_call_target="tpu_custom_call" | custom-call | tf_op jit(solution)/shard_map/pallas_call | solution.py:129
  1.6 0.0 copy-start
  1.7 0.0 copy-start.1
  1.7 0.0 copy-start.2
  1.7 3.0 %collective-permute-start = (bf16[720,128]{1,0:T(8,128)(2,1)S(1)}, bf16[720,128]{1,0:T(8,128)(2,1)S(1)}, u32[]{:S(2)}, u32[]{:S(2)}) collective-permute-start(bf16[720,128]{1,0:T(8,128)(2,1)S(1)} %fusion.1.give), channel_id=1, source_target_pairs={{0,2},{1,3},{2,0},{3,1},{4,6},{5,7},{6,4},{7,5},{8,10},{9,11},{10,... | collective-permute-start | bytes 552968 | tf_op jit(solution)/shard_map/ppermute | solution.py:89
  4.7 0.0 copy-done
  4.7 3.7 %collective-permute-start.1 = (bf16[128,128]{1,0:T(8,128)(2,1)S(1)}, bf16[128,128]{1,0:T(8,128)(2,1)S(1)}, u32[]{:S(2)}, u32[]{:S(2)}) collective-permute-start(bf16[128,128]{1,0:T(8,128)(2,1)S(1)} %copy-done), channel_id=1, source_target_pairs={{0,14},{1,13},{2,12},{3,15},{4,10},{5,9},{6,8},{7,11},{8,6},{9,5},... | collective-permute-start | bytes 98312 | tf_op jit(solution)/shard_map/ppermute | solution.py:89
  8.4 0.0 collective-permute-start.3
  8.4 0.8 %collective-permute-start.2 = (bf16[128,128]{1,0:T(8,128)(2,1)S(1)}, bf16[128,128]{1,0:T(8,128)(2,1)S(1)}, u32[]{:S(2)}, u32[]{:S(2)}) collective-permute-start(bf16[128,128]{1,0:T(8,128)(2,1)S(1)} %copy-done), channel_id=1, source_target_pairs={{0,4},{1,7},{2,6},{3,5},{4,0},{5,3},{6,2},{7,1},{8,12},{9,15},{10,... | collective-permute-start | bytes 98312 | tf_op jit(solution)/shard_map/ppermute | solution.py:89
  9.2 2.5 %collective-permute-done.1.refs_1_ = bf16[128,128]{1,0:T(8,128)(2,1)S(1)} collective-permute-done((bf16[128,128]{1,0:T(8,128)(2,1)S(1)}, bf16[128,128]{1,0:T(8,128)(2,1)S(1)}, u32[]{:S(2)}, u32[]{:S(2)}) %collective-permute-start.1) | collective-permute-done | bytes 32800 | tf_op jit(solution)/shard_map/ppermute | solution.py:89
  11.7 1.5 %collective-permute-done.3.refs_3_ = bf16[128,128]{1,0:T(8,128)(2,1)S(1)} collective-permute-done((bf16[128,128]{1,0:T(8,128)(2,1)S(1)}, bf16[128,128]{1,0:T(8,128)(2,1)S(1)}, u32[]{:S(2)}, u32[]{:S(2)}) %collective-permute-start.3) | collective-permute-done | bytes 32800 | tf_op jit(solution)/shard_map/ppermute | solution.py:89
  13.2 0.0 collective-permute-done.2.refs_2_
  13.2 0.0 collective-permute-done.refs_0_
  13.2 0.0 copy-done.1
  13.2 0.0 copy-done.2
  13.2 0.0 copy-start.3
  13.3 0.1 collective-permute-start.4
  13.3 0.8 %copy-done.3 = bf16[256,4,128]{2,1,0:T(4,128)(2,1)S(1)} copy-done((bf16[256,4,128]{2,1,0:T(4,128)(2,1)S(1)}, bf16[256,4,128]{2,1,0:T(4,128)(2,1)}, u32[]{:S(2)}) %copy-start.3) | copy-done | bytes 262168
  14.2 0.8 %collective-permute-done.4.there = bf16[1376,128]{1,0:T(8,128)(2,1)S(1)} collective-permute-done((bf16[1376,128]{1,0:T(8,128)(2,1)S(1)}, bf16[1376,128]{1,0:T(8,128)(2,1)S(1)}, u32[]{:S(2)}, u32[]{:S(2)}) %collective-permute-start.4) | collective-permute-done | bytes 352288 | tf_op jit(solution)/shard_map/ppermute | solution.py:93
  15.0 1.1 %shard_map.87 = (bf16[128,128]{1,0:T(8,128)(2,1)S(1)}, bf16[384,128]{1,0:T(8,128)(2,1)S(1)}, bf16[192,128]{1,0:T(8,128)(2,1)S(1)}, f32[128,128]{1,0:T(8,128)S(1)}) custom-call(bf16[4,256,128]{2,1,0:T(8,128)(2,1)S(1)} %bitcast.12, bf16[720,128]{1,0:T(8,128)(2,1)S(1)} %fusion.1.give, bf16[128,128]{1,0:T(8,128)(2,1)S(1)} %copy-done, ...), custom_call_target="tpu_custom_call" | custom-call | tf_op jit(solution)/shard_map/pallas_call | solution.py:288
  16.1 1.8 %collective-permute-start.5 = (bf16[384,128]{1,0:T(8,128)(2,1)S(1)}, bf16[384,128]{1,0:T(8,128)(2,1)S(1)}, u32[]{:S(2)}, u32[]{:S(2)}) collective-permute-start(bf16[384,128]{1,0:T(8,128)(2,1)S(1)} %get-tuple-element.23.refs_1_), channel_id=1, source_target_pairs={{0,12},{1,9},{2,14},{3,11},{4,8},{5,13},{6,10},{7,15},{8,4},{9,1},... | collective-permute-start | bytes 294920 | tf_op jit(solution)/shard_map/ppermute | solution.py:89
  17.9 0.8 %collective-permute-start.6 = (bf16[192,128]{1,0:T(8,128)(2,1)S(1)}, bf16[192,128]{1,0:T(8,128)(2,1)S(1)}, u32[]{:S(2)}, u32[]{:S(2)}) collective-permute-start(bf16[192,128]{1,0:T(8,128)(2,1)S(1)} %get-tuple-element.24), channel_id=1, source_target_pairs={{0,4},{1,5},{2,6},{3,7},{4,0},{5,1},{6,2},{7,3},{8,12},{9,13},{10,... | collective-permute-start | bytes 147464 | tf_op jit(solution)/shard_map/ppermute | solution.py:89
  18.7 4.8 %collective-permute-done.6.near.refs_3_ = bf16[192,128]{1,0:T(8,128)(2,1)S(1)} collective-permute-done((bf16[192,128]{1,0:T(8,128)(2,1)S(1)}, bf16[192,128]{1,0:T(8,128)(2,1)S(1)}, u32[]{:S(2)}, u32[]{:S(2)}) %collective-permute-start.6) | collective-permute-done | bytes 49184 | tf_op jit(solution)/shard_map/ppermute | solution.py:89
  23.6 0.0 collective-permute-done.5.far.refs_2_
  23.6 0.1 collective-permute-start.7
  23.6 1.3 %collective-permute-done.7.refs_4_ = bf16[320,128]{1,0:T(8,128)(2,1)S(1)} collective-permute-done((bf16[320,128]{1,0:T(8,128)(2,1)S(1)}, bf16[320,128]{1,0:T(8,128)(2,1)S(1)}, u32[]{:S(2)}, u32[]{:S(2)}) %collective-permute-start.7) | collective-permute-done | bytes 81952 | tf_op jit(solution)/shard_map/ppermute | solution.py:93
  24.9 0.7 %shard_map.89 = (bf16[128,128]{1,0:T(8,128)(2,1)}, f32[128,128]{1,0:T(8,128)}, bf16[128,128]{1,0:T(8,128)(2,1)}) custom-call(f32[128,128]{1,0:T(8,128)S(1)} %get-tuple-element.22.refs_0_, bf16[384,128]{1,0:T(8,128)(2,1)S(1)} %get-tuple-element.23.refs_1_, bf16[384,128]{1,0:T(8,128)(2,1)S(1)} %collective-permute-done.5.far.refs_2_, ...), custom_call_target="tpu_custom_call" | custom-call | tf_op jit(solution)/shard_map/pallas_call | solution.py:309
  (7 shorter events, 0.1 us)
Async XLA Ops:
  1.6 3.1 %copy-start = (bf16[128,128]{1,0:T(8,128)(2,1)S(1)}, bf16[128,128]{1,0:T(8,128)(2,1)}, u32[]{:S(2)}) copy-start(bf16[128,128]{1,0:T(8,128)(2,1)} %x.5) | copy-start | bytes 98308
  1.7 11.5 %copy-start.1 = (bf16[128,128]{1,0:T(8,128)(2,1)S(1)}, bf16[128,128]{1,0:T(8,128)(2,1)}, u32[]{:S(2)}) copy-start(bf16[128,128]{1,0:T(8,128)(2,1)} %refs_4_.1) | copy-start | bytes 98308
  1.7 11.5 %copy-start.2 = (f32[128]{0:T(128)S(1)}, f32[128]{0:T(128)}, u32[]{:S(2)}) copy-start(f32[128]{0:T(128)} %param.10) | copy-start | bytes 1540
  1.7 11.5 %collective-permute-start = (bf16[720,128]{1,0:T(8,128)(2,1)S(1)}, bf16[720,128]{1,0:T(8,128)(2,1)S(1)}, u32[]{:S(2)}, u32[]{:S(2)}) collective-permute-start(bf16[720,128]{1,0:T(8,128)(2,1)S(1)} %fusion.1.give), channel_id=1, source_target_pairs={{0,2},{1,3},{2,0},{3,1},{4,6},{5,7},{6,4},{7,5},{8,10},{9,11},{10,... | collective-permute-start | bytes 552968 | tf_op jit(solution)/shard_map/ppermute | solution.py:89
  4.7 7.0 %collective-permute-start.1 = (bf16[128,128]{1,0:T(8,128)(2,1)S(1)}, bf16[128,128]{1,0:T(8,128)(2,1)S(1)}, u32[]{:S(2)}, u32[]{:S(2)}) collective-permute-start(bf16[128,128]{1,0:T(8,128)(2,1)S(1)} %copy-done), channel_id=1, source_target_pairs={{0,14},{1,13},{2,12},{3,15},{4,10},{5,9},{6,8},{7,11},{8,6},{9,5},... | collective-permute-start | bytes 98312 | tf_op jit(solution)/shard_map/ppermute | solution.py:89
  8.4 4.8 %collective-permute-start.3 = (bf16[128,128]{1,0:T(8,128)(2,1)S(1)}, bf16[128,128]{1,0:T(8,128)(2,1)S(1)}, u32[]{:S(2)}, u32[]{:S(2)}) collective-permute-start(bf16[128,128]{1,0:T(8,128)(2,1)S(1)} %copy-done), channel_id=1, source_target_pairs={{0,8},{1,11},{2,10},{3,9},{4,12},{5,15},{6,14},{7,13},{8,0},{9,3},... | collective-permute-start | bytes 98312 | tf_op jit(solution)/shard_map/ppermute | solution.py:89
  8.4 4.8 %collective-permute-start.2 = (bf16[128,128]{1,0:T(8,128)(2,1)S(1)}, bf16[128,128]{1,0:T(8,128)(2,1)S(1)}, u32[]{:S(2)}, u32[]{:S(2)}) collective-permute-start(bf16[128,128]{1,0:T(8,128)(2,1)S(1)} %copy-done), channel_id=1, source_target_pairs={{0,4},{1,7},{2,6},{3,5},{4,0},{5,3},{6,2},{7,1},{8,12},{9,15},{10,... | collective-permute-start | bytes 98312 | tf_op jit(solution)/shard_map/ppermute | solution.py:89
  13.2 1.0 %copy-start.3 = (bf16[256,4,128]{2,1,0:T(4,128)(2,1)S(1)}, bf16[256,4,128]{2,1,0:T(4,128)(2,1)}, u32[]{:S(2)}) copy-start(bf16[256,4,128]{2,1,0:T(4,128)(2,1)} %a.1) | copy-start | bytes 786436
  13.3 1.7 %collective-permute-start.4 = (bf16[1376,128]{1,0:T(8,128)(2,1)S(1)}, bf16[1376,128]{1,0:T(8,128)(2,1)S(1)}, u32[]{:S(2)}, u32[]{:S(2)}) collective-permute-start(bf16[1376,128]{1,0:T(8,128)(2,1)S(1)} %shard_map.86.here), channel_id=1, source_target_pairs={{0,1},{1,0},{2,3},{3,2},{4,5},{5,4},{6,7},{7,6},{8,9},{9,8},{10,11... | collective-permute-start | bytes 1056776 | tf_op jit(solution)/shard_map/ppermute | solution.py:93
  16.1 7.5 %collective-permute-start.5 = (bf16[384,128]{1,0:T(8,128)(2,1)S(1)}, bf16[384,128]{1,0:T(8,128)(2,1)S(1)}, u32[]{:S(2)}, u32[]{:S(2)}) collective-permute-start(bf16[384,128]{1,0:T(8,128)(2,1)S(1)} %get-tuple-element.23.refs_1_), channel_id=1, source_target_pairs={{0,12},{1,9},{2,14},{3,11},{4,8},{5,13},{6,10},{7,15},{8,4},{9,1},... | collective-permute-start | bytes 294920 | tf_op jit(solution)/shard_map/ppermute | solution.py:89
  17.9 5.7 %collective-permute-start.6 = (bf16[192,128]{1,0:T(8,128)(2,1)S(1)}, bf16[192,128]{1,0:T(8,128)(2,1)S(1)}, u32[]{:S(2)}, u32[]{:S(2)}) collective-permute-start(bf16[192,128]{1,0:T(8,128)(2,1)S(1)} %get-tuple-element.24), channel_id=1, source_target_pairs={{0,4},{1,5},{2,6},{3,7},{4,0},{5,1},{6,2},{7,3},{8,12},{9,13},{10,... | collective-permute-start | bytes 147464 | tf_op jit(solution)/shard_map/ppermute | solution.py:89
  23.6 1.3 %collective-permute-start.7 = (bf16[320,128]{1,0:T(8,128)(2,1)S(1)}, bf16[320,128]{1,0:T(8,128)(2,1)S(1)}, u32[]{:S(2)}, u32[]{:S(2)}) collective-permute-start(bf16[320,128]{1,0:T(8,128)(2,1)S(1)} %shard_map.88), channel_id=1, source_target_pairs={{0,1},{1,0},{2,3},{3,2},{4,5},{5,4},{6,7},{7,6},{8,9},{9,8},{10,11... | collective-permute-start | bytes 245768 | tf_op jit(solution)/shard_map/ppermute | solution.py:93

commit v5 on v4

--- a/solution.py
+++ b/solution.py
@@ -158,13 +158,16 @@
         out[at : at + ref.shape[0]] = ref[...]
         at += ref.shape[0]
     rest = row[...]
+    tail = jnp.zeros((out.shape[0] - at, rest.shape[1]), F32)
+    line = lax.broadcasted_iota(jnp.int32, tail.shape, 0)
     for i in range(3):
-        part = rest.astype(BF16)
-        out[at + i : at + i + 1] = part
-        rest = rest - part.astype(F32)
-
-
-def forward_kernel(own, give, x, here, there, act, far, near, kept, rows, xs):
+        part = rest.astype(BF16).astype(F32)
+        tail = jnp.where(line == i, part, tail)
+        rest = rest - part
+    out[at:] = tail.astype(BF16)
+
+
+def forward_kernel(own, give, x, p, q, here, there, act, far, near, kept, rows, xs):
     n = x.shape[0]
     sections = own.shape[0]
     d, r, c = (lax.axis_index(a) for a in CORES)
@@ -175,8 +178,8 @@
     low, high = (sections + 1) * n, (sections + 1) * n + n // 2
     end = give.shape[0]
     flags = mask_rows(give[high:end], 2, sections)
-    flags_ = mask_rows(here[high:end], 2, sections)
-    first, second = in_order(here[...], there[...])
+    flags_ = mask_rows(p[high:end], 2, sections)
+    first, second = in_order(p[:end], q[:end])
     for s in range(sections):
         for k, part in enumerate((first, second)):
             at = slice(k * n, (k + 1) * n)
@@ -185,18 +188,19 @@
             rows[at, columns(s, 1 - r)] = part[s * n : (s + 1) * n] * flags_[entry]
     xs[columns(d, r), :] = x[...]
     xs[columns(d, 1 - r), :] = jnp.concatenate([first[low:high], second[low:high]], axis=0)
+    sides = in_order(here[...], there[...])
     for i, pair in enumerate(SHARED):
-        for (dx, rx), part in zip(pair, (first, second)):
-            xs[columns(d ^ dx, r ^ rx), :] = part[end + i * n : end + (i + 1) * n]
-    end += len(SHARED) * n
+        for (dx, rx), part in zip(pair, sides):
+            xs[columns(d ^ dx, r ^ rx), :] = part[i * n : (i + 1) * n]
+    end = len(SHARED) * n
 
     weight, ours = (
-        jnp.concatenate([part[k : k + n] for part in (first, second)], axis=1)
+        jnp.concatenate([part[k : k + n] for part in sides], axis=1)
         for k in (end, end + n)
     )
     end += 2 * n
     bias = jnp.concatenate(
-        [jnp.sum(part[end : end + 3].astype(F32), axis=0, keepdims=True) for part in (first, second)],
+        [jnp.sum(part[end : end + 3].astype(F32), axis=0, keepdims=True) for part in sides],
         axis=1,
     )
     theirs = jnp.concatenate([part[sections * n : low] for part in (first, second)], axis=1)
@@ -265,9 +269,6 @@
     sections, width = adjacency.shape[1:]
     total = sections * 2 * width
     half = weight.shape[1]
-    c = lax.axis_index("sub")
-
-
     x0 = fetch(features, *SHARED[0])
     x2 = fetch(features, *SHARED[2])
     give, few, grads, flat = load(adjacency, features, cotangent, mask.transpose(0, 2, 1))
@@ -282,7 +283,8 @@
     x1 = fetch(late, *SHARED[1])
     taken = fetch(give, (0, 1))
     xs = [x0, x1, x2]
-    parts = (taken, *xs, weight, grads, bias[None, :])
+    q = swap(taken)
+    parts = (*xs, weight, grads, bias[None, :])
     (here,) = vmem_call(pack_kernel, [vmem(sum(x.shape[0] for x in parts) + 15, width)], *parts)
     there = swap(here)
     act, far, near, kept = pl.pallas_call(
@@ -293,13 +295,13 @@
             vmem(nodes + nodes // 2, feat),
             vmem(nodes, feat, dtype=F32),
         ],
-        in_specs=[pl.BlockSpec(memory_space=pltpu.VMEM)] * 5,
+        in_specs=[pl.BlockSpec(memory_space=pltpu.VMEM)] * 7,
         out_specs=[pl.BlockSpec(memory_space=pltpu.VMEM)] * 4,
         scratch_shapes=[vmem(2 * nodes, total), vmem(total, feat)],
     )(
         *(
             pltpu.with_memory_space_constraint(x, pltpu.VMEM)
-            for x in (own, give, features, here, there)
+            for x in (own, give, features, taken, q, here, there)
         )
     )
     far_, near_ = fetch(far, *ACROSS), fetch(near, (1, 0))

time: 25.8 us -> 25.5 us (0.988)
  local copies, waits for them, and re-layouts: 0.9 us -> 0.09 us
  waiting for transfers between devices: 10.9 us -> 11.4 us
    unnamed x10, local copies, waits for them, and re-layouts: 0.88 us -> 0.07 us
    ppermute x2 -> x3, waiting for transfers between devices: 2.05 us -> 2.6 us  [swap(): return lax.ppermute(value, 'sub', [(0, 1), (1, 0)])]
  transfers between devices with their start and end apart: 8 -> 9, of which waited for: 5 -> 6; matrix products, arithmetic and copies ran while one was open for 0% -> 0% of each run, Pallas kernels for 0% -> 0%
where the time goes in v5:
time: 25.5 us; the launch traced here: 25.3 us
  waiting for transfers between devices  11.4 us (45%)
  starting transfers between devices  10.2 us (40%)
  Pallas kernels  2.76 us (11%)
  between operations  0.76 us (3%)
    ppermute x6, starting transfers between devices, fetch(): return lax.ppermute(value, CORES, pairs)  10.1 us
    ppermute x6, waiting for transfers between devices, fetch(): return lax.ppermute(value, CORES, pairs)  8.85 us
    ppermute x3, waiting for transfers between devices, swap(): return lax.ppermute(value, 'sub', [(0, 1), (1, 0)])  2.6 us
    pallas_call x1, Pallas kernels, direct(): pl.pallas_call(forward_kernel, out_shape=[vmem(nodes, half), vmem(3 * nod...  1.09 us
    pallas_call x1, Pallas kernels, load(): pl.pallas_call(load_kernel, out_shape=outs, in_specs=[pl.BlockSpec(memory...  0.95 us
    pallas_call x1, Pallas kernels, direct(): pl.pallas_call(lambda *refs: backward_kernel(scale, *refs), out_shape=[ja...  0.68 us
  transfers between devices with their start and end apart: 9, of which 6 were waited for; matrix products, arithmetic and copies ran while one was open for 0% of the time, Pallas kernels for 0%

profile of v5, /device:TPU:0, one launch (start us, length us, event | category | flops | bytes accessed | tf_op | source)
XLA Modules:
  0.0 25.3 jit_solution(14244070776386123189)
XLA Ops:
  0.6 1.0 %shard_map.85 = (bf16[128,4,128]{2,1,0:T(4,128)(2,1)S(1)}, bf16[64,128]{1,0:T(8,128)(2,1)S(1)}, bf16[128,128]{1,0:T(8,128)(2,1)S(1)}, s32[2,1,4]{2,1,0:T(1,128)S(1)}) custom-call(bf16[256,4,128]{2,1,0:T(4,128)(2,1)} %a.1, bf16[128,128]{1,0:T(8,128)(2,1)} %x.5, bf16[128,128]{1,0:T(8,128)(2,1)} %g.1, s32[2,1,4]{2,1,0:T(1,128)} %bitcast.16), custom_call_target="tpu_custom_call" | custom-call | tf_op jit(solution)/shard_map/pallas_call | solution.py:129
  1.6 0.0 copy-start
  1.7 0.0 copy-start.1
  1.7 0.0 copy-start.3
  1.7 0.0 copy-start.2
  1.7 3.0 %collective-permute-start = (bf16[720,128]{1,0:T(8,128)(2,1)S(1)}, bf16[720,128]{1,0:T(8,128)(2,1)S(1)}, u32[]{:S(2)}, u32[]{:S(2)}) collective-permute-start(bf16[720,128]{1,0:T(8,128)(2,1)S(1)} %fusion.1.give), channel_id=1, source_target_pairs={{0,2},{1,3},{2,0},{3,1},{4,6},{5,7},{6,4},{7,5},{8,10},{9,11},{10,... | collective-permute-start | bytes 552968 | tf_op jit(solution)/shard_map/ppermute | solution.py:89
  4.7 0.0 copy-done
  4.7 3.7 %collective-permute-start.2 = (bf16[128,128]{1,0:T(8,128)(2,1)S(1)}, bf16[128,128]{1,0:T(8,128)(2,1)S(1)}, u32[]{:S(2)}, u32[]{:S(2)}) collective-permute-start(bf16[128,128]{1,0:T(8,128)(2,1)S(1)} %copy-done), channel_id=1, source_target_pairs={{0,14},{1,13},{2,12},{3,15},{4,10},{5,9},{6,8},{7,11},{8,6},{9,5},... | collective-permute-start | bytes 98312 | tf_op jit(solution)/shard_map/ppermute | solution.py:89
  8.4 0.0 collective-permute-start.4
  8.4 0.8 %collective-permute-start.3 = (bf16[128,128]{1,0:T(8,128)(2,1)S(1)}, bf16[128,128]{1,0:T(8,128)(2,1)S(1)}, u32[]{:S(2)}, u32[]{:S(2)}) collective-permute-start(bf16[128,128]{1,0:T(8,128)(2,1)S(1)} %copy-done), channel_id=1, source_target_pairs={{0,4},{1,7},{2,6},{3,5},{4,0},{5,3},{6,2},{7,1},{8,12},{9,15},{10,... | collective-permute-start | bytes 98312 | tf_op jit(solution)/shard_map/ppermute | solution.py:89
  9.2 0.2 collective-permute-done.p
  9.4 0.0 collective-permute-start.1
  9.4 2.3 %collective-permute-done.2.refs_0_ = bf16[128,128]{1,0:T(8,128)(2,1)S(1)} collective-permute-done((bf16[128,128]{1,0:T(8,128)(2,1)S(1)}, bf16[128,128]{1,0:T(8,128)(2,1)S(1)}, u32[]{:S(2)}, u32[]{:S(2)}) %collective-permute-start.2) | collective-permute-done | bytes 32800 | tf_op jit(solution)/shard_map/ppermute | solution.py:89
  11.7 1.5 %collective-permute-done.4.refs_2_ = bf16[128,128]{1,0:T(8,128)(2,1)S(1)} collective-permute-done((bf16[128,128]{1,0:T(8,128)(2,1)S(1)}, bf16[128,128]{1,0:T(8,128)(2,1)S(1)}, u32[]{:S(2)}, u32[]{:S(2)}) %collective-permute-start.4) | collective-permute-done | bytes 32800 | tf_op jit(solution)/shard_map/ppermute | solution.py:89
  13.2 0.0 collective-permute-done.3.refs_1_
  13.2 0.0 copy-done.1
  13.2 0.0 copy-done.2
  13.2 0.1 collective-permute-start.5
  13.3 0.0 copy-done.3
  13.4 1.3 %collective-permute-done.5.there = bf16[656,128]{1,0:T(8,128)(2,1)S(1)} collective-permute-done((bf16[656,128]{1,0:T(8,128)(2,1)S(1)}, bf16[656,128]{1,0:T(8,128)(2,1)S(1)}, u32[]{:S(2)}, u32[]{:S(2)}) %collective-permute-start.5) | collective-permute-done | bytes 167968 | tf_op jit(solution)/shard_map/ppermute | solution.py:93
  14.7 0.0 collective-permute-done.1.q
  14.7 1.1 %shard_map.87 = (bf16[128,128]{1,0:T(8,128)(2,1)S(1)}, bf16[384,128]{1,0:T(8,128)(2,1)S(1)}, bf16[192,128]{1,0:T(8,128)(2,1)S(1)}, f32[128,128]{1,0:T(8,128)S(1)}) custom-call(bf16[4,256,128]{2,1,0:T(8,128)(2,1)S(1)} %bitcast.12, bf16[720,128]{1,0:T(8,128)(2,1)S(1)} %fusion.1.give, bf16[128,128]{1,0:T(8,128)(2,1)S(1)} %copy-done, ...), custom_call_target="tpu_custom_call" | custom-call | tf_op jit(solution)/shard_map/pallas_call | solution.py:290
  15.8 1.8 %collective-permute-start.6 = (bf16[384,128]{1,0:T(8,128)(2,1)S(1)}, bf16[384,128]{1,0:T(8,128)(2,1)S(1)}, u32[]{:S(2)}, u32[]{:S(2)}) collective-permute-start(bf16[384,128]{1,0:T(8,128)(2,1)S(1)} %get-tuple-element.23.refs_1_), channel_id=1, source_target_pairs={{0,12},{1,9},{2,14},{3,11},{4,8},{5,13},{6,10},{7,15},{8,4},{9,1},... | collective-permute-start | bytes 294920 | tf_op jit(solution)/shard_map/ppermute | solution.py:89
  17.6 0.8 %collective-permute-start.7 = (bf16[192,128]{1,0:T(8,128)(2,1)S(1)}, bf16[192,128]{1,0:T(8,128)(2,1)S(1)}, u32[]{:S(2)}, u32[]{:S(2)}) collective-permute-start(bf16[192,128]{1,0:T(8,128)(2,1)S(1)} %get-tuple-element.24), channel_id=1, source_target_pairs={{0,4},{1,5},{2,6},{3,7},{4,0},{5,1},{6,2},{7,3},{8,12},{9,13},{10,... | collective-permute-start | bytes 147464 | tf_op jit(solution)/shard_map/ppermute | solution.py:89
  18.4 4.8 %collective-permute-done.7.near.refs_3_ = bf16[192,128]{1,0:T(8,128)(2,1)S(1)} collective-permute-done((bf16[192,128]{1,0:T(8,128)(2,1)S(1)}, bf16[192,128]{1,0:T(8,128)(2,1)S(1)}, u32[]{:S(2)}, u32[]{:S(2)}) %collective-permute-start.7) | collective-permute-done | bytes 49184 | tf_op jit(solution)/shard_map/ppermute | solution.py:89
  23.3 0.0 collective-permute-done.6.far.refs_2_
  23.3 0.1 collective-permute-start.8
  23.4 1.3 %collective-permute-done.8.refs_4_ = bf16[320,128]{1,0:T(8,128)(2,1)S(1)} collective-permute-done((bf16[320,128]{1,0:T(8,128)(2,1)S(1)}, bf16[320,128]{1,0:T(8,128)(2,1)S(1)}, u32[]{:S(2)}, u32[]{:S(2)}) %collective-permute-start.8) | collective-permute-done | bytes 81952 | tf_op jit(solution)/shard_map/ppermute | solution.py:93
  24.6 0.7 %shard_map.89 = (bf16[128,128]{1,0:T(8,128)(2,1)}, f32[128,128]{1,0:T(8,128)}, bf16[128,128]{1,0:T(8,128)(2,1)}) custom-call(f32[128,128]{1,0:T(8,128)S(1)} %get-tuple-element.22.refs_0_, bf16[384,128]{1,0:T(8,128)(2,1)S(1)} %get-tuple-element.23.refs_1_, bf16[384,128]{1,0:T(8,128)(2,1)S(1)} %collective-permute-done.6.far.refs_2_, ...), custom_call_target="tpu_custom_call" | custom-call | tf_op jit(solution)/shard_map/pallas_call | solution.py:311
  (7 shorter events, 0.1 us)
Async XLA Ops:
  1.6 3.1 %copy-start = (bf16[128,128]{1,0:T(8,128)(2,1)S(1)}, bf16[128,128]{1,0:T(8,128)(2,1)}, u32[]{:S(2)}) copy-start(bf16[128,128]{1,0:T(8,128)(2,1)} %x.5) | copy-start | bytes 98308
  1.7 11.5 %copy-start.1 = (bf16[128,128]{1,0:T(8,128)(2,1)S(1)}, bf16[128,128]{1,0:T(8,128)(2,1)}, u32[]{:S(2)}) copy-start(bf16[128,128]{1,0:T(8,128)(2,1)} %refs_3_.1) | copy-start | bytes 98308
  1.7 11.6 %copy-start.3 = (bf16[256,4,128]{2,1,0:T(4,128)(2,1)S(1)}, bf16[256,4,128]{2,1,0:T(4,128)(2,1)}, u32[]{:S(2)}) copy-start(bf16[256,4,128]{2,1,0:T(4,128)(2,1)} %a.1) | copy-start | bytes 786436
  1.7 11.5 %copy-start.2 = (f32[128]{0:T(128)S(1)}, f32[128]{0:T(128)}, u32[]{:S(2)}) copy-start(f32[128]{0:T(128)} %param.10) | copy-start | bytes 1540
  1.7 7.6 %collective-permute-start = (bf16[720,128]{1,0:T(8,128)(2,1)S(1)}, bf16[720,128]{1,0:T(8,128)(2,1)S(1)}, u32[]{:S(2)}, u32[]{:S(2)}) collective-permute-start(bf16[720,128]{1,0:T(8,128)(2,1)S(1)} %fusion.1.give), channel_id=1, source_target_pairs={{0,2},{1,3},{2,0},{3,1},{4,6},{5,7},{6,4},{7,5},{8,10},{9,11},{10,... | collective-permute-start | bytes 552968 | tf_op jit(solution)/shard_map/ppermute | solution.py:89
  4.7 7.0 %collective-permute-start.2 = (bf16[128,128]{1,0:T(8,128)(2,1)S(1)}, bf16[128,128]{1,0:T(8,128)(2,1)S(1)}, u32[]{:S(2)}, u32[]{:S(2)}) collective-permute-start(bf16[128,128]{1,0:T(8,128)(2,1)S(1)} %copy-done), channel_id=1, source_target_pairs={{0,14},{1,13},{2,12},{3,15},{4,10},{5,9},{6,8},{7,11},{8,6},{9,5},... | collective-permute-start | bytes 98312 | tf_op jit(solution)/shard_map/ppermute | solution.py:89
  8.4 4.8 %collective-permute-start.4 = (bf16[128,128]{1,0:T(8,128)(2,1)S(1)}, bf16[128,128]{1,0:T(8,128)(2,1)S(1)}, u32[]{:S(2)}, u32[]{:S(2)}) collective-permute-start(bf16[128,128]{1,0:T(8,128)(2,1)S(1)} %copy-done), channel_id=1, source_target_pairs={{0,8},{1,11},{2,10},{3,9},{4,12},{5,15},{6,14},{7,13},{8,0},{9,3},... | collective-permute-start | bytes 98312 | tf_op jit(solution)/shard_map/ppermute | solution.py:89
  8.4 4.8 %collective-permute-start.3 = (bf16[128,128]{1,0:T(8,128)(2,1)S(1)}, bf16[128,128]{1,0:T(8,128)(2,1)S(1)}, u32[]{:S(2)}, u32[]{:S(2)}) collective-permute-start(bf16[128,128]{1,0:T(8,128)(2,1)S(1)} %copy-done), channel_id=1, source_target_pairs={{0,4},{1,7},{2,6},{3,5},{4,0},{5,3},{6,2},{7,1},{8,12},{9,15},{10,... | collective-permute-start | bytes 98312 | tf_op jit(solution)/shard_map/ppermute | solution.py:89
  9.4 5.3 %collective-permute-start.1 = (bf16[720,128]{1,0:T(8,128)(2,1)S(1)}, bf16[720,128]{1,0:T(8,128)(2,1)S(1)}, u32[]{:S(2)}, u32[]{:S(2)}) collective-permute-start(bf16[720,128]{1,0:T(8,128)(2,1)S(1)} %collective-permute-done.p), channel_id=1, source_target_pairs={{0,1},{1,0},{2,3},{3,2},{4,5},{5,4},{6,7},{7,6},{8,9},{9,8},{10,11... | collective-permute-start | bytes 552968 | tf_op jit(solution)/shard_map/ppermute | solution.py:93
  13.2 1.5 %collective-permute-start.5 = (bf16[656,128]{1,0:T(8,128)(2,1)S(1)}, bf16[656,128]{1,0:T(8,128)(2,1)S(1)}, u32[]{:S(2)}, u32[]{:S(2)}) collective-permute-start(bf16[656,128]{1,0:T(8,128)(2,1)S(1)} %shard_map.86.here), channel_id=1, source_target_pairs={{0,1},{1,0},{2,3},{3,2},{4,5},{5,4},{6,7},{7,6},{8,9},{9,8},{10,11... | collective-permute-start | bytes 503816 | tf_op jit(solution)/shard_map/ppermute | solution.py:93
  15.8 7.5 %collective-permute-start.6 = (bf16[384,128]{1,0:T(8,128)(2,1)S(1)}, bf16[384,128]{1,0:T(8,128)(2,1)S(1)}, u32[]{:S(2)}, u32[]{:S(2)}) collective-permute-start(bf16[384,128]{1,0:T(8,128)(2,1)S(1)} %get-tuple-element.23.refs_1_), channel_id=1, source_target_pairs={{0,12},{1,9},{2,14},{3,11},{4,8},{5,13},{6,10},{7,15},{8,4},{9,1},... | collective-permute-start | bytes 294920 | tf_op jit(solution)/shard_map/ppermute | solution.py:89
  17.6 5.6 %collective-permute-start.7 = (bf16[192,128]{1,0:T(8,128)(2,1)S(1)}, bf16[192,128]{1,0:T(8,128)(2,1)S(1)}, u32[]{:S(2)}, u32[]{:S(2)}) collective-permute-start(bf16[192,128]{1,0:T(8,128)(2,1)S(1)} %get-tuple-element.24), channel_id=1, source_target_pairs={{0,4},{1,5},{2,6},{3,7},{4,0},{5,1},{6,2},{7,3},{8,12},{9,13},{10,... | collective-permute-start | bytes 147464 | tf_op jit(solution)/shard_map/ppermute | solution.py:89
  23.3 1.3 %collective-permute-start.8 = (bf16[320,128]{1,0:T(8,128)(2,1)S(1)}, bf16[320,128]{1,0:T(8,128)(2,1)S(1)}, u32[]{:S(2)}, u32[]{:S(2)}) collective-permute-start(bf16[320,128]{1,0:T(8,128)(2,1)S(1)} %shard_map.88), channel_id=1, source_target_pairs={{0,1},{1,0},{2,3},{3,2},{4,5},{5,4},{6,7},{7,6},{8,9},{9,8},{10,11... | collective-permute-start | bytes 245768 | tf_op jit(solution)/shard_map/ppermute | solution.py:93

commit v6 on v5

--- a/solution.py
+++ b/solution.py
@@ -75,7 +75,7 @@
     return activation, grad_input, total / math.sqrt(sections * reps * width)
 
 
-SHARED = (((3, 1), (3, 0)), ((1, 0), (1, 1)), ((2, 0), (2, 1)))
+SHARED = (((3, 1), (3, 0)), ((2, 0), (2, 1)), ((1, 0), (1, 1)))
 ACROSS = ((3, 0), (2, 0))
 
 
@@ -167,27 +167,37 @@
     out[at:] = tail.astype(BF16)
 
 
-def forward_kernel(own, give, x, p, q, here, there, act, far, near, kept, rows, xs):
+def block_columns(s, rep, n):
+    return pl.ds(pl.multiple_of((s * 2 + rep) * n, n), n)
+
+
+def rows_kernel(own, give, p, q, rows):
+    sections = own.shape[0]
+    n = own.shape[1] // 2
+    r = lax.axis_index("rep")
+    start, end = (sections + 1) * n + n // 2, give.shape[0]
+    flags = mask_rows(give[start:end], 2, sections)
+    flags_ = mask_rows(p[start:end], 2, sections)
+    for k, part in enumerate(in_order(p[: sections * n], q[: sections * n])):
+        at = slice(k * n, (k + 1) * n)
+        for s in range(sections):
+            entry = slice(k * sections + s, k * sections + s + 1)
+            rows[at, block_columns(s, r, n)] = own[s, at] * flags[entry]
+            rows[at, block_columns(s, 1 - r, n)] = part[s * n : (s + 1) * n] * flags_[entry]
+
+
+def forward_kernel(rows, x, p, q, here, there, act, far, near, kept, xs):
     n = x.shape[0]
-    sections = own.shape[0]
+    sections = xs.shape[0] // (2 * n)
     d, r, c = (lax.axis_index(a) for a in CORES)
 
     def columns(s, rep):
-        return pl.ds(pl.multiple_of((s * 2 + rep) * n, n), n)
-
-    low, high = (sections + 1) * n, (sections + 1) * n + n // 2
-    end = give.shape[0]
-    flags = mask_rows(give[high:end], 2, sections)
-    flags_ = mask_rows(p[high:end], 2, sections)
-    first, second = in_order(p[:end], q[:end])
-    for s in range(sections):
-        for k, part in enumerate((first, second)):
-            at = slice(k * n, (k + 1) * n)
-            entry = slice(k * sections + s, k * sections + s + 1)
-            rows[at, columns(s, r)] = own[s, at] * flags[entry]
-            rows[at, columns(s, 1 - r)] = part[s * n : (s + 1) * n] * flags_[entry]
+        return block_columns(s, rep, n)
+
+    high = (sections + 1) * n + n // 2
+    first, second = in_order(p[sections * n : high], q[sections * n : high])
     xs[columns(d, r), :] = x[...]
-    xs[columns(d, 1 - r), :] = jnp.concatenate([first[low:high], second[low:high]], axis=0)
+    xs[columns(d, 1 - r), :] = jnp.concatenate([first[n:], second[n:]], axis=0)
     sides = in_order(here[...], there[...])
     for i, pair in enumerate(SHARED):
         for (dx, rx), part in zip(pair, sides):
@@ -203,7 +213,7 @@
         [jnp.sum(part[end : end + 3].astype(F32), axis=0, keepdims=True) for part in sides],
         axis=1,
     )
-    theirs = jnp.concatenate([part[sections * n : low] for part in (first, second)], axis=1)
+    theirs = jnp.concatenate([first[:n], second[:n]], axis=1)
     zero = r == 0
     cotangent = jnp.concatenate(
         [jnp.where(zero, ours, theirs), jnp.where(zero, theirs, ours)], axis=0
@@ -270,6 +280,7 @@
     total = sections * 2 * width
     half = weight.shape[1]
     x0 = fetch(features, *SHARED[0])
+    x1 = fetch(features, *SHARED[1])
     x2 = fetch(features, *SHARED[2])
     give, few, grads, flat = load(adjacency, features, cotangent, mask.transpose(0, 2, 1))
     own = adjacency.transpose(1, 0, 2)
@@ -279,14 +290,13 @@
         [give.reshape(sections * nodes, width), grads, few, flat],
         axis=0,
     )
-    late, give = lax.optimization_barrier((features, give))
-    x1 = fetch(late, *SHARED[1])
     taken = fetch(give, (0, 1))
     xs = [x0, x1, x2]
     q = swap(taken)
     parts = (*xs, weight, grads, bias[None, :])
     (here,) = vmem_call(pack_kernel, [vmem(sum(x.shape[0] for x in parts) + 15, width)], *parts)
     there = swap(here)
+    (rows,) = vmem_call(rows_kernel, [vmem(2 * nodes, total)], own, give, taken, q)
     act, far, near, kept = pl.pallas_call(
         forward_kernel,
         out_shape=[
@@ -295,13 +305,13 @@
             vmem(nodes + nodes // 2, feat),
             vmem(nodes, feat, dtype=F32),
         ],
-        in_specs=[pl.BlockSpec(memory_space=pltpu.VMEM)] * 7,
+        in_specs=[pl.BlockSpec(memory_space=pltpu.VMEM)] * 6,
         out_specs=[pl.BlockSpec(memory_space=pltpu.VMEM)] * 4,
-        scratch_shapes=[vmem(2 * nodes, total), vmem(total, feat)],
+        scratch_shapes=[vmem(total, feat)],
     )(
         *(
             pltpu.with_memory_space_constraint(x, pltpu.VMEM)
-            for x in (own, give, features, taken, q, here, there)
+            for x in (rows, features, taken, q, here, there)
         )
     )
     far_, near_ = fetch(far, *ACROSS), fetch(near, (1, 0))

time: 25.5 us -> 25.3 us (level)
    ppermute x3, waiting for transfers between devices: 2.6 us -> 2.33 us  [swap(): return lax.ppermute(value, 'sub', [(0, 1), (1, 0)])]
  transfers between devices with their start and end apart: 9 -> 9, of which waited for: 6 -> 6; matrix products, arithmetic and copies ran while one was open for 0% -> 0% of each run, Pallas kernels for 0% -> 1%
where the time goes in v6:
time: 25.3 us; the launch traced here: 25.1 us
  waiting for transfers between devices  11.2 us (44%)
  starting transfers between devices  10.2 us (40%)
  Pallas kernels  2.83 us (11%)
  between operations  0.77 us (3%)
    ppermute x6, starting transfers between devices, fetch(): return lax.ppermute(value, CORES, pairs)  10.1 us
    ppermute x6, waiting for transfers between devices, fetch(): return lax.ppermute(value, CORES, pairs)  8.84 us
    ppermute x3, waiting for transfers between devices, swap(): return lax.ppermute(value, 'sub', [(0, 1), (1, 0)])  2.33 us
    pallas_call x1, Pallas kernels, load(): pl.pallas_call(load_kernel, out_shape=outs, in_specs=[pl.BlockSpec(memory...  0.95 us
    pallas_call x1, Pallas kernels, direct(): pl.pallas_call(forward_kernel, out_shape=[vmem(nodes, half), vmem(3 * nod...  0.91 us
    pallas_call x1, Pallas kernels, direct(): pl.pallas_call(lambda *refs: backward_kernel(scale, *refs), out_shape=[ja...  0.68 us
  transfers between devices with their start and end apart: 9, of which 6 were waited for; matrix products, arithmetic and copies ran while one was open for 0% of the time, Pallas kernels for 1%

profile of v6, /device:TPU:0, one launch (start us, length us, event | category | flops | bytes accessed | tf_op | source)
XLA Modules:
  0.0 25.1 jit_solution(9195744670811711217)
XLA Ops:
  0.6 1.0 %shard_map.85 = (bf16[128,4,128]{2,1,0:T(4,128)(2,1)S(1)}, bf16[64,128]{1,0:T(8,128)(2,1)S(1)}, bf16[128,128]{1,0:T(8,128)(2,1)S(1)}, s32[2,1,4]{2,1,0:T(1,128)S(1)}) custom-call(bf16[256,4,128]{2,1,0:T(4,128)(2,1)} %a.1, bf16[128,128]{1,0:T(8,128)(2,1)} %x.5, bf16[128,128]{1,0:T(8,128)(2,1)} %g.1, s32[2,1,4]{2,1,0:T(1,128)} %bitcast.16), custom_call_target="tpu_custom_call" | custom-call | tf_op jit(solution)/shard_map/pallas_call | solution.py:129
  1.6 0.0 copy-start
  1.7 0.0 copy-start.1
  1.7 0.0 copy-start.3
  1.7 0.0 copy-start.2
  1.7 3.0 %collective-permute-start = (bf16[720,128]{1,0:T(8,128)(2,1)S(1)}, bf16[720,128]{1,0:T(8,128)(2,1)S(1)}, u32[]{:S(2)}, u32[]{:S(2)}) collective-permute-start(bf16[720,128]{1,0:T(8,128)(2,1)S(1)} %fusion.1.give), channel_id=1, source_target_pairs={{0,2},{1,3},{2,0},{3,1},{4,6},{5,7},{6,4},{7,5},{8,10},{9,11},{10,... | collective-permute-start | bytes 552968 | tf_op jit(solution)/shard_map/ppermute | solution.py:89
  4.7 0.0 copy-done
  4.7 3.7 %collective-permute-start.2 = (bf16[128,128]{1,0:T(8,128)(2,1)S(1)}, bf16[128,128]{1,0:T(8,128)(2,1)S(1)}, u32[]{:S(2)}, u32[]{:S(2)}) collective-permute-start(bf16[128,128]{1,0:T(8,128)(2,1)S(1)} %copy-done), channel_id=1, source_target_pairs={{0,14},{1,13},{2,12},{3,15},{4,10},{5,9},{6,8},{7,11},{8,6},{9,5},... | collective-permute-start | bytes 98312 | tf_op jit(solution)/shard_map/ppermute | solution.py:89
  8.4 0.0 collective-permute-start.3
  8.4 0.8 %collective-permute-start.4 = (bf16[128,128]{1,0:T(8,128)(2,1)S(1)}, bf16[128,128]{1,0:T(8,128)(2,1)S(1)}, u32[]{:S(2)}, u32[]{:S(2)}) collective-permute-start(bf16[128,128]{1,0:T(8,128)(2,1)S(1)} %copy-done), channel_id=1, source_target_pairs={{0,4},{1,7},{2,6},{3,5},{4,0},{5,3},{6,2},{7,1},{8,12},{9,15},{10,... | collective-permute-start | bytes 98312 | tf_op jit(solution)/shard_map/ppermute | solution.py:89
  9.2 0.2 collective-permute-done.p
  9.4 0.0 collective-permute-start.1
  9.4 2.3 %collective-permute-done.2.refs_0_ = bf16[128,128]{1,0:T(8,128)(2,1)S(1)} collective-permute-done((bf16[128,128]{1,0:T(8,128)(2,1)S(1)}, bf16[128,128]{1,0:T(8,128)(2,1)S(1)}, u32[]{:S(2)}, u32[]{:S(2)}) %collective-permute-start.2) | collective-permute-done | bytes 32800 | tf_op jit(solution)/shard_map/ppermute | solution.py:89
  11.7 1.5 %collective-permute-done.3.refs_1_ = bf16[128,128]{1,0:T(8,128)(2,1)S(1)} collective-permute-done((bf16[128,128]{1,0:T(8,128)(2,1)S(1)}, bf16[128,128]{1,0:T(8,128)(2,1)S(1)}, u32[]{:S(2)}, u32[]{:S(2)}) %collective-permute-start.3) | collective-permute-done | bytes 32800 | tf_op jit(solution)/shard_map/ppermute | solution.py:89
  13.2 0.0 collective-permute-done.4.refs_2_
  13.2 0.0 copy-done.1
  13.2 0.0 copy-done.2
  13.2 0.1 collective-permute-start.5
  13.3 0.0 copy-done.3
  13.4 0.0 collective-permute-done.1.q
  13.4 0.2 shard_map.86.rows
  13.6 1.1 %collective-permute-done.5.there = bf16[656,128]{1,0:T(8,128)(2,1)S(1)} collective-permute-done((bf16[656,128]{1,0:T(8,128)(2,1)S(1)}, bf16[656,128]{1,0:T(8,128)(2,1)S(1)}, u32[]{:S(2)}, u32[]{:S(2)}) %collective-permute-start.5) | collective-permute-done | bytes 167968 | tf_op jit(solution)/shard_map/ppermute | solution.py:93
  14.7 0.9 %shard_map.88 = (bf16[128,128]{1,0:T(8,128)(2,1)S(1)}, bf16[384,128]{1,0:T(8,128)(2,1)S(1)}, bf16[192,128]{1,0:T(8,128)(2,1)S(1)}, f32[128,128]{1,0:T(8,128)S(1)}) custom-call(bf16[256,1024]{1,0:T(8,128)(2,1)S(1)} %shard_map.86.rows, bf16[128,128]{1,0:T(8,128)(2,1)S(1)} %copy-done, bf16[720,128]{1,0:T(8,128)(2,1)S(1)} %collective-permute-done.p, ...), custom_call_target="tpu_custom_call" | custom-call | tf_op jit(solution)/shard_map/pallas_call | solution.py:300
  15.6 1.8 %collective-permute-start.6 = (bf16[384,128]{1,0:T(8,128)(2,1)S(1)}, bf16[384,128]{1,0:T(8,128)(2,1)S(1)}, u32[]{:S(2)}, u32[]{:S(2)}) collective-permute-start(bf16[384,128]{1,0:T(8,128)(2,1)S(1)} %get-tuple-element.19.refs_1_), channel_id=1, source_target_pairs={{0,12},{1,9},{2,14},{3,11},{4,8},{5,13},{6,10},{7,15},{8,4},{9,1},... | collective-permute-start | bytes 294920 | tf_op jit(solution)/shard_map/ppermute | solution.py:89
  17.4 0.8 %collective-permute-start.7 = (bf16[192,128]{1,0:T(8,128)(2,1)S(1)}, bf16[192,128]{1,0:T(8,128)(2,1)S(1)}, u32[]{:S(2)}, u32[]{:S(2)}) collective-permute-start(bf16[192,128]{1,0:T(8,128)(2,1)S(1)} %get-tuple-element.20), channel_id=1, source_target_pairs={{0,4},{1,5},{2,6},{3,7},{4,0},{5,1},{6,2},{7,3},{8,12},{9,13},{10,... | collective-permute-start | bytes 147464 | tf_op jit(solution)/shard_map/ppermute | solution.py:89
  18.3 4.8 %collective-permute-done.7.near.refs_3_ = bf16[192,128]{1,0:T(8,128)(2,1)S(1)} collective-permute-done((bf16[192,128]{1,0:T(8,128)(2,1)S(1)}, bf16[192,128]{1,0:T(8,128)(2,1)S(1)}, u32[]{:S(2)}, u32[]{:S(2)}) %collective-permute-start.7) | collective-permute-done | bytes 49184 | tf_op jit(solution)/shard_map/ppermute | solution.py:89
  23.1 0.0 collective-permute-done.6.far.refs_2_
  23.1 0.1 collective-permute-start.8
  23.2 1.3 %collective-permute-done.8.refs_4_ = bf16[320,128]{1,0:T(8,128)(2,1)S(1)} collective-permute-done((bf16[320,128]{1,0:T(8,128)(2,1)S(1)}, bf16[320,128]{1,0:T(8,128)(2,1)S(1)}, u32[]{:S(2)}, u32[]{:S(2)}) %collective-permute-start.8) | collective-permute-done | bytes 81952 | tf_op jit(solution)/shard_map/ppermute | solution.py:93
  24.4 0.7 %shard_map.90 = (bf16[128,128]{1,0:T(8,128)(2,1)}, f32[128,128]{1,0:T(8,128)}, bf16[128,128]{1,0:T(8,128)(2,1)}) custom-call(f32[128,128]{1,0:T(8,128)S(1)} %get-tuple-element.18.refs_0_, bf16[384,128]{1,0:T(8,128)(2,1)S(1)} %get-tuple-element.19.refs_1_, bf16[384,128]{1,0:T(8,128)(2,1)S(1)} %collective-permute-done.6.far.refs_2_, ...), custom_call_target="tpu_custom_call" | custom-call | tf_op jit(solution)/shard_map/pallas_call | solution.py:321
  (7 shorter events, 0.1 us)
Async XLA Ops:
  1.6 3.1 %copy-start = (bf16[128,128]{1,0:T(8,128)(2,1)S(1)}, bf16[128,128]{1,0:T(8,128)(2,1)}, u32[]{:S(2)}) copy-start(bf16[128,128]{1,0:T(8,128)(2,1)} %x.5) | copy-start | bytes 98308
  1.7 11.5 %copy-start.1 = (bf16[128,128]{1,0:T(8,128)(2,1)S(1)}, bf16[128,128]{1,0:T(8,128)(2,1)}, u32[]{:S(2)}) copy-start(bf16[128,128]{1,0:T(8,128)(2,1)} %refs_3_.1) | copy-start | bytes 98308
  1.7 11.6 %copy-start.3 = (bf16[256,4,128]{2,1,0:T(4,128)(2,1)S(1)}, bf16[256,4,128]{2,1,0:T(4,128)(2,1)}, u32[]{:S(2)}) copy-start(bf16[256,4,128]{2,1,0:T(4,128)(2,1)} %a.1) | copy-start | bytes 786436
  1.7 11.5 %copy-start.2 = (f32[128]{0:T(128)S(1)}, f32[128]{0:T(128)}, u32[]{:S(2)}) copy-start(f32[128]{0:T(128)} %param.10) | copy-start | bytes 1540
  1.7 7.6 %collective-permute-start = (bf16[720,128]{1,0:T(8,128)(2,1)S(1)}, bf16[720,128]{1,0:T(8,128)(2,1)S(1)}, u32[]{:S(2)}, u32[]{:S(2)}) collective-permute-start(bf16[720,128]{1,0:T(8,128)(2,1)S(1)} %fusion.1.give), channel_id=1, source_target_pairs={{0,2},{1,3},{2,0},{3,1},{4,6},{5,7},{6,4},{7,5},{8,10},{9,11},{10,... | collective-permute-start | bytes 552968 | tf_op jit(solution)/shard_map/ppermute | solution.py:89
  4.7 7.0 %collective-permute-start.2 = (bf16[128,128]{1,0:T(8,128)(2,1)S(1)}, bf16[128,128]{1,0:T(8,128)(2,1)S(1)}, u32[]{:S(2)}, u32[]{:S(2)}) collective-permute-start(bf16[128,128]{1,0:T(8,128)(2,1)S(1)} %copy-done), channel_id=1, source_target_pairs={{0,14},{1,13},{2,12},{3,15},{4,10},{5,9},{6,8},{7,11},{8,6},{9,5},... | collective-permute-start | bytes 98312 | tf_op jit(solution)/shard_map/ppermute | solution.py:89
  8.4 4.8 %collective-permute-start.3 = (bf16[128,128]{1,0:T(8,128)(2,1)S(1)}, bf16[128,128]{1,0:T(8,128)(2,1)S(1)}, u32[]{:S(2)}, u32[]{:S(2)}) collective-permute-start(bf16[128,128]{1,0:T(8,128)(2,1)S(1)} %copy-done), channel_id=1, source_target_pairs={{0,8},{1,11},{2,10},{3,9},{4,12},{5,15},{6,14},{7,13},{8,0},{9,3},... | collective-permute-start | bytes 98312 | tf_op jit(solution)/shard_map/ppermute | solution.py:89
  8.4 4.8 %collective-permute-start.4 = (bf16[128,128]{1,0:T(8,128)(2,1)S(1)}, bf16[128,128]{1,0:T(8,128)(2,1)S(1)}, u32[]{:S(2)}, u32[]{:S(2)}) collective-permute-start(bf16[128,128]{1,0:T(8,128)(2,1)S(1)} %copy-done), channel_id=1, source_target_pairs={{0,4},{1,7},{2,6},{3,5},{4,0},{5,3},{6,2},{7,1},{8,12},{9,15},{10,... | collective-permute-start | bytes 98312 | tf_op jit(solution)/shard_map/ppermute | solution.py:89
  9.4 4.0 %collective-permute-start.1 = (bf16[720,128]{1,0:T(8,128)(2,1)S(1)}, bf16[720,128]{1,0:T(8,128)(2,1)S(1)}, u32[]{:S(2)}, u32[]{:S(2)}) collective-permute-start(bf16[720,128]{1,0:T(8,128)(2,1)S(1)} %collective-permute-done.p), channel_id=1, source_target_pairs={{0,1},{1,0},{2,3},{3,2},{4,5},{5,4},{6,7},{7,6},{8,9},{9,8},{10,11... | collective-permute-start | bytes 552968 | tf_op jit(solution)/shard_map/ppermute | solution.py:93
  13.2 1.5 %collective-permute-start.5 = (bf16[656,128]{1,0:T(8,128)(2,1)S(1)}, bf16[656,128]{1,0:T(8,128)(2,1)S(1)}, u32[]{:S(2)}, u32[]{:S(2)}) collective-permute-start(bf16[656,128]{1,0:T(8,128)(2,1)S(1)} %shard_map.87.here), channel_id=1, source_target_pairs={{0,1},{1,0},{2,3},{3,2},{4,5},{5,4},{6,7},{7,6},{8,9},{9,8},{10,11... | collective-permute-start | bytes 503816 | tf_op jit(solution)/shard_map/ppermute | solution.py:93
  15.6 7.5 %collective-permute-start.6 = (bf16[384,128]{1,0:T(8,128)(2,1)S(1)}, bf16[384,128]{1,0:T(8,128)(2,1)S(1)}, u32[]{:S(2)}, u32[]{:S(2)}) collective-permute-start(bf16[384,128]{1,0:T(8,128)(2,1)S(1)} %get-tuple-element.19.refs_1_), channel_id=1, source_target_pairs={{0,12},{1,9},{2,14},{3,11},{4,8},{5,13},{6,10},{7,15},{8,4},{9,1},... | collective-permute-start | bytes 294920 | tf_op jit(solution)/shard_map/ppermute | solution.py:89
  17.4 5.6 %collective-permute-start.7 = (bf16[192,128]{1,0:T(8,128)(2,1)S(1)}, bf16[192,128]{1,0:T(8,128)(2,1)S(1)}, u32[]{:S(2)}, u32[]{:S(2)}) collective-permute-start(bf16[192,128]{1,0:T(8,128)(2,1)S(1)} %get-tuple-element.20), channel_id=1, source_target_pairs={{0,4},{1,5},{2,6},{3,7},{4,0},{5,1},{6,2},{7,3},{8,12},{9,13},{10,... | collective-permute-start | bytes 147464 | tf_op jit(solution)/shard_map/ppermute | solution.py:89
  23.1 1.3 %collective-permute-start.8 = (bf16[320,128]{1,0:T(8,128)(2,1)S(1)}, bf16[320,128]{1,0:T(8,128)(2,1)S(1)}, u32[]{:S(2)}, u32[]{:S(2)}) collective-permute-start(bf16[320,128]{1,0:T(8,128)(2,1)S(1)} %shard_map.89), channel_id=1, source_target_pairs={{0,1},{1,0},{2,3},{3,2},{4,5},{5,4},{6,7},{7,6},{8,9},{9,8},{10,11... | collective-permute-start | bytes 245768 | tf_op jit(solution)/shard_map/ppermute | solution.py:93
